TPU v7x, 32 devices: a whole 2x2x4 slice. The times are simulated.
32 devices in a mesh: dp: 4 (over y, core), seq: 8 (over z, x).
Axes of the slice: x: 2, y: 2, z: 4, core: 2. Of those that a mesh axis runs over, the one named last changes fastest.
Arguments:
- stream_in: float32 [4, 1024, 1536], P('dp', 'seq'), may hold values from -6 to 6
- doc_starts: int32 [4, 4], P('dp'), may hold values from 0 to 1023, as said below
- norm_mix: float32 [2, 1536], P(None, ('dp', 'seq')), may hold values from 0.5 to 1.5
- in_proj: float32 [2, 1536, 4608], P(None, ('dp', 'seq')), may hold values from -0.15625 to 0.15625
- conv_taps: float32 [2, 1536, 3], P(None, ('dp', 'seq')), may hold values from -3.5 to 3.5
- out_proj: float32 [2, 1536, 1536], P(None, ('dp', 'seq')), may hold values from -0.15625 to 0.15625
- norm_ffn: float32 [2, 1536], P(None, ('dp', 'seq')), may hold values from 0.5 to 1.5
- w_gate: float32 [2, 1536, 4608], P(None, ('dp', 'seq')), may hold values from -0.15625 to 0.15625
- w_up: float32 [2, 1536, 4608], P(None, ('dp', 'seq')), may hold values from -0.15625 to 0.15625
- w_down: float32 [2, 4608, 1536], P(None, ('dp', 'seq')), may hold values from -0.125 to 0.125
- grad_out: float32 [4, 1024, 1536], P('dp', 'seq'), may hold values from -6 to 6
Outputs:
- stream_out: float32 [4, 1024, 1536], P('dp', 'seq')
- grad_in: float32 [4, 1024, 1536], P('dp', 'seq')
- grad_norm_mix: float32 [2, 1536], P(None, ('dp', 'seq'))
- grad_in_proj: float32 [2, 1536, 4608], P(None, ('dp', 'seq'))
- grad_conv_taps: float32 [2, 1536, 3], P(None, ('dp', 'seq'))
- grad_out_proj: float32 [2, 1536, 1536], P(None, ('dp', 'seq'))
- grad_norm_ffn: float32 [2, 1536], P(None, ('dp', 'seq'))
- grad_gate: float32 [2, 1536, 4608], P(None, ('dp', 'seq'))
- grad_up: float32 [2, 1536, 4608], P(None, ('dp', 'seq'))
- grad_down: float32 [2, 4608, 1536], P(None, ('dp', 'seq'))
Inputs may be any that keep to these rules, and one draw needn't show every extreme that they name: `doc_starts`: in each row the starts rise strictly and the first is 0; every other start lies in positions 1 to 63 or in the last 64 positions of the row.
All inputs are finite; a program needn't handle non-finite values.
Results may differ from a plain program's by a relative error of at most 0.017.
The roundings to bfloat16 on the way count: a program that leaves them out, or rounds other values in their place, can miss the bound.
Values may be sent and summed in bfloat16 or wider, within the bound.
A program may use at most 704 MiB of HBM per device.

v0:
```python
import jax
import jax.numpy as jnp
from jax import lax
from jax.sharding import PartitionSpec as P

EPSILON = 1e-05


def passed_along(array, axis, by):
    devices = lax.axis_size(axis)
    pairs = [(i, i + by) for i in range(devices) if 0 <= i + by < devices]
    return lax.ppermute(array, axis, pairs)


def rms_scale(values):
    return lax.rsqrt(jnp.mean(values * values, axis=-1, keepdims=True) + EPSILON)


def matmul(left, right):
    return jnp.dot(left, right, preferred_element_type=jnp.float32)


def inner_rows(left, right):
    return lax.dot_general(
        left, right, (((0,), (0,)), ((), ())), preferred_element_type=jnp.float32
    )


def outer_cols(left, right):
    return lax.dot_general(
        left, right, (((1,), (1,)), ((), ())), preferred_element_type=jnp.float32
    )


def tap_masks(starts, token_count):
    places = lax.axis_index("seq") * token_count + jnp.arange(token_count, dtype=jnp.int32)

    def segment_of(where):
        return jnp.sum((starts[:, None, :] <= where[None, :, None]).astype(jnp.int32), axis=2)

    own_segment = segment_of(places)
    keep_one = (segment_of(places - 1) == own_segment).astype(jnp.float32)[:, :, None]
    keep_two = (segment_of(places - 2) == own_segment).astype(jnp.float32)[:, :, None]
    return (keep_one, keep_two)


def layer_slices(weights, layer_index):
    return tuple((weight[layer_index].astype(jnp.bfloat16) for weight in weights))


def layer_forward(stream, gathered, keep_one, keep_two, batch_rows):
    gain_mix, in_weight, conv_weight, out_weight, gain_ffn, gate_weight, up_weight, down_weight = (
        gathered
    )
    features = stream.shape[1]
    token_count = stream.shape[0] // batch_rows
    scale_mix = rms_scale(stream)
    normed = (stream * scale_mix * gain_mix.astype(jnp.float32)).astype(jnp.bfloat16)
    joint = matmul(normed, in_weight)
    b_part = joint[:, :features]
    c_part = joint[:, features : 2 * features]
    x_part = joint[:, 2 * features :]
    carried = (b_part * x_part).reshape(batch_rows, token_count, features)
    previous = passed_along(carried[:, token_count - 2 :], "seq", 1)
    padded = jnp.concatenate([previous, carried], axis=1)
    conv_float = conv_weight.astype(jnp.float32)
    mixed = (
        conv_float[:, 0] * padded[:, :token_count] * keep_two
        + conv_float[:, 1] * padded[:, 1 : token_count + 1] * keep_one
        + conv_float[:, 2] * carried
    ).reshape(-1, features)
    gated = (c_part * mixed).astype(jnp.bfloat16)
    middle = stream + matmul(gated, out_weight)
    scale_ffn = rms_scale(middle)
    normed_ffn = (middle * scale_ffn * gain_ffn.astype(jnp.float32)).astype(jnp.bfloat16)
    gate_value = matmul(normed_ffn, gate_weight)
    up_value = matmul(normed_ffn, up_weight)
    hidden = (jax.nn.silu(gate_value) * up_value).astype(jnp.bfloat16)
    result = middle + matmul(hidden, down_weight)
    saved = (
        stream,
        scale_mix,
        normed,
        joint,
        padded,
        mixed,
        gated,
        middle,
        scale_ffn,
        normed_ffn,
        gate_value,
        up_value,
        hidden,
    )
    return (result, saved)


def layer_backward(grad_stream, saved, gathered, keep_one, keep_two, batch_rows):
    (
        stream,
        scale_mix,
        normed,
        joint,
        padded,
        mixed,
        gated,
        middle,
        scale_ffn,
        normed_ffn,
        gate_value,
        up_value,
        hidden,
    ) = saved
    gain_mix, in_weight, conv_weight, out_weight, gain_ffn, gate_weight, up_weight, down_weight = (
        gathered
    )
    features = stream.shape[1]
    hidden_width = hidden.shape[1]
    token_count = stream.shape[0] // batch_rows
    conv_float = conv_weight.astype(jnp.float32)
    down_in = grad_stream.astype(jnp.bfloat16)
    grad_down = lax.psum_scatter(
        inner_rows(hidden, down_in), ("dp", "seq"), scatter_dimension=0, tiled=True
    )
    grad_hidden = outer_cols(down_in, down_weight)
    sigmoid_gate = jax.nn.sigmoid(gate_value)
    grad_gate_value = (
        grad_hidden * up_value * sigmoid_gate * (1.0 + gate_value * (1.0 - sigmoid_gate))
    ).astype(jnp.bfloat16)
    grad_up_value = (grad_hidden * gate_value * sigmoid_gate).astype(jnp.bfloat16)
    both_values = jnp.concatenate([grad_gate_value, grad_up_value], axis=1)
    ffn_shares = lax.psum_scatter(
        inner_rows(normed_ffn, both_values), ("dp", "seq"), scatter_dimension=0, tiled=True
    )
    grad_gate = ffn_shares[:, :hidden_width]
    grad_up = ffn_shares[:, hidden_width:]
    grad_normed_ffn = outer_cols(grad_gate_value, gate_weight) + outer_cols(
        grad_up_value, up_weight
    )
    grad_gain_ffn = jnp.sum(grad_normed_ffn * middle * scale_ffn, axis=0)
    scaled_ffn = grad_normed_ffn * gain_ffn.astype(jnp.float32)
    grad_middle = (
        grad_stream
        + scale_ffn * scaled_ffn
        - middle * scale_ffn**3 * jnp.mean(scaled_ffn * middle, axis=-1, keepdims=True)
    )
    mix_in = grad_middle.astype(jnp.bfloat16)
    grad_gated = outer_cols(mix_in, out_weight)
    b_part = joint[:, :features]
    c_part = joint[:, features : 2 * features]
    x_part = joint[:, 2 * features :]
    grad_c = grad_gated * mixed
    grad_mixed = (grad_gated * c_part).reshape(batch_rows, token_count, features)
    first_tap = grad_mixed * keep_two
    second_tap = grad_mixed * keep_one
    grad_conv = jnp.stack(
        [
            jnp.sum(first_tap * padded[:, :token_count], axis=(0, 1)),
            jnp.sum(second_tap * padded[:, 1 : token_count + 1], axis=(0, 1)),
            jnp.sum(grad_mixed * padded[:, 2:], axis=(0, 1)),
        ],
        axis=1,
    )
    zeros_one = jnp.zeros((batch_rows, 1, features), jnp.float32)
    zeros_two = jnp.zeros((batch_rows, 2, features), jnp.float32)
    grad_padded = jnp.concatenate(
        [first_tap * conv_float[:, 0], zeros_two], axis=1
    ) + jnp.concatenate([zeros_one, second_tap * conv_float[:, 1], zeros_one], axis=1)
    returned = passed_along(grad_padded[:, :2], "seq", -1)
    arriving = jnp.concatenate(
        [jnp.zeros((batch_rows, token_count - 2, features), jnp.float32), returned], axis=1
    )
    grad_carried = (grad_padded[:, 2:] + grad_mixed * conv_float[:, 2] + arriving).reshape(
        -1, features
    )
    grad_joint = jnp.concatenate(
        [grad_carried * x_part, grad_c, grad_carried * b_part], axis=1
    ).astype(jnp.bfloat16)
    mix_shares = lax.psum_scatter(
        jnp.concatenate([inner_rows(normed, grad_joint), inner_rows(gated, mix_in)], axis=1),
        ("dp", "seq"),
        scatter_dimension=0,
        tiled=True,
    )
    grad_in_weight = mix_shares[:, : 3 * features]
    grad_out_weight = mix_shares[:, 3 * features :]
    grad_normed = outer_cols(grad_joint, in_weight)
    grad_gain_mix = jnp.sum(grad_normed * stream * scale_mix, axis=0)
    small_shares = (
        lax.psum_scatter(grad_gain_mix, ("dp", "seq"), scatter_dimension=0, tiled=True),
        lax.psum_scatter(grad_gain_ffn, ("dp", "seq"), scatter_dimension=0, tiled=True),
        lax.psum_scatter(grad_conv, ("dp", "seq"), scatter_dimension=0, tiled=True),
    )
    scaled_mix = grad_normed * gain_mix.astype(jnp.float32)
    grad_input = (
        grad_middle
        + scale_mix * scaled_mix
        - stream * scale_mix**3 * jnp.mean(scaled_mix * stream, axis=-1, keepdims=True)
    )
    pieces = (
        small_shares[0],
        grad_in_weight,
        small_shares[2],
        grad_out_weight,
        small_shares[1],
        grad_gate,
        grad_up,
        grad_down,
    )
    return (grad_input, pieces)


def local(
    stream_in,
    doc_starts,
    norm_mix,
    in_proj,
    conv_taps,
    out_proj,
    norm_ffn,
    w_gate,
    w_up,
    w_down,
    grad_out,
):
    weights = (norm_mix, in_proj, conv_taps, out_proj, norm_ffn, w_gate, w_up, w_down)
    batch_rows, token_count, features = stream_in.shape
    layer_total = norm_mix.shape[0]
    keep_one, keep_two = tap_masks(doc_starts, token_count)
    stream = stream_in.reshape(-1, features)
    saved_all = []
    gathered = None
    for layer_index in range(layer_total):
        (
            gain_mix,
            in_weight,
            conv_weight,
            out_weight,
            gain_ffn,
            gate_weight,
            up_weight,
            down_weight,
        ) = layer_slices(weights, layer_index)
        gathered = (
            lax.all_gather(gain_mix, ("dp", "seq"), axis=0, tiled=True),
            lax.all_gather(in_weight, ("dp", "seq"), axis=0, tiled=True),
            lax.all_gather(conv_weight, ("dp", "seq"), axis=0, tiled=True),
            lax.all_gather(out_weight, ("dp", "seq"), axis=0, tiled=True),
            lax.all_gather(gain_ffn, ("dp", "seq"), axis=0, tiled=True),
            lax.all_gather(gate_weight, ("dp", "seq"), axis=0, tiled=True),
            lax.all_gather(up_weight, ("dp", "seq"), axis=0, tiled=True),
            lax.all_gather(down_weight, ("dp", "seq"), axis=0, tiled=True),
        )
        stream, saved = layer_forward(stream, gathered, keep_one, keep_two, batch_rows)
        saved_all.append(saved)
    grad_stream = grad_out.reshape(-1, features)
    piece_list = []
    for layer_index in reversed(range(layer_total)):
        (
            gain_mix,
            in_weight,
            conv_weight,
            out_weight,
            gain_ffn,
            gate_weight,
            up_weight,
            down_weight,
        ) = layer_slices(weights, layer_index)
        weights_now = (
            lax.all_gather(gain_mix, ("dp", "seq"), axis=0, tiled=True),
            lax.all_gather(in_weight, ("dp", "seq"), axis=0, tiled=True),
            lax.all_gather(conv_weight, ("dp", "seq"), axis=0, tiled=True),
            lax.all_gather(out_weight, ("dp", "seq"), axis=0, tiled=True),
            lax.all_gather(gain_ffn, ("dp", "seq"), axis=0, tiled=True),
            lax.all_gather(gate_weight, ("dp", "seq"), axis=0, tiled=True),
            lax.all_gather(up_weight, ("dp", "seq"), axis=0, tiled=True),
            lax.all_gather(down_weight, ("dp", "seq"), axis=0, tiled=True),
        )
        grad_stream, pieces = layer_backward(
            grad_stream, saved_all[layer_index], weights_now, keep_one, keep_two, batch_rows
        )
        piece_list.insert(0, pieces)
    stream_out = stream.reshape(batch_rows, token_count, features)
    grad_in = grad_stream.reshape(batch_rows, token_count, features)
    stacked = tuple((jnp.stack([pieces[member] for pieces in piece_list]) for member in range(8)))
    return (stream_out, grad_in) + stacked


def solution(mesh):
    return jax.shard_map(
        local,
        mesh=mesh,
        in_specs=(
            P("dp", "seq", None),
            P("dp", None),
            P(None, ("dp", "seq")),
            P(None, ("dp", "seq"), None),
            P(None, ("dp", "seq"), None),
            P(None, ("dp", "seq"), None),
            P(None, ("dp", "seq")),
            P(None, ("dp", "seq"), None),
            P(None, ("dp", "seq"), None),
            P(None, ("dp", "seq"), None),
            P("dp", "seq", None),
        ),
        out_specs=(
            P("dp", "seq", None),
            P("dp", "seq", None),
            P(None, ("dp", "seq")),
            P(None, ("dp", "seq"), None),
            P(None, ("dp", "seq"), None),
            P(None, ("dp", "seq"), None),
            P(None, ("dp", "seq")),
            P(None, ("dp", "seq"), None),
            P(None, ("dp", "seq"), None),
            P(None, ("dp", "seq"), None),
        ),
        check_vma=False,
    )
```

profile of v0, /device:TPU:0, one launch (start us, length us, event | category | flops | bytes accessed | tf_op | source)
XLA Modules:
  0.0 3510.4 jit_solution(17651129934380801873)
XLA Ops:
  19.4 43.4 %all-reduce.13 = (bf16[1536]{0:T(1024)(128)(2,1)S(1)}, bf16[1536]{0:T(1024)(128)(2,1)S(1)}, bf16[1536]{0:T(1024)(128)(2,1)S(1)}, bf16[1536]{0:T(1024)(128)(2,1)S(1)}) all-reduce(bf16[1536]{0:T(1024)(128)(2,1)S(1)} %dynamic-update-slice, bf16[1536]{0:T(1024)(128)(2,1)S(1)} %dynamic-update-slice.1, ...), channel_id=2, replica_groups=mesh['dp'=4,'seq'=8] {'dp','seq'}, use_global_device_ids=true, to_apply=%add.4 | all-reduce | flops 6144 | bytes 24576
  63.0 75.0 %all-gather.2 = bf16[1,1536,3]{2,0,1:T(2,128)(2,1)S(1)} all-gather(bf16[1,48,3]{2,0,1:T(2,128)(2,1)S(1)} %get-tuple-element.119), channel_id=4, replica_groups=mesh['dp'=4,'seq'=8] {'dp','seq'}, dimensions={1}, use_global_device_ids=true | all-gather | bytes 9504 | tf_op jit(solution)/shard_map/all_gather | solution.py:247
  138.5 70.9 %all-gather.10 = bf16[1,1536,3]{2,0,1:T(2,128)(2,1)S(1)} all-gather(bf16[1,48,3]{2,0,1:T(2,128)(2,1)S(1)} %get-tuple-element.118), channel_id=12, replica_groups=mesh['dp'=4,'seq'=8] {'dp','seq'}, dimensions={1}, use_global_device_ids=true | all-gather | bytes 9504 | tf_op jit(solution)/shard_map/all_gather | solution.py:247
  212.0 7.1 fusion.30
  219.3 3.6 collective-permute-start
  226.1 3.3 multiply_reduce_fusion.10
  230.5 73.5 %all-gather.31.cloned.1.call-done = bf16[1,1536,4608]{2,1,0:T(8,128)(2,1)} async-done(((bf16[1,48,4608]{2,1,0:T(8,128)(2,1)}), bf16[1,1536,4608]{2,1,0:T(8,128)(2,1)}) %all-gather.31.cloned.1.call-update) | async-done | bytes 14155792 | tf_op jit(solution)/shard_map/all_gather | solution.py:250
  304.0 8.6 fusion.26
  312.6 96.2 %all-gather.33.cloned.1.call-done = bf16[1,1536,4608]{2,1,0:T(8,128)(2,1)} async-done(((bf16[1,48,4608]{2,1,0:T(8,128)(2,1)}), bf16[1,1536,4608]{2,1,0:T(8,128)(2,1)}) %all-gather.33.cloned.1.call-update) | async-done | bytes 14155792 | tf_op jit(solution)/shard_map/all_gather | solution.py:251
  408.8 10.2 multiply_convert_fusion.5
  419.0 94.0 %all-gather.35.cloned.1.call-done = bf16[1,4608,1536]{2,1,0:T(8,128)(2,1)} async-done(((bf16[1,144,1536]{2,1,0:T(8,128)(2,1)}), bf16[1,4608,1536]{2,1,0:T(8,128)(2,1)}) %all-gather.35.cloned.1.call-update) | async-done | bytes 14155792 | tf_op jit(solution)/shard_map/all_gather | solution.py:252
  513.1 7.6 multiply_reduce_fusion.9
  521.2 96.7 %all-gather.37.cloned.1.call-done = bf16[1,1536,4608]{2,1,0:T(8,128)(2,1)} async-done(((bf16[1,48,4608]{2,1,0:T(8,128)(2,1)}), bf16[1,1536,4608]{2,1,0:T(8,128)(2,1)}) %all-gather.37.cloned.1.call-update) | async-done | bytes 14155792 | tf_op jit(solution)/shard_map/all_gather | solution.py:246
  617.9 7.1 fusion.14
  627.4 3.5 collective-permute-start.1
  630.9 91.8 %all-gather.45.cloned.1.call-done = bf16[1,4608,1536]{2,1,0:T(8,128)(2,1)} async-done(((bf16[1,144,1536]{2,1,0:T(8,128)(2,1)}), bf16[1,4608,1536]{2,1,0:T(8,128)(2,1)}) %all-gather.45.cloned.1.call-update) | async-done | bytes 14155792 | tf_op jit(solution)/shard_map/all_gather | solution.py:252
  722.7 11.4 fusion
  736.9 50.6 %all-gather.39.cloned.1.call-done = bf16[1,1536,1536]{2,1,0:T(8,128)(2,1)} async-done(((bf16[1,48,1536]{2,1,0:T(8,128)(2,1)}), bf16[1,1536,1536]{2,1,0:T(8,128)(2,1)}) %all-gather.39.cloned.1.call-update) | async-done | bytes 4718608 | tf_op jit(solution)/shard_map/all_gather | solution.py:248
  792.8 100.4 %all-gather.43.cloned.1.call-done = bf16[1,1536,4608]{2,1,0:T(8,128)(2,1)} async-done(((bf16[1,48,4608]{2,1,0:T(8,128)(2,1)}), bf16[1,1536,4608]{2,1,0:T(8,128)(2,1)}) %all-gather.43.cloned.1.call-update) | async-done | bytes 14155792 | tf_op jit(solution)/shard_map/all_gather | solution.py:251
  893.2 8.6 fusion.6
  901.8 96.2 %all-gather.41.cloned.1.call-done = bf16[1,1536,4608]{2,1,0:T(8,128)(2,1)} async-done(((bf16[1,48,4608]{2,1,0:T(8,128)(2,1)}), bf16[1,1536,4608]{2,1,0:T(8,128)(2,1)}) %all-gather.41.cloned.1.call-update) | async-done | bytes 14155792 | tf_op jit(solution)/shard_map/all_gather | solution.py:250
  998.0 10.8 multiply_convert_fusion.3
  1008.8 10.0 fusion.4
  1018.9 12.1 multiply_reduce_fusion
  1037.8 3.7 collective-permute-done.2
  1041.9 10.6 multiply_reduce_fusion.4
  1053.7 12.8 multiply_convert_fusion.1
  1066.5 10.0 fusion.20
  1076.5 11.6 multiply_reduce_fusion.1
  1101.7 14.9 fusion.125
  1116.7 14.9 fusion.101
  1131.7 6.2 fusion.104
  1138.0 11.5 fusion.96
  1149.5 25.2 pad_maximum_fusion.1
  1178.4 5.0 fusion.98
  1184.7 11.6 fusion.95
  1196.3 25.1 pad_maximum_fusion
  1223.1 20.6 fusion.65
  1245.5 20.5 fusion.61
  1267.5 8.1 fusion.58
  1275.6 9.8 fusion.94
  1285.5 42.5 %all-reduce.12 = (f32[1536]{0:T(1024)S(1)}, f32[1536]{0:T(1024)S(1)}, f32[1536]{0:T(1024)S(1)}, f32[1536]{0:T(1024)S(1)}) all-reduce(f32[1536]{0:T(1024)S(1)} %copy-done.86, f32[1536]{0:T(1024)S(1)} %get-tuple-element.58, f32[1536]{0:T(1024)S(1)} %copy-done.73, ...), channel_id=19, replica_groups=mesh['dp'=4,'seq'=8] {'dp','seq'}, use_global_device_ids=true, to_apply=%region_14.15.clone | all-reduce | flops 6144 | bytes 49152
  1332.8 228.1 %reduce-scatter.23.cloned.1.call-done = f32[144,1536]{1,0:T(8,128)} async-done(((f32[4608,1536]{1,0:T(8,128)}), f32[144,1536]{1,0:T(8,128)}) %reduce-scatter.23.cloned.1.call-update) | async-done | bytes 884752 | tf_op jit(solution)/shard_map/reduce_scatter | solution.py:122
  1560.8 269.7 %reduce-scatter.21.cloned.1.call-done = f32[144,1536]{1,0:T(8,128)} async-done(((f32[4608,1536]{1,0:T(8,128)}), f32[144,1536]{1,0:T(8,128)}) %reduce-scatter.21.cloned.1.call-update) | async-done | bytes 884752 | tf_op jit(solution)/shard_map/reduce_scatter | solution.py:122
  1833.3 351.7 %reduce-scatter.15.cloned.1.call-done = f32[48,6144]{1,0:T(8,128)} async-done(((f32[1536,6144]{1,0:T(8,128)}), f32[48,6144]{1,0:T(8,128)}) %reduce-scatter.15.cloned.1.call-update) | async-done | bytes 1179664 | tf_op jit(solution)/shard_map/reduce_scatter | solution.py:179
  2187.2 352.8 %reduce-scatter.13.cloned.1.call-done = f32[48,6144]{1,0:T(8,128)} async-done(((f32[1536,6144]{1,0:T(8,128)}), f32[48,6144]{1,0:T(8,128)}) %reduce-scatter.13.cloned.1.call-update) | async-done | bytes 1179664 | tf_op jit(solution)/shard_map/reduce_scatter | solution.py:179
  2543.4 475.8 %reduce-scatter.19.cloned.1.call-done = f32[48,9216]{1,0:T(8,128)} async-done(((f32[1536,9216]{1,0:T(8,128)}), f32[48,9216]{1,0:T(8,128)}) %reduce-scatter.19.cloned.1.call-update) | async-done | bytes 1769488 | tf_op jit(solution)/shard_map/reduce_scatter | solution.py:132
  3020.8 478.1 %reduce-scatter.17.cloned.1.call-done = f32[48,9216]{1,0:T(8,128)} async-done(((f32[1536,9216]{1,0:T(8,128)}), f32[48,9216]{1,0:T(8,128)}) %reduce-scatter.17.cloned.1.call-update) | async-done | bytes 1769488 | tf_op jit(solution)/shard_map/reduce_scatter | solution.py:132
  (358 shorter events, 80.7 us)
Async XLA Ops:
  7.2 204.8 %all-gather.27.cloned.1.call-start = ((), (), s32[]{:S(2)}) async-start(), calls=%async_computation.14 | async-start | bytes 14598144 | tf_op jit(solution)/shard_map/all_gather | solution.py:246
  9.9 216.3 %all-gather.29.cloned.1.call-start = ((), (), s32[]{:S(2)}) async-start(), calls=%async_computation.15 | async-start | bytes 4866048 | tf_op jit(solution)/shard_map/all_gather | solution.py:248
  10.7 293.3 %all-gather.31.cloned.1.call-start = ((), (), s32[]{:S(2)}) async-start(), calls=%async_computation.16 | async-start | bytes 14598144 | tf_op jit(solution)/shard_map/all_gather | solution.py:250
  11.9 397.0 %all-gather.33.cloned.1.call-start = ((), (), s32[]{:S(2)}) async-start(), calls=%async_computation.17 | async-start | bytes 14598144 | tf_op jit(solution)/shard_map/all_gather | solution.py:251
  13.6 499.5 %all-gather.35.cloned.1.call-start = ((), (), s32[]{:S(2)}) async-start(), calls=%async_computation.18 | async-start | bytes 14598144 | tf_op jit(solution)/shard_map/all_gather | solution.py:252
  13.8 49.1 %copy-start.91 = (f32[2,48,3]{1,0,2:T(2,128)S(1)}, f32[2,48,3]{1,0,2:T(2,128)}, u32[]{:S(2)}) copy-start(f32[2,48,3]{1,0,2:T(2,128)} %param.15) | copy-start | bytes 3460
  14.9 603.0 %all-gather.37.cloned.1.call-start = ((), (), s32[]{:S(2)}) async-start(), calls=%async_computation.19 | async-start | bytes 14598144 | tf_op jit(solution)/shard_map/all_gather | solution.py:246
  15.5 707.3 %all-gather.45.cloned.1.call-start = ((), (), s32[]{:S(2)}) async-start(), calls=%async_computation.23 | async-start | bytes 14598144 | tf_op jit(solution)/shard_map/all_gather | solution.py:252
  16.2 193.8 %copy-start.96 = (s32[1,4]{1,0:T(1,128)S(1)}, s32[1,4]{1,0:T(1,128)}, u32[]{:S(2)}) copy-start(s32[1,4]{1,0:T(1,128)} %param.12) | copy-start | bytes 52
  16.2 194.6 %copy-start.3 = (f32[1,128,1536]{2,1,0:T(8,128)S(1)}, f32[1,128,1536]{2,1,0:T(8,128)}, u32[]{:S(2)}) copy-start(f32[1,128,1536]{2,1,0:T(8,128)} %param.11) | copy-start | bytes 2359300
  16.2 771.3 %all-gather.39.cloned.1.call-start = ((), (), s32[]{:S(2)}) async-start(), calls=%async_computation.20 | async-start | bytes 4866048 | tf_op jit(solution)/shard_map/all_gather | solution.py:248
  17.0 876.2 %all-gather.43.cloned.1.call-start = ((), (), s32[]{:S(2)}) async-start(), calls=%async_computation.22 | async-start | bytes 14598144 | tf_op jit(solution)/shard_map/all_gather | solution.py:251
  17.7 980.3 %all-gather.41.cloned.1.call-start = ((), (), s32[]{:S(2)}) async-start(), calls=%async_computation.21 | async-start | bytes 14598144 | tf_op jit(solution)/shard_map/all_gather | solution.py:250
  18.3 1312.2 %reduce-scatter.25.cloned.1.call-start = ((), (), s32[]{:S(2)}) async-start(), calls=%async_computation.24 | async-start | bytes 811008
  62.8 156.3 %copy-start.54 = (f32[1536]{0:T(1024)}, f32[1536]{0:T(1024)S(1)}, u32[]{:S(2)}) copy-start(f32[1536]{0:T(1024)S(1)} %convert_element_type.254) | copy-start | bytes 18436
  219.3 4.9 collective-permute-start
  230.1 82.5 %copy-start.87 = (f32[128]{0:T(128)}, f32[128]{0:T(128)S(1)}, u32[]{:S(2)}) copy-start(f32[128]{0:T(128)S(1)} %get-tuple-element.123) | copy-start | bytes 1540
  230.5 178.3 %copy-start.32 = (bf16[128,1536]{1,0:T(8,128)(2,1)}, bf16[128,1536]{1,0:T(8,128)(2,1)S(1)}, u32[]{:S(2)}) copy-start(bf16[128,1536]{1,0:T(8,128)(2,1)S(1)} %multiply_convert_fusion.12) | copy-start | bytes 1179652
  521.2 103.8 %copy-start.77 = (f32[128]{0:T(128)}, f32[128]{0:T(128)S(1)}, u32[]{:S(2)}) copy-start(f32[128]{0:T(128)S(1)} %get-tuple-element.125) | copy-start | bytes 1540
  627.4 106.8 %collective-permute-start.1 = (f32[1,2,1536]{2,1,0:T(2,128)S(1)}, f32[1,2,1536]{2,1,0:T(2,128)S(1)}, u32[]{:S(2)}, u32[]{:S(2)}) collective-permute-start(f32[1,2,1536]{2,1,0:T(2,128)S(1)} %slice.253), channel_id=1, source_target_pairs={{0,1},{1,2},{2,3},{3,4},{4,5},{5,6},{6,7},{8,9},{9,10},{10,11},{11... | collective-permute-start | bytes 36872 | tf_op jit(solution)/shard_map/ppermute | solution.py:12
  722.7 12.0 copy-start.1
  722.7 12.0 copy-start.22
  1008.8 10.1 copy-start.26
  1008.8 10.1 copy-start.6
  1008.8 10.1 copy-start.57
  1008.8 10.1 copy-start.90
  1018.9 13.8 slice-start.2
  1018.9 12.1 copy-start.95
  1018.9 13.8 slice-start.3
  1032.7 19.8 copy-start.18
  1035.9 5.6 collective-permute-start.2
  1041.9 10.6 copy-start.44
  1041.9 10.6 copy-start.46
  1041.9 10.6 copy-start.94
  1066.5 10.0 copy-start.88
  1076.5 13.3 slice-start
  1076.5 11.7 copy-start.93
  1076.5 13.3 slice-start.1
  1097.6 233.8 %reduce-scatter.27.cloned.1.call-start = ((), (), s32[]{:S(2)}) async-start(), calls=%async_computation.25 | async-start | bytes 811008
  1101.6 459.2 %reduce-scatter.23.cloned.1.call-start = ((), (), s32[]{:S(2)}) async-start(), calls=%async_computation.13 | async-start | bytes 29196288 | tf_op jit(solution)/shard_map/reduce_scatter | solution.py:122
  1116.6 713.9 %reduce-scatter.21.cloned.1.call-start = ((), (), s32[]{:S(2)}) async-start(), calls=%async_computation.12 | async-start | bytes 29196288 | tf_op jit(solution)/shard_map/reduce_scatter | solution.py:122
  1131.7 1053.3 %reduce-scatter.15.cloned.1.call-start = ((), (), s32[]{:S(2)}) async-start(), calls=%async_computation.9 | async-start | bytes 38928384 | tf_op jit(solution)/shard_map/reduce_scatter | solution.py:179
  1174.7 1365.3 %reduce-scatter.13.cloned.1.call-start = ((), (), s32[]{:S(2)}) async-start(), calls=%async_computation.8 | async-start | bytes 38928384 | tf_op jit(solution)/shard_map/reduce_scatter | solution.py:179
  1176.9 6.5 collective-permute-start.3
  1221.4 1797.8 %reduce-scatter.19.cloned.1.call-start = ((), (), s32[]{:S(2)}) async-start(), calls=%async_computation.11 | async-start | bytes 58392576 | tf_op jit(solution)/shard_map/reduce_scatter | solution.py:132
  1243.8 2255.1 %reduce-scatter.17.cloned.1.call-start = ((), (), s32[]{:S(2)}) async-start(), calls=%async_computation.10 | async-start | bytes 58392576 | tf_op jit(solution)/shard_map/reduce_scatter | solution.py:132
  1275.6 53.8 %copy-start.17 = (f32[128,1536]{1,0:T(8,128)S(1)}, f32[128,1536]{1,0:T(8,128)}, u32[]{:S(2)}) copy-start(f32[128,1536]{1,0:T(8,128)} %copy-done.15) | copy-start | bytes 2359300
  1275.6 53.8 %copy-start.92 = (f32[128]{0:T(128)S(1)}, f32[128]{0:T(128)}, u32[]{:S(2)}) copy-start(f32[128]{0:T(128)} %get-tuple-element.120) | copy-start | bytes 1540
  (77 other events, 261.2 us)
Sparse Core Ops, SparseCore 0:
  11.6 115.5 all-gather.26
  130.7 67.0 all-gather.28
  201.3 102.6 all-gather.30
  307.4 101.3 all-gather.32
  411.7 101.3 all-gather.34
  516.5 101.3 all-gather.36
  620.9 101.8 all-gather.44
  725.7 61.8 all-gather.38
  791.1 102.0 all-gather.42
  896.6 101.3 all-gather.40
  1097.7 94.4 reduce-scatter.24
  1197.2 94.5 reduce-scatter.26
  1298.3 262.5 reduce-scatter.22
  1567.1 263.3 reduce-scatter.20
  1836.8 348.1 reduce-scatter.14
  2192.4 347.5 reduce-scatter.12
  2546.3 472.8 reduce-scatter.18
  3026.7 472.2 reduce-scatter.16
where the time goes:
time: 3520 us; the launch traced here: 3510 us
  waiting for transfers between devices  2860 us (81%)
  matrix products  272 us (8%)
  blocking collectives  232 us (7%)
  other arithmetic  81.8 us (2%)
  local copies, waits for them, and re-layouts  35.4 us (1%)
    reduce_scatter x2, waiting for transfers between devices, layer_backward(): lax.psum_scatter(inner_rows(normed_ffn, both_values), ('dp', 'seq'), scat...  954 us
    reduce_scatter x2, waiting for transfers between devices, layer_backward(): lax.psum_scatter(jnp.concatenate([inner_rows(normed, grad_joint), inner_r...  705 us
    reduce_scatter x2, waiting for transfers between devices, layer_backward(): lax.psum_scatter(inner_rows(hidden, down_in), ('dp', 'seq'), scatter_dime...  498 us
    all_gather x2, waiting for transfers between devices, local(): lax.all_gather(up_weight, ('dp', 'seq'), axis=0, tiled=True)  197 us
    all_gather x2, waiting for transfers between devices, local(): lax.all_gather(down_weight, ('dp', 'seq'), axis=0, tiled=True)  186 us
    all_gather x2, waiting for transfers between devices, local(): lax.all_gather(gate_weight, ('dp', 'seq'), axis=0, tiled=True)  170 us
    all_gather x2, blocking collectives, local(): lax.all_gather(conv_weight, ('dp', 'seq'), axis=0, tiled=True)  146 us
    dot_general x8, matrix products, inner_rows(): lax.dot_general(left, right, (((0,), (0,)), ((), ())), preferred_element_...  105 us
  transfers between devices with their start and end apart: 22, of which 15 were waited for; matrix products, arithmetic and copies ran while one was open for 8% of the time, Pallas kernels for 0%

commit v1 on v0

v1 whole, which is shorter than its diff:
```python
import jax
import jax.numpy as jnp
from jax import lax
from jax.sharding import Mesh, PartitionSpec as P

EPSILON = 1e-05
TP = ("yl", "core", "xl")
DP = ("yh", "z", "xh")
ROW_AXES = ("yh", "yl", "core")
SEQ_AXES = ("z", "xh", "xl")
OWNERS = ROW_AXES + SEQ_AXES
BF16 = jnp.bfloat16
F32 = jnp.float32


def rms_scale(values):
    return lax.rsqrt(jnp.mean(values * values, axis=-1, keepdims=True) + EPSILON)


def matmul(left, right):
    return jnp.dot(left, right, preferred_element_type=F32)


def inner_rows(left, right):
    return lax.dot_general(left, right, (((0,), (0,)), ((), ())), preferred_element_type=F32)


def outer_cols(left, right):
    return lax.dot_general(left, right, (((1,), (1,)), ((), ())), preferred_element_type=F32)


def sizes_of(axes):
    return tuple(lax.axis_size(axis) for axis in axes)


def split_owners(array, dim):
    owners = sizes_of(OWNERS)
    count = 1
    for size in owners:
        count *= size
    shape = array.shape
    return array.reshape(shape[:dim] + owners + (shape[dim] // count,) + shape[dim + 1 :])


def column_shards(weight, groups):
    rows = weight.shape[0]
    parts = split_owners(weight.reshape(rows, groups, -1), 2)
    parts = parts.transpose(3, 4, 7, 0, 1, 2, 5, 6, 8)
    return parts.reshape(8, rows, -1)


def column_whole(shards, groups):
    rows = shards.shape[1]
    yh, yl, core, z, xh, xl = sizes_of(OWNERS)
    parts = shards.reshape(yl, core, xl, rows, groups, yh, z, xh, -1)
    return parts.transpose(3, 4, 5, 0, 1, 6, 7, 2, 8).reshape(rows, -1)


def gather_columns(shards):
    mine = lax.all_to_all(shards, TP, split_axis=0, concat_axis=0, tiled=True)
    whole = lax.all_gather(mine, DP, axis=0, tiled=False)
    yh, yl, core, z, xh, xl = sizes_of(OWNERS)
    rows, columns = shards.shape[1:]
    whole = whole.reshape(yh, z, xh, yl, core, xl, rows, columns)
    return whole.transpose(0, 3, 4, 1, 2, 5, 6, 7).reshape(-1, columns)


def scatter_columns(total):
    yh, yl, core, z, xh, xl = sizes_of(OWNERS)
    columns = total.shape[1]
    parts = split_owners(total, 0).transpose(0, 3, 4, 1, 2, 5, 6, 7)
    parts = parts.reshape(yh * z * xh, -1, columns)
    mine = lax.psum_scatter(parts, DP, scatter_dimension=0, tiled=False)
    mine = mine.reshape(8, -1, columns)
    return lax.all_to_all(mine, TP, split_axis=0, concat_axis=0, tiled=True)


def gather_tokens(array):
    return lax.all_gather(array, TP, axis=0, tiled=True)


def scatter_tokens(partial):
    return lax.psum_scatter(partial, TP, scatter_dimension=0, tiled=True)


def beside(array, by):
    axes = ("z", "xh")
    count = lax.axis_size("z") * lax.axis_size("xh")
    pairs = [(i, i + by) for i in range(count) if 0 <= i + by < count]
    return lax.ppermute(array, axes, pairs)


def tap_masks(starts, position_count):
    group = lax.axis_index("z") * lax.axis_size("xh") + lax.axis_index("xh")
    places = group * position_count + jnp.arange(position_count, dtype=jnp.int32)

    def segment_of(where):
        return jnp.sum((starts[:, None, :] <= where[None, :, None]).astype(jnp.int32), axis=2)

    own_segment = segment_of(places)
    keep_one = (segment_of(places - 1) == own_segment).astype(F32)[:, :, None]
    keep_two = (segment_of(places - 2) == own_segment).astype(F32)[:, :, None]
    return keep_one, keep_two


def conv_forward(joint, taps, keep_one, keep_two):
    rows, positions, _ = joint.shape
    b_part, c_part, x_part = jnp.split(joint, 3, axis=2)
    carried = b_part * x_part
    previous = beside(carried[:, positions - 2 :], 1)
    padded = jnp.concatenate([previous, carried], axis=1)
    mixed = (
        taps[:, 0] * padded[:, :positions] * keep_two
        + taps[:, 1] * padded[:, 1 : positions + 1] * keep_one
        + taps[:, 2] * carried
    )
    return (c_part * mixed).astype(BF16), mixed, padded


def conv_backward(grad_gated, joint, mixed, padded, taps, keep_one, keep_two):
    rows, positions, width = grad_gated.shape
    b_part, c_part, x_part = jnp.split(joint, 3, axis=2)
    grad_c = grad_gated * mixed
    grad_mixed = grad_gated * c_part
    first_tap = grad_mixed * keep_two
    second_tap = grad_mixed * keep_one
    grad_taps = jnp.stack(
        [
            jnp.sum(first_tap * padded[:, :positions], axis=(0, 1)),
            jnp.sum(second_tap * padded[:, 1 : positions + 1], axis=(0, 1)),
            jnp.sum(grad_mixed * padded[:, 2:], axis=(0, 1)),
        ],
        axis=0,
    )
    one = jnp.zeros((rows, 1, width), F32)
    two = jnp.zeros((rows, 2, width), F32)
    grad_padded = jnp.concatenate([first_tap * taps[:, 0], two], axis=1) + jnp.concatenate(
        [one, second_tap * taps[:, 1], one], axis=1
    )
    returned = beside(grad_padded[:, :2], -1)
    arriving = jnp.concatenate([jnp.zeros((rows, positions - 2, width), F32), returned], axis=1)
    grad_carried = grad_padded[:, 2:] + grad_mixed * taps[:, 2] + arriving
    grad_joint = jnp.concatenate([grad_carried * x_part, grad_c, grad_carried * b_part], axis=2)
    return grad_joint.astype(BF16), grad_taps


def local(stream_in, doc_starts, norm_mix, in_proj, conv_taps, out_proj, norm_ffn, w_gate, w_up, w_down, grad_out):
    batch_rows, token_count, features = stream_in.shape
    layers = norm_mix.shape[0]
    rows, positions = 4 * batch_rows, 2 * token_count
    tokens = rows * positions
    starts = lax.all_gather(doc_starts, ("yl", "core"), axis=0, tiled=True)
    keep_one, keep_two = tap_masks(starts, positions)

    def by_row(array):
        return array.reshape(4, 2, batch_rows, token_count, -1).transpose(0, 2, 1, 3, 4).reshape(rows, positions, -1)

    def by_device(array):
        return array.reshape(4, batch_rows, 2, token_count, -1).transpose(0, 2, 1, 3, 4).reshape(tokens, -1)

    small = jnp.concatenate(
        [norm_mix[:, :, None], norm_ffn[:, :, None], conv_taps], axis=2
    ).astype(BF16)
    gains = lax.all_gather(small[:, :, :2], OWNERS, axis=1, tiled=True).astype(F32)
    taps_all = lax.all_gather(small[:, :, 2:], DP, axis=1, tiled=True).astype(F32)
    weights = []
    for layer in range(layers):
        in_w = gather_columns(column_shards(in_proj[layer].astype(BF16), 3))
        out_w = lax.all_gather(out_proj[layer].astype(BF16), DP, axis=0, tiled=True)
        both = jnp.concatenate(
            [column_shards(w_gate[layer].astype(BF16), 1), column_shards(w_up[layer].astype(BF16), 1)], axis=2
        )
        both_w = gather_columns(both)
        down_w = lax.all_gather(w_down[layer].astype(BF16), DP, axis=0, tiled=True)
        weights.append((gains[layer, :, 0], in_w, taps_all[layer], out_w, gains[layer, :, 1], both_w, down_w))

    stream = stream_in.reshape(-1, features)
    saved = []
    for layer in range(layers):
        gain_mix, in_w, taps, out_w, gain_ffn, both_w, down_w = weights[layer]
        width = down_w.shape[0]
        scale_mix = rms_scale(stream)
        normed = gather_tokens((stream * scale_mix * gain_mix).astype(BF16))
        joint = by_row(matmul(normed, in_w))
        gated, mixed, padded = conv_forward(joint, taps, keep_one, keep_two)
        gated = by_device(gated)
        middle = stream + scatter_tokens(matmul(gated, out_w))
        scale_ffn = rms_scale(middle)
        normed_ffn = gather_tokens((middle * scale_ffn * gain_ffn).astype(BF16))
        gate_up = matmul(normed_ffn, both_w)
        gate, up = gate_up[:, :width], gate_up[:, width:]
        hidden = (jax.nn.silu(gate) * up).astype(BF16)
        result = middle + scatter_tokens(matmul(hidden, down_w))
        saved.append((stream, scale_mix, normed, joint, mixed, padded, gated, middle, scale_ffn, normed_ffn, gate, up, hidden))
        stream = result
    grad_stream = grad_out.reshape(-1, features)
    pieces = [None] * layers
    for layer in reversed(range(layers)):
        gain_mix, in_w, taps, out_w, gain_ffn, both_w, down_w = weights[layer]
        source, scale_mix, normed, joint, mixed, padded, gated, middle, scale_ffn, normed_ffn, gate, up, hidden = saved[layer]
        down_in = gather_tokens(grad_stream.astype(BF16))
        grad_down = lax.psum_scatter(inner_rows(hidden, down_in), DP, scatter_dimension=0, tiled=True)
        grad_hidden = outer_cols(down_in, down_w)
        sigmoid = jax.nn.sigmoid(gate)
        grad_gate_up = jnp.concatenate(
            [grad_hidden * up * sigmoid * (1.0 + gate * (1.0 - sigmoid)), grad_hidden * gate * sigmoid], axis=1
        ).astype(BF16)
        grad_both = scatter_columns(inner_rows(normed_ffn, grad_gate_up))
        width = down_w.shape[0]
        grad_gate = column_whole(grad_both[:, :, :width], 1)
        grad_up = column_whole(grad_both[:, :, width:], 1)
        grad_normed_ffn = scatter_tokens(outer_cols(grad_gate_up, both_w))
        grad_gain_ffn = jnp.sum(grad_normed_ffn * middle * scale_ffn, axis=0)
        scaled = grad_normed_ffn * gain_ffn
        grad_middle = grad_stream + scale_ffn * scaled - middle * scale_ffn**3 * jnp.mean(scaled * middle, axis=-1, keepdims=True)
        mix_in = gather_tokens(grad_middle.astype(BF16))
        grad_out_w = lax.psum_scatter(inner_rows(gated, mix_in), DP, scatter_dimension=0, tiled=True)
        grad_gated = by_row(outer_cols(mix_in, out_w))
        grad_joint, grad_taps = conv_backward(grad_gated, joint, mixed, padded, taps, keep_one, keep_two)
        grad_joint = by_device(grad_joint)
        grad_in_w = column_whole(scatter_columns(inner_rows(normed, grad_joint)), 3)
        grad_normed = scatter_tokens(outer_cols(grad_joint, in_w))
        grad_gain_mix = jnp.sum(grad_normed * source * scale_mix, axis=0)
        scaled = grad_normed * gain_mix
        grad_stream = grad_middle + scale_mix * scaled - source * scale_mix**3 * jnp.mean(scaled * source, axis=-1, keepdims=True)
        pieces[layer] = (grad_gain_mix, grad_in_w, grad_taps, grad_out_w, grad_gain_ffn, grad_gate, grad_up, grad_down)
    gain_grads = jnp.stack([jnp.stack([p[0], p[4]]) for p in pieces])
    gain_grads = lax.psum_scatter(gain_grads, OWNERS, scatter_dimension=2, tiled=True)
    tap_grads = lax.psum_scatter(jnp.stack([p[2] for p in pieces]), DP, scatter_dimension=2, tiled=True)
    return (
        stream.reshape(batch_rows, token_count, features),
        grad_stream.reshape(batch_rows, token_count, features),
        gain_grads[:, 0],
        jnp.stack([p[1] for p in pieces]),
        tap_grads.transpose(0, 2, 1),
        jnp.stack([p[3] for p in pieces]),
        gain_grads[:, 1],
        jnp.stack([p[5] for p in pieces]),
        jnp.stack([p[6] for p in pieces]),
        jnp.stack([p[7] for p in pieces]),
    )


def solution(mesh):
    dp, seq = mesh.shape["dp"], mesh.shape["seq"]
    side = dp // 2
    split = Mesh(mesh.devices.reshape(side // 2, 2, 2, seq // side, side // 2, 2), OWNERS)
    token = P(ROW_AXES, SEQ_AXES, None)
    vector = P(None, OWNERS)
    matrix = P(None, OWNERS, None)
    return jax.shard_map(
        local,
        mesh=split,
        in_specs=(token, P(ROW_AXES, None), vector, matrix, matrix, matrix, vector, matrix, matrix, matrix, token),
        out_specs=(token, token, vector, matrix, matrix, matrix, vector, matrix, matrix, matrix),
        check_vma=False,
    )
```

time: 3520 us -> 2070 us (0.59)
  waiting for transfers between devices: 2860 us -> 1410 us
  local copies, waits for them, and re-layouts: 35.4 us -> 175 us
  matrix products: 272 us -> 134 us
    reduce_scatter x6 -> x16, waiting for transfers between devices: 2160 us -> 832 us  [the longest x8 401 us: scatter_tokens(): return lax.psum_scatter(partial, TP, scatter_dimension=0, tiled=True)]
    all_gather x10 -> x14, waiting for transfers between devices: 700 us -> 432 us  [the longest x8 194 us: gather_tokens(): return lax.all_gather(array, TP, axis=0, tiled=True)]
    unnamed x20 -> x34, waiting for transfers between devices: 3.35 us -> 115 us
    all_to_all x0 -> x6, blocking collectives: none -> 108 us  [the longest x4 63.3 us: gather_columns(): mine = lax.all_to_all(shards, TP, split_axis=0, concat_axis=0, tiled=True)]
    unnamed x2 -> x0, blocking collectives: 85.9 us -> none
    dot_general x8, matrix products: 105 us -> 43 us  [inner_rows(): lax.dot_general(left, right, (((0,), (0,)), ((), ())), preferred_element_...]
    concatenate x2 -> x3, other arithmetic: 50.3 us -> 1.63 us  [the longest x2 1.62 us: local(): jnp.concatenate([column_shards(w_gate[layer].astype(BF16), 1), column_sha...]
    dot_general x10 -> x8, matrix products: 91.7 us -> 45.2 us  [outer_cols(): lax.dot_general(left, right, (((1,), (1,)), ((), ())), preferred_element_...]
  transfers between devices with their start and end apart: 22 -> 38, of which waited for: 15 -> 32; matrix products, arithmetic and copies ran while one was open for 8% -> 13% of each run, Pallas kernels for 0% -> 0%
where the time goes in v1:
time: 2070 us
  waiting for transfers between devices  1410 us (68%)
  blocking collectives  247 us (12%)
  local copies, waits for them, and re-layouts  175 us (8%)
  matrix products  134 us (6%)
  other arithmetic  61.9 us (3%)
  starting transfers between devices  20.7 us (1%)
    reduce_scatter x8, waiting for transfers between devices, scatter_tokens(): return lax.psum_scatter(partial, TP, scatter_dimension=0, tiled=True)  401 us
    reduce_scatter x4, waiting for transfers between devices, scatter_columns(): mine = lax.psum_scatter(parts, DP, scatter_dimension=0, tiled=False)  264 us
    all_gather x8, waiting for transfers between devices, gather_tokens(): return lax.all_gather(array, TP, axis=0, tiled=True)  194 us
    all_gather x4, waiting for transfers between devices, gather_columns(): whole = lax.all_gather(mine, DP, axis=0, tiled=False)  173 us
    unnamed x34, waiting for transfers between devices  115 us
    reduce_scatter x2, waiting for transfers between devices, local(): lax.psum_scatter(inner_rows(hidden, down_in), DP, scatter_dimension=0, ti...  109 us
    all_gather x1, blocking collectives, local(): lax.all_gather(small[:, :, :2], OWNERS, axis=1, tiled=True).astype(F32)  76.2 us
    all_gather x2, waiting for transfers between devices, local(): down_w = lax.all_gather(w_down[layer].astype(BF16), DP, axis=0, tiled=True)  65.5 us
  transfers between devices with their start and end apart: 38, of which 32 were waited for; matrix products, arithmetic and copies ran while one was open for 13% of the time, Pallas kernels for 0%

profile of v1, /device:TPU:0, one launch (start us, length us, event | category | flops | bytes accessed | tf_op | source)
XLA Modules:
  0.0 2068.4 jit_solution(14501591593344436665)
XLA Ops:
  11.9 14.1 all_to_all.40
  26.2 76.2 %all_gather.69 = bf16[2,1536,2]{2,0,1:T(2,128)(2,1)S(1)} all-gather(bf16[2,48,2]{2,0,1:T(2,128)(2,1)S(1)} %copy.231), channel_id=1, replica_groups=mesh['yh'=1,'yl'=2,'core'=2,'z'=4,'xh'=1,'xl'=2] {'yh','yl','core','z','..., dimensions={1}, use_global_device_ids=true | all-gather | bytes 12672 | tf_op jit(solution)/shard_map/all_gather | solution.py:164
  103.7 39.3 %slice_reduce_fusion = (f32[1536]{0:T(1024)}, f32[1536]{0:T(1024)}, f32[1536]{0:T(1024)S(1)}, f32[1536]{0:T(1024)S(1)}) fusion(f32[2,1536,2]{2,0,1:T(2,128)S(1)} %convert_element_type.154), kind=kLoop, calls=%fused_computation.56 | loop fusion | bytes 49152 | tf_op jit(solution)/shard_map/slice | solution.py:175
  149.1 13.4 all_gather.73
  182.0 22.2 %all-gather.1 = bf16[1,192,1536]{2,1,0:T(8,128)(2,1)S(1)} all-gather(bf16[1,48,1536]{2,1,0:T(8,128)(2,1)S(1)} %get-tuple-element.80), channel_id=3, replica_groups=mesh['yh'=1,'yl'=2,'core'=2,'z'=4,'xh'=1,'xl'=2] {'yh','z','xh'}, dimensions={1}, use_global_device_ids=true | all-gather | bytes 737280 | tf_op jit(solution)/shard_map/all_gather | solution.py:169
  220.0 16.5 all_to_all.41
  236.6 35.1 %reduce-scatter.23.cloned.1.call-done = f32[128,1536]{1,0:T(8,128)} async-done(((f32[1024,1536]{1,0:T(8,128)}), f32[128,1536]{1,0:T(8,128)}) %reduce-scatter.23.cloned.1.call-update) | async-done | bytes 786448 | tf_op jit(solution)/shard_map/reduce_scatter | solution.py:83
  277.5 65.7 %all-gather.42.cloned.1.call-done = bf16[32,48,1152]{2,1,0:T(8,128)(2,1)} async-done(((bf16[8,48,1152]{2,1,0:T(8,128)(2,1)}), bf16[32,48,1152]{2,1,0:T(8,128)(2,1)}) %all-gather.42.cloned.1.call-update) | async-done | bytes 3538960 | tf_op jit(solution)/shard_map/all_gather | solution.py:61
  347.3 29.3 %all-gather.26.cloned.1.call-done = bf16[1024,1536]{1,0:T(8,128)(2,1)} async-done(((bf16[128,1536]{1,0:T(8,128)(2,1)}), bf16[1024,1536]{1,0:T(8,128)(2,1)}) %all-gather.26.cloned.1.call-update) | async-done | bytes 3145744 | tf_op jit(solution)/shard_map/all_gather | solution.py:79
  376.6 7.2 fusion.70
  386.8 32.3 %all-gather.44.cloned.1.call-done = bf16[1,576,1536]{2,1,0:T(8,128)(2,1)} async-done(((bf16[1,144,1536]{2,1,0:T(8,128)(2,1)}), bf16[1,576,1536]{2,1,0:T(8,128)(2,1)}) %all-gather.44.cloned.1.call-update) | async-done | bytes 1769488 | tf_op jit(solution)/shard_map/all_gather | solution.py:174
  428.2 12.5 all_to_all.42
  440.8 45.0 %reduce-scatter.25.cloned.1.call-done = f32[128,1536]{1,0:T(8,128)} async-done(((f32[1024,1536]{1,0:T(8,128)}), f32[128,1536]{1,0:T(8,128)}) %reduce-scatter.25.cloned.1.call-update) | async-done | bytes 786448 | tf_op jit(solution)/shard_map/reduce_scatter | solution.py:83
  488.7 42.2 %all-gather.46.cloned.1.call-done = bf16[32,48,576]{2,1,0:T(8,128)(2,1)} async-done(((bf16[8,48,576]{2,1,0:T(8,128)(2,1)}), bf16[32,48,576]{2,1,0:T(8,128)(2,1)}) %all-gather.46.cloned.1.call-update) | async-done | bytes 1769488 | tf_op jit(solution)/shard_map/all_gather | solution.py:61
  533.9 30.6 %all-gather.28.cloned.1.call-done = bf16[1024,1536]{1,0:T(8,128)(2,1)} async-done(((bf16[128,1536]{1,0:T(8,128)(2,1)}), bf16[1024,1536]{1,0:T(8,128)(2,1)}) %all-gather.28.cloned.1.call-update) | async-done | bytes 3145744 | tf_op jit(solution)/shard_map/all_gather | solution.py:79
  572.8 22.3 %all-gather.5 = bf16[1,192,1536]{2,1,0:T(8,128)(2,1)S(1)} all-gather(bf16[1,48,1536]{2,1,0:T(8,128)(2,1)S(1)} %copy-done.38), channel_id=7, replica_groups=mesh['yh'=1,'yl'=2,'core'=2,'z'=4,'xh'=1,'xl'=2] {'yh','z','xh'}, dimensions={1}, use_global_device_ids=true | all-gather | bytes 737280 | tf_op jit(solution)/shard_map/all_gather | solution.py:169
  613.9 20.1 all_to_all.43
  634.1 30.7 %reduce-scatter.27.cloned.1.call-done = f32[128,1536]{1,0:T(8,128)} async-done(((f32[1024,1536]{1,0:T(8,128)}), f32[128,1536]{1,0:T(8,128)}) %reduce-scatter.27.cloned.1.call-update) | async-done | bytes 786448 | tf_op jit(solution)/shard_map/reduce_scatter | solution.py:83
  671.6 64.8 %all-gather.48.cloned.1.call-done = bf16[32,48,1152]{2,1,0:T(8,128)(2,1)} async-done(((bf16[8,48,1152]{2,1,0:T(8,128)(2,1)}), bf16[32,48,1152]{2,1,0:T(8,128)(2,1)}) %all-gather.48.cloned.1.call-update) | async-done | bytes 3538960 | tf_op jit(solution)/shard_map/all_gather | solution.py:61
  740.6 29.3 %all-gather.30.cloned.1.call-done = bf16[1024,1536]{1,0:T(8,128)(2,1)} async-done(((bf16[128,1536]{1,0:T(8,128)(2,1)}), bf16[1024,1536]{1,0:T(8,128)(2,1)}) %all-gather.30.cloned.1.call-update) | async-done | bytes 3145744 | tf_op jit(solution)/shard_map/all_gather | solution.py:79
  769.9 9.4 fusion.72
  779.3 33.2 %all-gather.50.cloned.1.call-done = bf16[1,576,1536]{2,1,0:T(8,128)(2,1)} async-done(((bf16[1,144,1536]{2,1,0:T(8,128)(2,1)}), bf16[1,576,1536]{2,1,0:T(8,128)(2,1)}) %all-gather.50.cloned.1.call-update) | async-done | bytes 1769488 | tf_op jit(solution)/shard_map/all_gather | solution.py:174
  812.5 33.7 %all-gather.32.cloned.1.call-done = bf16[1024,1536]{1,0:T(8,128)(2,1)} async-done(((bf16[128,1536]{1,0:T(8,128)(2,1)}), bf16[1024,1536]{1,0:T(8,128)(2,1)}) %all-gather.32.cloned.1.call-update) | async-done | bytes 3145744 | tf_op jit(solution)/shard_map/all_gather | solution.py:79
  846.1 8.2 multiply_convert_fusion.3
  862.2 7.3 fusion.2
  869.6 54.5 %reduce-scatter.31.cloned.1.call-done = f32[128,1536]{1,0:T(8,128)} async-done(((f32[1024,1536]{1,0:T(8,128)}), f32[128,1536]{1,0:T(8,128)}) %reduce-scatter.31.cloned.1.call-update) | async-done | bytes 786448 | tf_op jit(solution)/shard_map/reduce_scatter | solution.py:83
  926.6 62.5 %reduce-scatter.29.cloned.1.call-done = f32[128,1536]{1,0:T(8,128)} async-done(((f32[1024,1536]{1,0:T(8,128)}), f32[128,1536]{1,0:T(8,128)}) %reduce-scatter.29.cloned.1.call-update) | async-done | bytes 786448 | tf_op jit(solution)/shard_map/reduce_scatter | solution.py:83
  992.4 32.4 %all-gather.34.cloned.1.call-done = bf16[1024,1536]{1,0:T(8,128)(2,1)} async-done(((bf16[128,1536]{1,0:T(8,128)(2,1)}), bf16[1024,1536]{1,0:T(8,128)(2,1)}) %all-gather.34.cloned.1.call-update) | async-done | bytes 3145744 | tf_op jit(solution)/shard_map/all_gather | solution.py:79
  1031.8 11.6 collective-permute-done.2
  1050.6 60.9 %reduce-scatter.33.cloned.1.call-done = f32[128,1536]{1,0:T(8,128)} async-done(((f32[1024,1536]{1,0:T(8,128)}), f32[128,1536]{1,0:T(8,128)}) %reduce-scatter.33.cloned.1.call-update) | async-done | bytes 786448 | tf_op jit(solution)/shard_map/reduce_scatter | solution.py:83
  1116.2 32.4 %all-gather.36.cloned.1.call-done = bf16[1024,1536]{1,0:T(8,128)(2,1)} async-done(((bf16[128,1536]{1,0:T(8,128)(2,1)}), bf16[1024,1536]{1,0:T(8,128)(2,1)}) %all-gather.36.cloned.1.call-update) | async-done | bytes 3145744 | tf_op jit(solution)/shard_map/all_gather | solution.py:79
  1163.7 61.9 %reduce-scatter.35.cloned.1.call-done = f32[128,1536]{1,0:T(8,128)} async-done(((f32[1024,1536]{1,0:T(8,128)}), f32[128,1536]{1,0:T(8,128)}) %reduce-scatter.35.cloned.1.call-update) | async-done | bytes 786448 | tf_op jit(solution)/shard_map/reduce_scatter | solution.py:83
  1253.2 7.2 fusion.8
  1270.0 7.3 fusion.77
  1298.5 21.8 %collective-permute-done.3 = f32[4,2,192]{1,2,0:T(8,128)} collective-permute-done((f32[4,2,192]{1,2,0:T(8,128)}, f32[4,2,192]{1,2,0:T(8,128)}, u32[]{:S(2)}, u32[]{:S(2)}) %collective-permute-start.3) | collective-permute-done | bytes 6176 | tf_op jit(solution)/shard_map/ppermute | solution.py:90
  1343.4 53.4 %reduce-scatter.49.cloned.1.call-done = f32[1,384,1152]{2,1,0:T(8,128)} async-done(((f32[4,384,1152]{2,1,0:T(8,128)}), f32[1,384,1152]{2,1,0:T(8,128)}) %reduce-scatter.49.cloned.1.call-update) | async-done | bytes 1769488 | tf_op jit(solution)/shard_map/reduce_scatter | solution.py:73
  1396.8 26.3 %all_to_all.44 = f32[8,48,1152]{2,1,0:T(8,128)S(1)} all-to-all(f32[8,48,1152]{2,1,0:T(8,128)} %bitcast.317), channel_id=1, replica_groups=mesh['yh'=1,'yl'=2,'core'=2,'z'=4,'xh'=1,'xl'=2] {'yl','core','xl'}, dimensions={0} | all-to-all | bytes 3538944 | tf_op jit(solution)/shard_map/all_to_all | solution.py:75
  1423.0 49.3 %reduce-scatter.41.cloned.1.call-done = f32[1,384,576]{2,1,0:T(8,128)} async-done(((f32[4,384,576]{2,1,0:T(8,128)}), f32[1,384,576]{2,1,0:T(8,128)}) %reduce-scatter.41.cloned.1.call-update) | async-done | bytes 884752 | tf_op jit(solution)/shard_map/reduce_scatter | solution.py:73
  1472.4 18.5 all_to_all.45
  1490.9 107.6 %reduce-scatter.47.cloned.1.call-done = f32[1,384,1152]{2,1,0:T(8,128)} async-done(((f32[4,384,1152]{2,1,0:T(8,128)}), f32[1,384,1152]{2,1,0:T(8,128)}) %reduce-scatter.47.cloned.1.call-update) | async-done | bytes 1769488 | tf_op jit(solution)/shard_map/reduce_scatter | solution.py:73
  1627.6 40.3 %reduce-scatter.53.cloned.1.call-done = f32[144,1536]{1,0:T(8,128)} async-done(((f32[576,1536]{1,0:T(8,128)}), f32[144,1536]{1,0:T(8,128)}) %reduce-scatter.53.cloned.1.call-update) | async-done | bytes 884752 | tf_op jit(solution)/shard_map/reduce_scatter | solution.py:202
  1667.9 69.0 %reduce-scatter.51.cloned.1.call-done = f32[144,1536]{1,0:T(8,128)} async-done(((f32[576,1536]{1,0:T(8,128)}), f32[144,1536]{1,0:T(8,128)}) %reduce-scatter.51.cloned.1.call-update) | async-done | bytes 884752 | tf_op jit(solution)/shard_map/reduce_scatter | solution.py:202
  1739.6 18.8 reduce-scatter.57.cloned.1.call-done
  1777.7 53.9 %reduce-scatter.39.cloned.1.call-done = f32[1,384,576]{2,1,0:T(8,128)} async-done(((f32[4,384,576]{2,1,0:T(8,128)}), f32[1,384,576]{2,1,0:T(8,128)}) %reduce-scatter.39.cloned.1.call-update) | async-done | bytes 884752 | tf_op jit(solution)/shard_map/reduce_scatter | solution.py:73
  1836.8 27.2 %reduce-scatter.45.cloned.1.call-done = f32[48,1536]{1,0:T(8,128)} async-done(((f32[192,1536]{1,0:T(8,128)}), f32[48,1536]{1,0:T(8,128)}) %reduce-scatter.45.cloned.1.call-update) | async-done | bytes 294928 | tf_op jit(solution)/shard_map/reduce_scatter | solution.py:217
  1864.0 30.1 %reduce-scatter.43.cloned.1.call-done = f32[48,1536]{1,0:T(8,128)} async-done(((f32[192,1536]{1,0:T(8,128)}), f32[48,1536]{1,0:T(8,128)}) %reduce-scatter.43.cloned.1.call-update) | async-done | bytes 294928 | tf_op jit(solution)/shard_map/reduce_scatter | solution.py:217
  1907.2 50.8 %reduce-scatter.37.cloned.1.call-done = f32[128,1536]{1,0:T(8,128)} async-done(((f32[1024,1536]{1,0:T(8,128)}), f32[128,1536]{1,0:T(8,128)}) %reduce-scatter.37.cloned.1.call-update) | async-done | bytes 786448 | tf_op jit(solution)/shard_map/reduce_scatter | solution.py:83
  1964.4 95.0 %reduce-scatter.55.cloned.1.call-done = f32[48,4]{1,0:T(8,128)} async-done(((f32[1536,4]{1,0:T(8,128)}), f32[48,4]{1,0:T(8,128)}) %reduce-scatter.55.cloned.1.call-update) | async-done | bytes 784
  (403 shorter events, 319.2 us)
Async XLA Ops:
  7.2 157.1 %all-gather.40.cloned.1.call-start = ((), (), s32[]{:S(2)}) async-start(), calls=%async_computation.50 | async-start | bytes 2457600 | tf_op jit(solution)/shard_map/all_gather | solution.py:61
  11.9 91.1 %copy-start = (f32[1,128,1536]{2,1,0:T(8,128)S(1)}, f32[1,128,1536]{2,1,0:T(8,128)}, u32[]{:S(2)}) copy-start(f32[1,128,1536]{2,1,0:T(8,128)} %param.11) | copy-start | bytes 2359300
  26.0 147.7 %all-gather.24.cloned.1.call-start = ((), (), s32[]{:S(2)}) async-start(), calls=%async_computation.26 | async-start | bytes 3538944 | tf_op jit(solution)/shard_map/all_gather | solution.py:79
  143.9 127.8 %reduce-scatter.23.cloned.1.call-start = ((), (), s32[]{:S(2)}) async-start(), calls=%async_computation.27 | async-start | bytes 7077888 | tf_op jit(solution)/shard_map/reduce_scatter | solution.py:83
  178.6 25.7 %collective-permute-start = (f32[4,2,192]{1,2,0:T(8,128)S(1)}, f32[4,2,192]{1,2,0:T(8,128)S(1)}, u32[]{:S(2)}, u32[]{:S(2)}) collective-permute-start(f32[4,2,192]{1,2,0:T(8,128)S(1)} %slice.198), channel_id=1, source_target_pairs={{0,2},{2,4},{4,6},{1,3},{3,5},{5,7},{8,10},{10,12},{12,14},{9,11},... | collective-permute-start | bytes 18440 | tf_op jit(solution)/shard_map/ppermute | solution.py:90
  210.4 132.8 %all-gather.42.cloned.1.call-start = ((), (), s32[]{:S(2)}) async-start(), calls=%async_computation.51 | async-start | bytes 4423680 | tf_op jit(solution)/shard_map/all_gather | solution.py:61
  236.5 140.1 %all-gather.26.cloned.1.call-start = ((), (), s32[]{:S(2)}) async-start(), calls=%async_computation.28 | async-start | bytes 3538944 | tf_op jit(solution)/shard_map/all_gather | solution.py:79
  274.4 144.6 %all-gather.44.cloned.1.call-start = ((), (), s32[]{:S(2)}) async-start(), calls=%async_computation.52 | async-start | bytes 2211840 | tf_op jit(solution)/shard_map/all_gather | solution.py:174
  277.0 208.7 %reduce-scatter.25.cloned.1.call-start = ((), (), s32[]{:S(2)}) async-start(), calls=%async_computation.29 | async-start | bytes 7077888 | tf_op jit(solution)/shard_map/reduce_scatter | solution.py:83
  425.0 105.9 %all-gather.46.cloned.1.call-start = ((), (), s32[]{:S(2)}) async-start(), calls=%async_computation.53 | async-start | bytes 2457600 | tf_op jit(solution)/shard_map/all_gather | solution.py:61
  427.5 60.1 %copy-start.42 = (f32[1536]{0:T(1024)S(1)}, f32[1536]{0:T(1024)}, u32[]{:S(2)}) copy-start(f32[1536]{0:T(1024)} %get-tuple-element.25) | copy-start | bytes 18436
  440.7 123.8 %all-gather.28.cloned.1.call-start = ((), (), s32[]{:S(2)}) async-start(), calls=%async_computation.30 | async-start | bytes 3538944 | tf_op jit(solution)/shard_map/all_gather | solution.py:79
  488.5 176.3 %reduce-scatter.27.cloned.1.call-start = ((), (), s32[]{:S(2)}) async-start(), calls=%async_computation.31 | async-start | bytes 7077888 | tf_op jit(solution)/shard_map/reduce_scatter | solution.py:83
  488.6 106.5 %copy-start.54 = (f32[192,1]{0,1:T(1,128)}, f32[192,1]{0,1:T(1,128)S(1)}, u32[]{:S(2)}) copy-start(f32[192,1]{0,1:T(1,128)S(1)} %get-tuple-element.86) | copy-start | bytes 2308
  488.6 106.5 %copy-start.56 = (f32[192,1]{0,1:T(1,128)}, f32[192,1]{0,1:T(1,128)S(1)}, u32[]{:S(2)}) copy-start(f32[192,1]{0,1:T(1,128)S(1)} %get-tuple-element.87) | copy-start | bytes 2308
  488.6 106.5 %copy-start.58 = (f32[192,1]{0,1:T(1,128)}, f32[192,1]{0,1:T(1,128)S(1)}, u32[]{:S(2)}) copy-start(f32[192,1]{0,1:T(1,128)S(1)} %get-tuple-element.85) | copy-start | bytes 2308
  569.4 25.7 %collective-permute-start.1 = (f32[4,2,192]{1,2,0:T(8,128)S(1)}, f32[4,2,192]{1,2,0:T(8,128)S(1)}, u32[]{:S(2)}, u32[]{:S(2)}) collective-permute-start(f32[4,2,192]{1,2,0:T(8,128)S(1)} %slice.214), channel_id=1, source_target_pairs={{0,2},{2,4},{4,6},{1,3},{3,5},{5,7},{8,10},{10,12},{12,14},{9,11},... | collective-permute-start | bytes 18440 | tf_op jit(solution)/shard_map/ppermute | solution.py:90
  600.4 136.1 %all-gather.48.cloned.1.call-start = ((), (), s32[]{:S(2)}) async-start(), calls=%async_computation.54 | async-start | bytes 4423680 | tf_op jit(solution)/shard_map/all_gather | solution.py:61
  634.1 135.8 %all-gather.30.cloned.1.call-start = ((), (), s32[]{:S(2)}) async-start(), calls=%async_computation.32 | async-start | bytes 3538944 | tf_op jit(solution)/shard_map/all_gather | solution.py:79
  668.9 143.6 %all-gather.50.cloned.1.call-start = ((), (), s32[]{:S(2)}) async-start(), calls=%async_computation.55 | async-start | bytes 2211840 | tf_op jit(solution)/shard_map/all_gather | solution.py:174
  669.6 176.5 %all-gather.32.cloned.1.call-start = ((), (), s32[]{:S(2)}) async-start(), calls=%async_computation.34 | async-start | bytes 3538944 | tf_op jit(solution)/shard_map/all_gather | solution.py:79
  671.6 252.5 %reduce-scatter.31.cloned.1.call-start = ((), (), s32[]{:S(2)}) async-start(), calls=%async_computation.35 | async-start | bytes 7077888 | tf_op jit(solution)/shard_map/reduce_scatter | solution.py:83
  862.2 126.9 %reduce-scatter.29.cloned.1.call-start = ((), (), s32[]{:S(2)}) async-start(), calls=%async_computation.33 | async-start | bytes 7077888 | tf_op jit(solution)/shard_map/reduce_scatter | solution.py:83
  869.6 155.2 %all-gather.34.cloned.1.call-start = ((), (), s32[]{:S(2)}) async-start(), calls=%async_computation.36 | async-start | bytes 3538944 | tf_op jit(solution)/shard_map/all_gather | solution.py:79
  992.3 119.2 %reduce-scatter.33.cloned.1.call-start = ((), (), s32[]{:S(2)}) async-start(), calls=%async_computation.37 | async-start | bytes 7077888 | tf_op jit(solution)/shard_map/reduce_scatter | solution.py:83
  1030.3 13.2 collective-permute-start.2
  1050.6 98.1 %all-gather.36.cloned.1.call-start = ((), (), s32[]{:S(2)}) async-start(), calls=%async_computation.38 | async-start | bytes 3538944 | tf_op jit(solution)/shard_map/all_gather | solution.py:79
  1116.2 109.4 %reduce-scatter.35.cloned.1.call-start = ((), (), s32[]{:S(2)}) async-start(), calls=%async_computation.39 | async-start | bytes 7077888 | tf_op jit(solution)/shard_map/reduce_scatter | solution.py:83
  1163.7 63.9 %copy-start.23 = (f32[128,1536]{1,0:T(8,128)S(1)}, f32[128,1536]{1,0:T(8,128)}, u32[]{:S(2)}) copy-start(f32[128,1536]{1,0:T(8,128)} %get-tuple-element.38) | copy-start | bytes 2359300
  1163.7 118.4 %all-gather.38.cloned.1.call-start = ((), (), s32[]{:S(2)}) async-start(), calls=%async_computation.40 | async-start | bytes 3538944 | tf_op jit(solution)/shard_map/all_gather | solution.py:79
  1230.0 166.8 %reduce-scatter.49.cloned.1.call-start = ((), (), s32[]{:S(2)}) async-start(), calls=%async_computation.47 | async-start | bytes 8847360 | tf_op jit(solution)/shard_map/reduce_scatter | solution.py:73
  1241.0 231.4 %reduce-scatter.41.cloned.1.call-start = ((), (), s32[]{:S(2)}) async-start(), calls=%async_computation.43 | async-start | bytes 4915200 | tf_op jit(solution)/shard_map/reduce_scatter | solution.py:73
  1252.9 345.6 %reduce-scatter.47.cloned.1.call-start = ((), (), s32[]{:S(2)}) async-start(), calls=%async_computation.46 | async-start | bytes 8847360 | tf_op jit(solution)/shard_map/reduce_scatter | solution.py:73
  1263.8 404.1 %reduce-scatter.53.cloned.1.call-start = ((), (), s32[]{:S(2)}) async-start(), calls=%async_computation.49 | async-start | bytes 4423680 | tf_op jit(solution)/shard_map/reduce_scatter | solution.py:202
  1269.9 466.9 %reduce-scatter.51.cloned.1.call-start = ((), (), s32[]{:S(2)}) async-start(), calls=%async_computation.48 | async-start | bytes 4423680 | tf_op jit(solution)/shard_map/reduce_scatter | solution.py:202
  1277.3 481.1 %reduce-scatter.57.cloned.1.call-start = ((), (), s32[]{:S(2)}) async-start(), calls=%async_computation.57 | async-start | bytes 122880
  1292.1 28.1 %collective-permute-start.3 = (f32[4,2,192]{1,2,0:T(8,128)}, f32[4,2,192]{1,2,0:T(8,128)}, u32[]{:S(2)}, u32[]{:S(2)}) collective-permute-start(f32[4,2,192]{1,2,0:T(8,128)} %slice.229), channel_id=1, source_target_pairs={{2,0},{4,2},{6,4},{3,1},{5,3},{7,5},{10,8},{12,10},{14,12},{11,9},... | collective-permute-start | bytes 18440 | tf_op jit(solution)/shard_map/ppermute | solution.py:90
  1298.0 533.6 %reduce-scatter.39.cloned.1.call-start = ((), (), s32[]{:S(2)}) async-start(), calls=%async_computation.42 | async-start | bytes 4915200 | tf_op jit(solution)/shard_map/reduce_scatter | solution.py:73
  1329.5 534.6 %reduce-scatter.45.cloned.1.call-start = ((), (), s32[]{:S(2)}) async-start(), calls=%async_computation.45 | async-start | bytes 1474560 | tf_op jit(solution)/shard_map/reduce_scatter | solution.py:217
  1333.4 560.7 %reduce-scatter.43.cloned.1.call-start = ((), (), s32[]{:S(2)}) async-start(), calls=%async_computation.44 | async-start | bytes 1474560 | tf_op jit(solution)/shard_map/reduce_scatter | solution.py:217
  1337.3 620.7 %reduce-scatter.37.cloned.1.call-start = ((), (), s32[]{:S(2)}) async-start(), calls=%async_computation.41 | async-start | bytes 7077888 | tf_op jit(solution)/shard_map/reduce_scatter | solution.py:83
  1472.4 130.5 %copy-start.45 = (f32[1536]{0:T(1024)S(1)}, f32[1536]{0:T(1024)}, u32[]{:S(2)}) copy-start(f32[1536]{0:T(1024)} %get-tuple-element.22) | copy-start | bytes 18436
  1598.5 161.4 %all-to-all-start.6 = ((f32[8,48,1152]{2,1,0:T(8,128)}), f32[8,48,1152]{2,1,0:T(8,128)}, u32[]{:S(2)}, u32[]{:S(2)}) async-start(f32[8,48,1152]{2,1,0:T(8,128)} %bitcast.316), calls=%async_computation.19 | async-start | bytes 3538944 | tf_op jit(solution)/shard_map/all_to_all | solution.py:75
  1627.5 112.0 %copy-start.47 = (f32[1536]{0:T(1024)S(1)}, f32[1536]{0:T(1024)}, u32[]{:S(2)}) copy-start(f32[1536]{0:T(1024)} %get-tuple-element.18) | copy-start | bytes 18436
  1774.8 60.7 %copy-start.15 = (f32[1,48,4608]{2,1,0:T(8,128)S(1)}, f32[1,48,4608]{2,1,0:T(8,128)}, u32[]{:S(2)}) copy-start(f32[1,48,4608]{2,1,0:T(8,128)} %stack_reshape.21) | copy-start | bytes 2654212
  1774.8 60.7 %copy-start.16 = (f32[1,48,4608]{2,1,0:T(8,128)S(1)}, f32[1,48,4608]{2,1,0:T(8,128)}, u32[]{:S(2)}) copy-start(f32[1,48,4608]{2,1,0:T(8,128)} %stack_reshape.20) | copy-start | bytes 2654212
  1831.6 64.5 %all-to-all-start.4 = ((f32[8,48,576]{2,1,0:T(8,128)}), f32[8,48,576]{2,1,0:T(8,128)S(1)}, u32[]{:S(2)}, u32[]{:S(2)}) async-start(f32[8,48,576]{2,1,0:T(8,128)} %bitcast.326), calls=%async_computation.13 | async-start | bytes 1966080 | tf_op jit(solution)/shard_map/all_to_all | solution.py:75
  1835.4 224.0 %reduce-scatter.55.cloned.1.call-start = ((), (), s32[]{:S(2)}) async-start(), calls=%async_computation.56 | async-start | bytes 811008
  (63 other events, 972.9 us)
Sparse Core Ops, SparseCore 0:
  26.1 47.1 all-gather.39
  144.0 29.7 all-gather.23
  210.5 61.1 reduce-scatter.22
  273.2 69.9 all-gather.41
  345.7 30.8 all-gather.25
  378.7 40.3 all-gather.43
  425.1 60.5 reduce-scatter.24
  487.3 43.5 all-gather.45
  533.4 31.1 all-gather.27
  600.5 64.2 reduce-scatter.26
  666.5 69.9 all-gather.47
  738.9 30.8 all-gather.29
  772.1 40.3 all-gather.49
  814.9 31.1 all-gather.31
  862.3 61.7 reduce-scatter.30
  927.3 61.7 reduce-scatter.28
  992.5 32.2 all-gather.33
  1050.7 60.8 reduce-scatter.32
  1116.3 32.2 all-gather.35
  1163.8 61.7 reduce-scatter.34
  1230.1 32.2 all-gather.37
  1264.8 131.9 reduce-scatter.48
  1399.2 73.1 reduce-scatter.40
  1474.6 123.8 reduce-scatter.46
  1600.9 66.8 reduce-scatter.52
  1670.1 66.6 reduce-scatter.50
  1739.0 19.3 reduce-scatter.56
  1760.7 70.8 reduce-scatter.38
  1834.5 29.5 reduce-scatter.44
  1866.2 27.8 reduce-scatter.42
  1897.5 60.4 reduce-scatter.36
  1963.9 95.4 reduce-scatter.54

commit v2 on v1

v2 whole, which is shorter than its diff:
```python
import functools

import jax
import jax.numpy as jnp
from jax import lax
from jax.experimental import pallas as pl
from jax.experimental.pallas import tpu as pltpu
from jax.sharding import Mesh, PartitionSpec as P

EPSILON = 1e-05
TP = ("zl", "yl", "core")
DP = ("yh", "zh", "x")
ROW_AXES = ("yh", "yl", "core")
SEQ_AXES = ("zh", "zl", "x")
OWNERS = ROW_AXES + SEQ_AXES
BF16 = jnp.bfloat16
F32 = jnp.float32
MESH = pl.DeviceIdType.MESH
HALVES = 2
IN_NAMES = {
    "first": ("stream", "gain"),
    "fwd": ("partial", "stream", "gain"),
    "turn": ("partial", "stream", "grad"),
    "bwd": ("partial", "grad", "stream", "gain"),
    "last": ("partial", "grad", "stream", "gain"),
}
OUT_NAMES = {
    "first": ("whole",),
    "fwd": ("stream_next", "whole"),
    "turn": ("stream_next", "whole"),
    "bwd": ("grad_next", "gain_grad", "whole"),
    "last": ("grad_next", "gain_grad"),
}
COLLECTIVE_ID = {"first": 0, "fwd": 1, "turn": 2, "bwd": 3, "last": 4}


def rms_scale(values):
    return lax.rsqrt(jnp.mean(values * values, axis=-1, keepdims=True) + EPSILON)


def exchange_kernel(kind, *refs):
    names = IN_NAMES[kind] + OUT_NAMES[kind]
    ref = dict(zip(names, refs))
    refs = refs[len(names) :]
    near, sib, yin, yout, zin, zout, mine, local_sem, sums_send, sums_recv, all_send, all_recv = refs
    zl, yl, core = (lax.axis_index(axis) for axis in TP)
    tokens = mine.shape[0]
    half = tokens // HALVES
    to_sibling, to_y, to_z = {"core": 1 - core}, {"yl": 1 - yl}, {"zl": 1 - zl}

    def rank(flip_z, flip_y, flip_core):
        return (1 - zl if flip_z else zl) * 4 + (1 - yl if flip_y else yl) * 2 + (1 - core if flip_core else core)

    def part(h):
        return pl.ds(h * half, half)

    reduces, gathers = kind != "first", kind != "last"
    chips = ((1, 1), (0, 1), (1, 0), (0, 0))
    if reduces:
        near_copies = [
            pltpu.make_async_copy(ref["partial"].at[rank(*chip, 0)], near.at[i], local_sem.at[i])
            for i, chip in enumerate(chips)
        ]
        for copy in near_copies:
            copy.start()
    if kind == "first":
        stream = ref["stream"][...]
        mine[...] = (stream * rms_scale(stream) * ref["gain"][...]).astype(BF16)
    if kind == "turn":
        mine[...] = ref["grad"][...].astype(BF16)

    barrier = pltpu.get_barrier_semaphore()
    for partner in (to_sibling, to_y, to_z):
        pl.semaphore_signal(barrier, inc=1, device_id=partner, device_id_type=MESH)
    pl.semaphore_wait(barrier, 3)

    def sums_copy(index, src, dst, device):
        return pltpu.make_async_remote_copy(
            src_ref=src, dst_ref=dst, send_sem=sums_send.at[index], recv_sem=sums_recv.at[index],
            device_id=device, device_id_type=MESH,
        )

    def gather_copy(index, src, dst, device):
        return pltpu.make_async_remote_copy(
            src_ref=src, dst_ref=dst, send_sem=all_send.at[index], recv_sem=all_recv.at[index],
            device_id=device, device_id_type=MESH,
        )

    waits = []
    own_places = []
    from_z, from_y, from_corner, to_core = [], [], [], []
    if gathers:
        whole = ref["whole"]
        n = HALVES
        own, beside_z, beside_y, corner = (rank(*chip, 0) for chip in ((0, 0), (1, 0), (0, 1), (1, 1)))
        for h in range(HALVES):
            rows = part(h)
            own_places.append(pltpu.make_async_copy(mine.at[rows], whole.at[own, rows], local_sem.at[4 + h]))
            to_core.append(gather_copy(h, mine.at[rows], whole.at[own, rows], to_sibling))
            from_z.append(gather_copy(n + h, mine.at[rows], whole.at[own, rows], to_z))
            from_y.append(gather_copy(2 * n + h, mine.at[rows], whole.at[own, rows], to_y))
        for h in range(HALVES):
            rows = part(h)
            from_corner.append(
                gather_copy(3 * n + h, whole.at[beside_z, rows], whole.at[beside_z, rows], to_y)
            )
        for i, place in enumerate((beside_z, beside_y, corner)):
            for h in range(HALVES):
                rows = part(h)
                to_core.append(gather_copy((4 + i) * n + h, whole.at[place, rows], whole.at[place, rows], to_sibling))

    def send_mine(h):
        from_z[h].start()
        from_y[h].start()
        to_core[h].start()
        own_places[h].start()

    if kind in ("first", "turn"):
        for h in range(HALVES):
            send_mine(h)

    if reduces:
        sib_copies = [
            sums_copy(i, ref["partial"].at[rank(*chip, 1)], sib.at[i], to_sibling) for i, chip in enumerate(chips)
        ]
        for copy in sib_copies:
            copy.start()
        y_copies = [
            [sums_copy(4 + i * HALVES + h, yout.at[i, part(h)], yin.at[i, part(h)], to_y) for h in range(HALVES)]
            for i in range(2)
        ]
        z_copies = [
            sums_copy(4 + 2 * HALVES + h, zout.at[part(h)], zin.at[part(h)], to_z) for h in range(HALVES)
        ]

        def chip_sum(i, h):
            return near[i, part(h)].astype(F32) + sib[i, part(h)].astype(F32)

        for i in range(2):
            near_copies[i].wait()
            sib_copies[i].wait_recv()
            for h in range(HALVES):
                yout[i, part(h)] = chip_sum(i, h).astype(BF16)
                y_copies[i][h].start()
        near_copies[2].wait()
        sib_copies[2].wait_recv()
        for h in range(HALVES):
            y_copies[0][h].wait_recv()
            zout[part(h)] = (chip_sum(2, h) + yin[0, part(h)].astype(F32)).astype(BF16)
            z_copies[h].start()
        near_copies[3].wait()
        sib_copies[3].wait_recv()
        for h in range(HALVES):
            rows = part(h)
            y_copies[1][h].wait_recv()
            z_copies[h].wait_recv()
            total = chip_sum(3, h) + yin[1, rows].astype(F32) + zin[rows].astype(F32)
            stream = ref["stream"][rows]
            if kind in ("fwd", "turn"):
                stream = stream + total
                ref["stream_next"][rows] = stream
            if kind == "fwd":
                mine[rows] = (stream * rms_scale(stream) * ref["gain"][...]).astype(BF16)
                send_mine(h)
            if kind in ("bwd", "last"):
                scale = rms_scale(stream)
                gain_grad = jnp.sum(total * stream * scale, axis=0, keepdims=True)
                ref["gain_grad"][...] = gain_grad if h == 0 else ref["gain_grad"][...] + gain_grad
                scaled = total * ref["gain"][...]
                grad = (
                    ref["grad"][rows]
                    + scale * scaled
                    - stream * (scale * scale * scale) * jnp.mean(scaled * stream, axis=-1, keepdims=True)
                )
                ref["grad_next"][rows] = grad
                if kind == "bwd":
                    mine[rows] = grad.astype(BF16)
                    send_mine(h)
        waits += sib_copies + y_copies[0] + y_copies[1] + z_copies

    if gathers:
        n = HALVES
        for h in range(HALVES):
            from_z[h].wait_recv()
            from_corner[h].start()
            to_core[n + h].start()
        for h in range(HALVES):
            from_y[h].wait_recv()
            to_core[2 * n + h].start()
        for h in range(HALVES):
            from_corner[h].wait_recv()
            to_core[3 * n + h].start()
        for copy in to_core:
            copy.wait_recv()
        waits += from_z + from_y + from_corner + to_core
        for copy in own_places:
            copy.wait()
    for copy in waits:
        copy.wait_send()


def exchange(kind, *operands):
    tokens, features = operands[-2 if kind in ("first", "fwd", "turn") else 1].shape
    shapes = {
        "whole": jax.ShapeDtypeStruct((8, tokens, features), BF16),
        "stream_next": jax.ShapeDtypeStruct((tokens, features), F32),
        "grad_next": jax.ShapeDtypeStruct((tokens, features), F32),
        "gain_grad": jax.ShapeDtypeStruct((1, features), F32),
    }
    anywhere = pl.BlockSpec(memory_space=pl.ANY)
    inside = pl.BlockSpec(memory_space=pltpu.VMEM)
    block = (tokens, features)
    return pl.pallas_call(
        functools.partial(exchange_kernel, kind),
        out_shape=tuple(shapes[name] for name in OUT_NAMES[kind]),
        in_specs=[anywhere if name == "partial" else inside for name in IN_NAMES[kind]],
        out_specs=tuple(anywhere if name == "whole" else inside for name in OUT_NAMES[kind]),
        scratch_shapes=[
            pltpu.VMEM((4,) + block, BF16),
            pltpu.VMEM((4,) + block, BF16),
            pltpu.VMEM((2,) + block, BF16),
            pltpu.VMEM((2,) + block, BF16),
            pltpu.VMEM(block, BF16),
            pltpu.VMEM(block, BF16),
            pltpu.VMEM(block, BF16),
            pltpu.SemaphoreType.DMA((4 + HALVES,)),
            pltpu.SemaphoreType.DMA((4 + 3 * HALVES,)),
            pltpu.SemaphoreType.DMA((4 + 3 * HALVES,)),
            pltpu.SemaphoreType.DMA((7 * HALVES,)),
            pltpu.SemaphoreType.DMA((7 * HALVES,)),
        ],
        compiler_params=pltpu.CompilerParams(
            collective_id=COLLECTIVE_ID[kind], has_side_effects=True, vmem_limit_bytes=40 << 20
        ),
        cost_estimate=pl.CostEstimate(flops=10**7, bytes_accessed=150 * 10**6, transcendentals=0),
        name="exchange_" + kind,
    )(*operands)


def matmul(left, right):
    return jnp.dot(left, right, preferred_element_type=F32)


def inner_rows(left, right):
    return lax.dot_general(left, right, (((0,), (0,)), ((), ())), preferred_element_type=F32)


def outer_cols(left, right):
    return lax.dot_general(left, right, (((1,), (1,)), ((), ())), preferred_element_type=F32)


def sizes_of(axes):
    return tuple(lax.axis_size(axis) for axis in axes)


def split_owners(array, dim):
    owners = sizes_of(OWNERS)
    count = 1
    for size in owners:
        count *= size
    shape = array.shape
    return array.reshape(shape[:dim] + owners + (shape[dim] // count,) + shape[dim + 1 :])


def column_shards(weight, groups):
    rows = weight.shape[0]
    parts = split_owners(weight.reshape(rows, groups, -1), 2)
    return parts.transpose(6, 3, 4, 0, 1, 2, 5, 7, 8).reshape(8, rows, -1)


def column_whole(shards, groups):
    rows = shards.shape[1]
    yh, yl, core, zh, zl, x = sizes_of(OWNERS)
    parts = shards.reshape(zl, yl, core, rows, groups, yh, zh, x, -1)
    return parts.transpose(3, 4, 5, 1, 2, 6, 0, 7, 8).reshape(rows, -1)


def gather_columns(shards):
    mine = lax.all_to_all(shards, TP, split_axis=0, concat_axis=0, tiled=True)
    whole = lax.all_gather(mine, DP, axis=0, tiled=False)
    yh, yl, core, zh, zl, x = sizes_of(OWNERS)
    rows, columns = shards.shape[1:]
    whole = whole.reshape(yh, zh, x, zl, yl, core, rows, columns)
    return whole.transpose(0, 4, 5, 1, 3, 2, 6, 7).reshape(-1, columns)


def scatter_columns(total):
    yh, yl, core, zh, zl, x = sizes_of(OWNERS)
    columns = total.shape[1]
    parts = split_owners(total, 0).transpose(0, 3, 5, 4, 1, 2, 6, 7)
    parts = parts.reshape(yh * zh * x, -1, columns)
    mine = lax.psum_scatter(parts, DP, scatter_dimension=0, tiled=False)
    mine = mine.reshape(8, -1, columns)
    return lax.all_to_all(mine, TP, split_axis=0, concat_axis=0, tiled=True)


def tails_before(tails):
    x_size, zh_size = lax.axis_size("x"), lax.axis_size("zh")
    tails = tails.reshape((2, 4) + tails.shape[1:])
    beside = lax.ppermute(tails, "x", [(i, (i + 1) % x_size) for i in range(x_size)])
    pairs = [(i * x_size + x_size - 1, (i + 1) * x_size) for i in range(zh_size - 1)]
    below = lax.ppermute(tails[1], ("zh", "x"), pairs)
    first = jnp.stack([below, beside[0]])
    return jnp.where(lax.axis_index("x") == 0, first, beside).reshape((8,) + tails.shape[2:])


def heads_after(heads):
    x_size, zh_size = lax.axis_size("x"), lax.axis_size("zh")
    heads = heads.reshape((2, 4) + heads.shape[1:])
    beside = lax.ppermute(heads, "x", [((i + 1) % x_size, i) for i in range(x_size)])
    pairs = [((i + 1) * x_size, i * x_size + x_size - 1) for i in range(zh_size - 1)]
    above = lax.ppermute(heads[0], ("zh", "x"), pairs)
    final = jnp.stack([beside[1], above])
    return jnp.where(lax.axis_index("x") == x_size - 1, final, beside).reshape((8,) + heads.shape[2:])


def tap_masks(starts, token_count):
    zh, x, x_size = lax.axis_index("zh"), lax.axis_index("x"), lax.axis_size("x")
    blocks = (zh * 2 + jnp.arange(2, dtype=jnp.int32)) * x_size + x
    places = blocks[:, None] * token_count + jnp.arange(token_count, dtype=jnp.int32)

    def segment_of(where):
        return jnp.sum((starts[None, :, None, :] <= where[:, None, :, None]).astype(jnp.int32), axis=3)

    own_segment = segment_of(places)
    keep_one = (segment_of(places - 1) == own_segment).astype(F32)
    keep_two = (segment_of(places - 2) == own_segment).astype(F32)
    return keep_one.reshape(8, token_count, 1), keep_two.reshape(8, token_count, 1)


def conv_forward(joint, taps, keep_one, keep_two):
    positions = joint.shape[1]
    b_part, c_part, x_part = jnp.split(joint, 3, axis=2)
    carried = b_part * x_part
    previous = tails_before(carried[:, positions - 2 :])
    padded = jnp.concatenate([previous, carried], axis=1)
    mixed = (
        taps[:, 0] * padded[:, :positions] * keep_two
        + taps[:, 1] * padded[:, 1 : positions + 1] * keep_one
        + taps[:, 2] * carried
    )
    return (c_part * mixed).astype(BF16), mixed, padded


def conv_backward(grad_gated, joint, mixed, padded, taps, keep_one, keep_two):
    rows, positions, width = grad_gated.shape
    b_part, c_part, x_part = jnp.split(joint, 3, axis=2)
    grad_c = grad_gated * mixed
    grad_mixed = grad_gated * c_part
    first_tap = grad_mixed * keep_two
    second_tap = grad_mixed * keep_one
    grad_taps = jnp.stack(
        [
            jnp.sum(first_tap * padded[:, :positions], axis=(0, 1)),
            jnp.sum(second_tap * padded[:, 1 : positions + 1], axis=(0, 1)),
            jnp.sum(grad_mixed * padded[:, 2:], axis=(0, 1)),
        ],
        axis=0,
    )
    one = jnp.zeros((rows, 1, width), F32)
    two = jnp.zeros((rows, 2, width), F32)
    grad_padded = jnp.concatenate([first_tap * taps[:, 0], two], axis=1) + jnp.concatenate(
        [one, second_tap * taps[:, 1], one], axis=1
    )
    returned = heads_after(grad_padded[:, :2])
    arriving = jnp.concatenate([jnp.zeros((rows, positions - 2, width), F32), returned], axis=1)
    grad_carried = grad_padded[:, 2:] + grad_mixed * taps[:, 2] + arriving
    grad_joint = jnp.concatenate([grad_carried * x_part, grad_c, grad_carried * b_part], axis=2)
    return grad_joint.astype(BF16), grad_taps


def local(stream_in, doc_starts, norm_mix, in_proj, conv_taps, out_proj, norm_ffn, w_gate, w_up, w_down, grad_out):
    _, token_count, features = stream_in.shape
    layers = norm_mix.shape[0]
    starts = lax.all_gather(doc_starts, ("yl", "core"), axis=0, tiled=True)
    keep_one, keep_two = tap_masks(starts, token_count)

    def blocks(array):
        return array.reshape(8, token_count, -1)

    def flat(array):
        return array.reshape(8 * token_count, -1)

    small = jnp.concatenate([norm_mix[:, :, None], norm_ffn[:, :, None], conv_taps], axis=2).astype(BF16)
    gains = lax.all_gather(small[:, :, :2], OWNERS, axis=1, tiled=True).astype(F32)
    gains = gains.transpose(0, 2, 1).reshape(layers, 2, 1, features)
    taps_all = lax.all_gather(small[:, :, 2:], DP, axis=1, tiled=True).astype(F32)
    weights = []
    for layer in range(layers):
        in_w = gather_columns(column_shards(in_proj[layer].astype(BF16), 3))
        out_w = lax.all_gather(out_proj[layer].astype(BF16), DP, axis=0, tiled=True)
        both = jnp.concatenate(
            [column_shards(w_gate[layer].astype(BF16), 1), column_shards(w_up[layer].astype(BF16), 1)], axis=2
        )
        both_w = gather_columns(both)
        down_w = lax.all_gather(w_down[layer].astype(BF16), DP, axis=0, tiled=True)
        weights.append((in_w, taps_all[layer], out_w, both_w, down_w))

    stream = stream_in.reshape(-1, features)
    grad_stream = grad_out.reshape(-1, features)
    saved = []
    (normed,) = exchange("first", stream, gains[0, 0])
    for layer in range(layers):
        in_w, taps, out_w, both_w, down_w = weights[layer]
        width = down_w.shape[0]
        normed = flat(normed)
        joint = blocks(matmul(normed, in_w))
        gated, mixed, padded = conv_forward(joint, taps, keep_one, keep_two)
        gated = flat(gated)
        middle, normed_ffn = exchange("fwd", blocks(matmul(gated, out_w).astype(BF16)), stream, gains[layer, 1])
        normed_ffn = flat(normed_ffn)
        gate_up = matmul(normed_ffn, both_w)
        gate, up = gate_up[:, :width], gate_up[:, width:]
        hidden = (jax.nn.silu(gate) * up).astype(BF16)
        saved.append((stream, normed, joint, mixed, padded, gated, middle, normed_ffn, gate, up, hidden))
        partial = blocks(matmul(hidden, down_w).astype(BF16))
        if layer + 1 < layers:
            stream, normed = exchange("fwd", partial, middle, gains[layer + 1, 0])
        else:
            stream, down_in = exchange("turn", partial, middle, grad_stream)
    pieces = [None] * layers
    for layer in reversed(range(layers)):
        in_w, taps, out_w, both_w, down_w = weights[layer]
        width = down_w.shape[0]
        source, normed, joint, mixed, padded, gated, middle, normed_ffn, gate, up, hidden = saved[layer]
        down_in = flat(down_in)
        grad_hidden = outer_cols(down_in, down_w)
        sigmoid = jax.nn.sigmoid(gate)
        grad_gate_up = jnp.concatenate(
            [grad_hidden * up * sigmoid * (1.0 + gate * (1.0 - sigmoid)), grad_hidden * gate * sigmoid], axis=1
        ).astype(BF16)
        partial = blocks(outer_cols(grad_gate_up, both_w).astype(BF16))
        grad_middle, grad_gain_ffn, mix_in = exchange("bwd", partial, grad_stream, middle, gains[layer, 1])
        grad_down = lax.psum_scatter(inner_rows(hidden, down_in).astype(BF16), DP, scatter_dimension=0, tiled=True).astype(F32)
        grad_both = scatter_columns(inner_rows(normed_ffn, grad_gate_up).astype(BF16)).astype(F32)
        grad_gate = column_whole(grad_both[:, :, :width], 1)
        grad_up = column_whole(grad_both[:, :, width:], 1)
        mix_in = flat(mix_in)
        grad_gated = blocks(outer_cols(mix_in, out_w))
        grad_joint, grad_taps = conv_backward(grad_gated, joint, mixed, padded, taps, keep_one, keep_two)
        grad_joint = flat(grad_joint)
        partial = blocks(outer_cols(grad_joint, in_w).astype(BF16))
        if layer > 0:
            grad_stream, grad_gain_mix, down_in = exchange("bwd", partial, grad_middle, source, gains[layer, 0])
        else:
            grad_stream, grad_gain_mix = exchange("last", partial, grad_middle, source, gains[layer, 0])
        grad_out_w = lax.psum_scatter(inner_rows(gated, mix_in).astype(BF16), DP, scatter_dimension=0, tiled=True).astype(F32)
        grad_in_w = column_whole(scatter_columns(inner_rows(normed, grad_joint).astype(BF16)).astype(F32), 3)
        pieces[layer] = (grad_gain_mix, grad_in_w, grad_taps, grad_out_w, grad_gain_ffn, grad_gate, grad_up, grad_down)
    gain_grads = jnp.stack([jnp.concatenate([p[0], p[4]]) for p in pieces])
    gain_grads = lax.psum_scatter(gain_grads, OWNERS, scatter_dimension=2, tiled=True)
    tap_grads = lax.psum_scatter(jnp.stack([p[2] for p in pieces]), DP, scatter_dimension=2, tiled=True)
    return (
        stream[None],
        grad_stream[None],
        gain_grads[:, 0],
        jnp.stack([p[1] for p in pieces]),
        tap_grads.transpose(0, 2, 1),
        jnp.stack([p[3] for p in pieces]),
        gain_grads[:, 1],
        jnp.stack([p[5] for p in pieces]),
        jnp.stack([p[6] for p in pieces]),
        jnp.stack([p[7] for p in pieces]),
    )


def solution(mesh):
    dp, seq = mesh.shape["dp"], mesh.shape["seq"]
    side = dp // 2
    split = Mesh(mesh.devices.reshape(side // 2, 2, 2, seq // side // 2, 2, side), OWNERS)
    token = P(ROW_AXES, SEQ_AXES, None)
    vector = P(None, OWNERS)
    matrix = P(None, OWNERS, None)
    return jax.shard_map(
        local,
        mesh=split,
        in_specs=(token, P(ROW_AXES, None), vector, matrix, matrix, matrix, vector, matrix, matrix, matrix, token),
        out_specs=(token, token, vector, matrix, matrix, matrix, vector, matrix, matrix, matrix),
        check_vma=False,
    )
```

time: 2070 us -> 1440 us (0.70)
  waiting for transfers between devices: 1410 us -> 426 us
  Pallas kernels: 0 us -> 370 us
  matrix products: 134 us -> 92 us
  starting transfers between devices: 20.7 us -> 46.7 us
  other arithmetic: 61.9 us -> 39.9 us
    reduce_scatter x12 -> x4, waiting for transfers between devices: 568 us -> 156 us  [the longest x2 97.8 us: local(): lax.psum_scatter(inner_rows(hidden, down_in).astype(BF16), DP, scatter_di...]
    pallas_call x0 -> x9, Pallas kernels: none -> 370 us  [exchange(): pl.pallas_call(functools.partial(exchange_kernel, kind), out_shape=tuple(...]
    all_gather x8 -> x0, waiting for transfers between devices: 194 us -> none  [gather_tokens(): return lax.all_gather(array, TP, axis=0, tiled=True)]
    all_gather x4, waiting for transfers between devices: 173 us -> 0.06 us  [gather_columns(): whole = lax.all_gather(mine, DP, axis=0, tiled=False)]
    reduce_scatter x4, waiting for transfers between devices: 264 us -> 133 us  [scatter_columns(): mine = lax.psum_scatter(parts, DP, scatter_dimension=0, tiled=False)]
    all_gather x2, waiting for transfers between devices: 65.5 us -> 0.02 us  [local(): down_w = lax.all_gather(w_down[layer].astype(BF16), DP, axis=0, tiled=True)]
    ppermute x4 -> x8, waiting for transfers between devices: 33.4 us -> 1.06 us  [the longest x2 1.04 us: heads_after(): lax.ppermute(heads, 'x', [((i + 1) % x_size, i) for i in range(x_size)])]
    all_to_all x2 -> x1, blocking collectives: 44.8 us -> 14 us  [scatter_columns(): return lax.all_to_all(mine, TP, split_axis=0, concat_axis=0, tiled=True)]
  transfers between devices with their start and end apart: 38 -> 28, of which waited for: 32 -> 11; matrix products, arithmetic and copies ran while one was open for 13% -> 17% of each run, Pallas kernels for 0% -> 20%
where the time goes in v2:
time: 1440 us; the launch traced here: 1430 us
  waiting for transfers between devices  426 us (30%)
  Pallas kernels  370 us (26%)
  blocking collectives  253 us (18%)
  local copies, waits for them, and re-layouts  182 us (13%)
  matrix products  92 us (6%)
  starting transfers between devices  46.7 us (3%)
  other arithmetic  39.9 us (3%)
  between operations  16 us (1%)
    pallas_call x9, Pallas kernels, exchange(): pl.pallas_call(functools.partial(exchange_kernel, kind), out_shape=tuple(...  370 us
    reduce_scatter x4, waiting for transfers between devices, scatter_columns(): mine = lax.psum_scatter(parts, DP, scatter_dimension=0, tiled=False)  133 us
    unnamed x18, waiting for transfers between devices  125 us
    reduce_scatter x2, waiting for transfers between devices, local(): lax.psum_scatter(inner_rows(hidden, down_in).astype(BF16), DP, scatter_di...  97.8 us
    all_gather x1, blocking collectives, local(): lax.all_gather(small[:, :, :2], OWNERS, axis=1, tiled=True).astype(F32)  77.1 us
    all_gather x2, blocking collectives, local(): out_w = lax.all_gather(out_proj[layer].astype(BF16), DP, axis=0, tiled=True)  65.7 us
    all_to_all x3, blocking collectives, gather_columns(): mine = lax.all_to_all(shards, TP, split_axis=0, concat_axis=0, tiled=True)  60.2 us
    reduce_scatter x2, waiting for transfers between devices, local(): lax.psum_scatter(inner_rows(gated, mix_in).astype(BF16), DP, scatter_dime...  58.4 us
  transfers between devices with their start and end apart: 28, of which 11 were waited for; matrix products, arithmetic and copies ran while one was open for 17% of the time, Pallas kernels for 20%

profile of v2, /device:TPU:0, one launch (start us, length us, event | category | flops | bytes accessed | tf_op | source)
XLA Modules:
  0.0 1425.6 jit_solution(11038243125887605702)
XLA Ops:
  11.6 13.8 all_to_all.40
  38.3 7.4 all-to-all-done.2
  49.3 23.9 %all_to_all.41 = bf16[8,48,1152]{2,1,0:T(8,128)(2,1)} all-to-all(bf16[8,48,1152]{2,1,0:T(8,128)(2,1)S(1)} %pad_maximum_fusion.12), channel_id=1, replica_groups=mesh['yh'=1,'yl'=2,'core'=2,'zh'=2,'zl'=2,'x'=2] {'zl','yl','core'}, dimensions={0} | all-to-all | bytes 1769472 | tf_op jit(solution)/shard_map/all_to_all | solution.py:279
  79.8 22.4 %all_to_all.42 = bf16[8,48,1152]{2,1,0:T(8,128)(2,1)} all-to-all(bf16[8,48,1152]{2,1,0:T(8,128)(2,1)S(1)} %pad_maximum_fusion.13), channel_id=1, replica_groups=mesh['yh'=1,'yl'=2,'core'=2,'zh'=2,'zl'=2,'x'=2] {'zl','yl','core'}, dimensions={0} | all-to-all | bytes 1769472 | tf_op jit(solution)/shard_map/all_to_all | solution.py:279
  103.0 5.0 all-gather.8
  108.1 77.1 %all_gather.45 = bf16[2,1536,2]{2,0,1:T(2,128)(2,1)S(1)} all-gather(bf16[2,48,2]{2,0,1:T(2,128)(2,1)S(1)} %copy.245), channel_id=1, replica_groups=mesh['yh'=1,'yl'=2,'core'=2,'zh'=2,'zl'=2,'x'=2] {'yh','yl','core','zh',..., dimensions={1}, use_global_device_ids=true | all-gather | bytes 12672 | tf_op jit(solution)/shard_map/all_gather | solution.py:385
  185.8 38.7 %slice_reduce_fusion = (f32[1536]{0:T(1024)S(1)}, f32[1536]{0:T(1024)S(1)}, f32[1536]{0:T(1024)S(1)}, f32[1536]{0:T(1024)S(1)}) fusion(f32[2,2,1,1536]{1,0,3,2:T(2,128)S(1)} %convert_bitcast_fusion), kind=kLoop, calls=%fused_computation.79 | loop fusion | bytes 49152 | tf_op jit(solution)/shard_map/slice | solution.py:410
  224.7 31.0 %all_gather.48 = bf16[2,192,3]{2,0,1:T(2,128)(2,1)S(1)} all-gather(bf16[2,48,3]{2,0,1:T(2,128)(2,1)S(1)} %copy.249), channel_id=1, replica_groups=mesh['yh'=1,'yl'=2,'core'=2,'zh'=2,'zl'=2,'x'=2] {'yh','zh','x'}, dimensions={1}, use_global_device_ids=true | all-gather | bytes 2880 | tf_op jit(solution)/shard_map/all_gather | solution.py:387
  256.1 21.6 %exchange_first.1 = bf16[8,128,1536]{2,1,0:T(8,128)(2,1)S(1)} custom-call(f32[128,1536]{1,0:T(8,128)S(1)} %bitcast.272, f32[1,1536]{1,0:T(1,128)S(1)} %squeeze.16.refs_1_.refs_3_), custom_call_target="tpu_custom_call" | custom-call | flops 10000000 | bytes 150000000 | tf_op jit(solution)/shard_map/exchange_first/pallas_call | solution.py:213
  288.2 41.1 %all-gather.1 = bf16[1,192,1536]{2,1,0:T(8,128)(2,1)S(1)} all-gather(bf16[1,48,1536]{2,1,0:T(8,128)(2,1)S(1)} %get-tuple-element.95), channel_id=3, replica_groups=mesh['yh'=1,'yl'=2,'core'=2,'zh'=2,'zl'=2,'x'=2] {'yh','zh','x'}, dimensions={1}, use_global_device_ids=true | all-gather | bytes 737280 | tf_op jit(solution)/shard_map/all_gather | solution.py:391
  337.3 67.9 %exchange_fwd.3 = (f32[128,1536]{1,0:T(8,128)S(1)}, bf16[8,128,1536]{2,1,0:T(8,128)(2,1)S(1)}) custom-call(bf16[8,128,1536]{2,1,0:T(8,128)(2,1)S(1)} %bitcast.271, f32[128,1536]{1,0:T(8,128)S(1)} %bitcast.273, f32[1,1536]{1,0:T(1,128)S(1)} %squeeze.18.refs_2_.refs_3_), custom_call_target="tpu_custom_call" | custom-call | flops 10000000 | bytes 150000000 | tf_op jit(solution)/shard_map/exchange_fwd/pallas_call | solution.py:213
  409.8 4.2 fusion.68
  417.0 4.7 convolution_convert_fusion.6
  421.8 40.7 %exchange_fwd.4 = (f32[128,1536]{1,0:T(8,128)S(1)}, bf16[8,128,1536]{2,1,0:T(8,128)(2,1)S(1)}) custom-call(bf16[8,128,1536]{2,1,0:T(8,128)(2,1)S(1)} %bitcast.282, f32[128,1536]{1,0:T(8,128)S(1)} %get-tuple-element.30.refs_1_.refs_2_, f32[1,1536]{1,0:T(1,128)S(1)} %squeeze.19.refs_2_.refs_3_), custom_call_target="tpu_custom_call" | custom-call | flops 10000000 | bytes 150000000 | tf_op jit(solution)/shard_map/exchange_fwd/pallas_call | solution.py:213
  471.5 24.7 %all-gather.5 = bf16[1,192,1536]{2,1,0:T(8,128)(2,1)} all-gather(bf16[1,48,1536]{2,1,0:T(8,128)(2,1)S(1)} %get-tuple-element.96), channel_id=7, replica_groups=mesh['yh'=1,'yl'=2,'core'=2,'zh'=2,'zl'=2,'x'=2] {'yh','zh','x'}, dimensions={1}, use_global_device_ids=true | all-gather | bytes 737280 | tf_op jit(solution)/shard_map/all_gather | solution.py:391
  507.1 49.9 %exchange_fwd.5 = (f32[128,1536]{1,0:T(8,128)S(1)}, bf16[8,128,1536]{2,1,0:T(8,128)(2,1)S(1)}) custom-call(bf16[8,128,1536]{2,1,0:T(8,128)(2,1)S(1)} %bitcast.270, f32[128,1536]{1,0:T(8,128)S(1)} %get-tuple-element.32.refs_1_.refs_2_, f32[1,1536]{1,0:T(1,128)S(1)} %squeeze.21.refs_2_.refs_3_), custom_call_target="tpu_custom_call" | custom-call | flops 10000000 | bytes 150000000 | tf_op jit(solution)/shard_map/exchange_fwd/pallas_call | solution.py:213
  557.0 4.2 fusion.70
  565.4 4.6 convolution_convert_fusion.4
  570.1 41.5 %exchange_turn.1 = (f32[128,1536]{1,0:T(8,128)S(1)}, bf16[8,128,1536]{2,1,0:T(8,128)(2,1)S(1)}) custom-call(bf16[8,128,1536]{2,1,0:T(8,128)(2,1)S(1)} %bitcast.281, f32[128,1536]{1,0:T(8,128)S(1)} %get-tuple-element.34.refs_1_.refs_2_, f32[128,1536]{1,0:T(8,128)S(1)} %bitcast.275), custom_call_target="tpu_custom_call" | custom-call | flops 10000000 | bytes 150000000 | tf_op jit(solution)/shard_map/exchange_turn/pallas_call | solution.py:213
  615.1 4.6 convolution_convert_fusion.9
  619.7 40.9 %exchange_bwd.3 = (f32[128,1536]{1,0:T(8,128)S(1)}, f32[1,1536]{1,0:T(1,128)S(1)}, bf16[8,128,1536]{2,1,0:T(8,128)(2,1)S(1)}) custom-call(bf16[8,128,1536]{2,1,0:T(8,128)(2,1)S(1)} %bitcast.280, f32[128,1536]{1,0:T(8,128)S(1)} %bitcast.276, f32[128,1536]{1,0:T(8,128)S(1)} %get-tuple-element.34.refs_1_.refs_2_, f32[1,1536]{1,0:T(1,128)S(1)} %squeeze.21.refs_2_.refs_3_), custom_call_target="tpu_custom_call" | custom-call | flops 10000000 | bytes 150000000 | tf_op jit(solution)/shard_map/exchange_bwd/pallas_call | solution.py:213
  689.6 4.4 convolution_convert_fusion.3
  694.1 40.5 %exchange_bwd.4 = (f32[128,1536]{1,0:T(8,128)S(1)}, f32[1,1536]{1,0:T(1,128)S(1)}, bf16[8,128,1536]{2,1,0:T(8,128)(2,1)S(1)}) custom-call(bf16[8,128,1536]{2,1,0:T(8,128)(2,1)S(1)} %bitcast.277, f32[128,1536]{1,0:T(8,128)S(1)} %copy-done.11, f32[128,1536]{1,0:T(8,128)S(1)} %copy-done.3, f32[1,1536]{1,0:T(1,128)S(1)} %squeeze.19.refs_2_.refs_3_), custom_call_target="tpu_custom_call" | custom-call | flops 10000000 | bytes 150000000 | tf_op jit(solution)/shard_map/exchange_bwd/pallas_call | solution.py:213
  734.7 6.2 multiply_convert_fusion.1
  740.9 4.7 convolution_convert_fusion.8
  745.6 41.2 %exchange_bwd.5 = (f32[128,1536]{1,0:T(8,128)S(1)}, f32[1,1536]{1,0:T(1,128)S(1)}, bf16[8,128,1536]{2,1,0:T(8,128)(2,1)S(1)}) custom-call(bf16[8,128,1536]{2,1,0:T(8,128)(2,1)S(1)} %bitcast.279, f32[128,1536]{1,0:T(8,128)S(1)} %get-tuple-element.40.refs_1_, f32[128,1536]{1,0:T(8,128)S(1)} %get-tuple-element.30.refs_1_.refs_2_, ...), custom_call_target="tpu_custom_call" | custom-call | flops 10000000 | bytes 150000000 | tf_op jit(solution)/shard_map/exchange_bwd/pallas_call | solution.py:213
  797.1 23.9 %collective-permute-start.6 = (f32[2,4,2,192]{3,1,2,0:T(4,128)S(1)}, f32[2,4,2,192]{3,1,2,0:T(4,128)S(1)}, u32[]{:S(2)}, u32[]{:S(2)}) collective-permute-start(f32[2,4,2,192]{3,1,2,0:T(4,128)S(1)} %copy.279), channel_id=1, source_target_pairs={{1,0},{0,1},{3,2},{2,3},{5,4},{4,5},{7,6},{6,7},{9,8},{8,9},{11,10... | collective-permute-start | bytes 36872 | tf_op jit(solution)/shard_map/ppermute | solution.py:310
  827.0 4.2 bitcast_convert_fusion.1
  838.2 7.0 convolution_convert_fusion
  848.8 4.5 convolution_convert_fusion.2
  853.3 25.6 %exchange_last.1 = (f32[128,1536]{1,0:T(8,128)S(1)}, f32[1,1536]{1,0:T(1,128)S(1)}) custom-call(bf16[8,128,1536]{2,1,0:T(8,128)(2,1)S(1)} %bitcast.278, f32[128,1536]{1,0:T(8,128)S(1)} %get-tuple-element.42.refs_1_, f32[128,1536]{1,0:T(8,128)S(1)} %bitcast.274, f32[1,1536]{1,0:T(1,128)S(1)} %squeeze.16.refs_1_.refs_3_), custom_call_target="tpu_custom_call" | custom-call | flops 10000000 | bytes 150000000 | tf_op jit(solution)/shard_map/exchange_last/pallas_call | solution.py:213
  881.9 7.1 convolution_convert_fusion.1
  899.7 4.6 convolution_convert_fusion.10
  904.3 4.2 all-to-all-start.5
  908.6 5.1 convolution_convert_fusion.11
  917.0 14.0 all_to_all.43
  931.1 54.9 %reduce-scatter.25.cloned.1.call-done = bf16[1,384,1152]{2,1,0:T(8,128)(2,1)} async-done(((bf16[4,384,1152]{2,1,0:T(8,128)(2,1)}), bf16[1,384,1152]{2,1,0:T(8,128)(2,1)}) %reduce-scatter.25.cloned.1.call-update) | async-done | bytes 884752 | tf_op jit(solution)/shard_map/reduce_scatter | solution.py:292
  989.5 24.3 %reduce-scatter.33.cloned.1.call-done = f32[48,6]{1,0:T(8,128)} async-done(((f32[192,6]{1,0:T(8,128)}), f32[48,6]{1,0:T(8,128)}) %reduce-scatter.33.cloned.1.call-update) | async-done | bytes 1168
  1015.3 99.6 %reduce-scatter.31.cloned.1.call-done = f32[48,4]{1,0:T(8,128)} async-done(((f32[1536,4]{1,0:T(8,128)}), f32[48,4]{1,0:T(8,128)}) %reduce-scatter.31.cloned.1.call-update) | async-done | bytes 784
  1115.8 77.9 %reduce-scatter.23.cloned.1.call-done = bf16[1,384,1152]{2,1,0:T(8,128)(2,1)} async-done(((bf16[4,384,1152]{2,1,0:T(8,128)(2,1)}), bf16[1,384,1152]{2,1,0:T(8,128)(2,1)}) %reduce-scatter.23.cloned.1.call-update) | async-done | bytes 884752 | tf_op jit(solution)/shard_map/reduce_scatter | solution.py:292
  1199.1 27.1 %reduce-scatter.21.cloned.1.call-done = bf16[48,1536]{1,0:T(8,128)(2,1)} async-done(((bf16[192,1536]{1,0:T(8,128)(2,1)}), bf16[48,1536]{1,0:T(8,128)(2,1)}) %reduce-scatter.21.cloned.1.call-update) | async-done | bytes 147472 | tf_op jit(solution)/shard_map/reduce_scatter | solution.py:447
  1226.2 31.3 %reduce-scatter.19.cloned.1.call-done = bf16[48,1536]{1,0:T(8,128)(2,1)} async-done(((bf16[192,1536]{1,0:T(8,128)(2,1)}), bf16[48,1536]{1,0:T(8,128)(2,1)}) %reduce-scatter.19.cloned.1.call-update) | async-done | bytes 147472 | tf_op jit(solution)/shard_map/reduce_scatter | solution.py:447
  1259.3 48.0 %reduce-scatter.29.cloned.1.call-done = bf16[144,1536]{1,0:T(8,128)(2,1)} async-done(((bf16[576,1536]{1,0:T(8,128)(2,1)}), bf16[144,1536]{1,0:T(8,128)(2,1)}) %reduce-scatter.29.cloned.1.call-update) | async-done | bytes 442384 | tf_op jit(solution)/shard_map/reduce_scatter | solution.py:434
  1307.3 49.9 %reduce-scatter.27.cloned.1.call-done = bf16[144,1536]{1,0:T(8,128)(2,1)} async-done(((bf16[576,1536]{1,0:T(8,128)(2,1)}), bf16[144,1536]{1,0:T(8,128)(2,1)}) %reduce-scatter.27.cloned.1.call-update) | async-done | bytes 442384 | tf_op jit(solution)/shard_map/reduce_scatter | solution.py:434
  1362.4 5.1 stack_reshape.21
  1370.3 4.5 stack_reshape.20
  1383.5 4.4 stack_reshape.25
  1393.6 4.4 stack_reshape.23
  (390 shorter events, 211.0 us)
Async XLA Ops:
  7.2 272.3 %all-gather.16.cloned.1.call-start = ((), (), s32[]{:S(2)}) async-start(), calls=%async_computation.26 | async-start | bytes 2457600 | tf_op jit(solution)/shard_map/all_gather | solution.py:280
  29.0 16.7 %all-to-all-start.2 = ((bf16[8,48,576]{2,1,0:T(8,128)(2,1)}), bf16[8,48,576]{2,1,0:T(8,128)(2,1)S(1)}, u32[]{:S(2)}, u32[]{:S(2)}) async-start(bf16[8,48,576]{2,1,0:T(8,128)(2,1)} %reshape.409), calls=%async_computation.2 | async-start | bytes 983040 | tf_op jit(solution)/shard_map/all_to_all | solution.py:279
  32.5 296.9 %all-gather.22.cloned.1.call-start = ((), (), s32[]{:S(2)}) async-start(), calls=%async_computation.29 | async-start | bytes 2457600 | tf_op jit(solution)/shard_map/all_gather | solution.py:280
  46.5 360.3 %all-gather.18.cloned.1.call-start = ((), (), s32[]{:S(2)}) async-start(), calls=%async_computation.27 | async-start | bytes 4423680 | tf_op jit(solution)/shard_map/all_gather | solution.py:280
  49.3 24.0 %copy-start.62 = (f32[2,144,1536]{2,1,0:T(8,128)S(1)}, f32[2,144,1536]{2,1,0:T(8,128)}, u32[]{:S(2)}) copy-start(f32[2,144,1536]{2,1,0:T(8,128)} %param.20) | copy-start | bytes 5308420
  73.3 343.7 %all-gather.20.cloned.1.call-start = ((), (), s32[]{:S(2)}) async-start(), calls=%async_computation.28 | async-start | bytes 2211840 | tf_op jit(solution)/shard_map/all_gather | solution.py:396
  74.4 421.7 %all-gather.24.cloned.1.call-start = ((), (), s32[]{:S(2)}) async-start(), calls=%async_computation.30 | async-start | bytes 4423680 | tf_op jit(solution)/shard_map/all_gather | solution.py:280
  79.5 23.4 %copy-start.77 = (s32[1,4]{1,0:T(1,128)S(1)}, s32[1,4]{1,0:T(1,128)}, u32[]{:S(2)}) copy-start(s32[1,4]{1,0:T(1,128)} %param.12) | copy-start | bytes 52
  79.5 28.5 %copy-start.75 = (f32[2,48]{1,0:T(2,128)S(1)}, f32[2,48]{1,0:T(2,128)}, u32[]{:S(2)}) copy-start(f32[2,48]{1,0:T(2,128)} %param.17) | copy-start | bytes 1156
  79.5 28.5 %copy-start.76 = (f32[2,48]{1,0:T(2,128)S(1)}, f32[2,48]{1,0:T(2,128)}, u32[]{:S(2)}) copy-start(f32[2,48]{1,0:T(2,128)} %param.13) | copy-start | bytes 1156
  102.2 463.2 %all-gather.26.cloned.1.call-start = ((), (), s32[]{:S(2)}) async-start(), calls=%async_computation.31 | async-start | bytes 2211840 | tf_op jit(solution)/shard_map/all_gather | solution.py:396
  102.8 801.5 %reduce-scatter.17.cloned.1.call-start = ((), (), s32[]{:S(2)}) async-start(), calls=%async_computation.19 | async-start | bytes 2457600 | tf_op jit(solution)/shard_map/reduce_scatter | solution.py:292
  185.2 39.3 %copy-start.74 = (f32[2,48,3]{1,0,2:T(2,128)S(1)}, f32[2,48,3]{1,0,2:T(2,128)}, u32[]{:S(2)}) copy-start(f32[2,48,3]{1,0,2:T(2,128)} %param.15) | copy-start | bytes 3460
  185.8 70.1 %copy-start.71 = (f32[2,48,1536]{2,1,0:T(8,128)S(1)}, f32[2,48,1536]{2,1,0:T(8,128)}, u32[]{:S(2)}) copy-start(f32[2,48,1536]{2,1,0:T(8,128)} %param.16) | copy-start | bytes 1769476
  185.8 70.2 %copy-start = (f32[1,128,1536]{2,1,0:T(8,128)S(1)}, f32[1,128,1536]{2,1,0:T(8,128)}, u32[]{:S(2)}) copy-start(f32[1,128,1536]{2,1,0:T(8,128)} %param.11) | copy-start | bytes 2359300
  284.1 49.1 %copy-start.24 = (f32[8,128,192]{1,2,0:T(8,128)}, f32[8,128,192]{1,2,0:T(8,128)S(1)}, u32[]{:S(2)}) copy-start(f32[8,128,192]{1,2,0:T(8,128)S(1)} %slice_multiply_fusion.2) | copy-start | bytes 2359300
  286.1 46.8 %collective-permute-start.1 = (f32[2,4,2,192]{3,1,2,0:T(4,128)S(1)}, f32[2,4,2,192]{3,1,2,0:T(4,128)S(1)}, u32[]{:S(2)}, u32[]{:S(2)}) collective-permute-start(f32[2,4,2,192]{3,1,2,0:T(4,128)S(1)} %copy.251), channel_id=1, source_target_pairs={{0,1},{1,0},{2,3},{3,2},{4,5},{5,4},{6,7},{7,6},{8,9},{9,8},{10,11... | collective-permute-start | bytes 36872 | tf_op jit(solution)/shard_map/ppermute | solution.py:300
  287.6 45.1 %collective-permute-start = (f32[4,2,192]{1,2,0:T(8,128)}, f32[4,2,192]{1,2,0:T(8,128)S(1)}, u32[]{:S(2)}, u32[]{:S(2)}) collective-permute-start(f32[4,2,192]{1,2,0:T(8,128)} %slice.242), channel_id=1, source_target_pairs={{1,4},{3,6},{9,12},{11,14},{17,20},{19,22},{25,28},{27,30}} | collective-permute-start | bytes 18440 | tf_op jit(solution)/shard_map/ppermute | solution.py:302
  329.3 6.9 copy-start.54
  421.8 40.7 %copy-start.59 = (bf16[1,2,2,2,2,2,48,576]{7,6,5,4,3,2,1,0:T(8,128)(2,1)S(1)}, bf16[1,2,2,2,2,2,48,576]{7,6,5,4,3,2,1,0:T(8,128)(2,1)}, u32[]{:S(2)}) copy-start(bf16[1,2,2,2,2,2,48,576]{7,6,5,4,3,2,1,0:T(8,128)(2,1)} %copy.259) | copy-start | bytes 5308420
  462.5 44.5 %copy-start.2 = (f32[128,1536]{1,0:T(8,128)}, f32[128,1536]{1,0:T(8,128)S(1)}, u32[]{:S(2)}) copy-start(f32[128,1536]{1,0:T(8,128)S(1)} %get-tuple-element.32.refs_1_.refs_2_) | copy-start | bytes 2359300
  464.7 38.0 %copy-start.26 = (f32[8,128,192]{1,2,0:T(8,128)}, f32[8,128,192]{1,2,0:T(8,128)S(1)}, u32[]{:S(2)}) copy-start(f32[8,128,192]{1,2,0:T(8,128)S(1)} %slice_multiply_fusion) | copy-start | bytes 2359300
  468.5 32.9 %collective-permute-start.3 = (f32[2,4,2,192]{3,1,2,0:T(4,128)S(1)}, f32[2,4,2,192]{3,1,2,0:T(4,128)S(1)}, u32[]{:S(2)}, u32[]{:S(2)}) collective-permute-start(f32[2,4,2,192]{3,1,2,0:T(4,128)S(1)} %copy.262), channel_id=1, source_target_pairs={{0,1},{1,0},{2,3},{3,2},{4,5},{5,4},{6,7},{7,6},{8,9},{9,8},{10,11... | collective-permute-start | bytes 36872 | tf_op jit(solution)/shard_map/ppermute | solution.py:300
  470.0 30.2 %collective-permute-start.2 = (f32[4,2,192]{1,2,0:T(8,128)}, f32[4,2,192]{1,2,0:T(8,128)}, u32[]{:S(2)}, u32[]{:S(2)}) collective-permute-start(f32[4,2,192]{1,2,0:T(8,128)} %slice.260), channel_id=1, source_target_pairs={{1,4},{3,6},{9,12},{11,14},{17,20},{19,22},{25,28},{27,30}} | collective-permute-start | bytes 18440 | tf_op jit(solution)/shard_map/ppermute | solution.py:302
  507.0 49.9 %copy-start.50 = (bf16[1,2,2,2,2,2,48,1152]{7,6,5,4,3,2,1,0:T(8,128)(2,1)S(1)}, bf16[1,2,2,2,2,2,48,1152]{7,6,5,4,3,2,1,0:T(8,128)(2,1)}, u32[]{:S(2)}) copy-start(bf16[1,2,2,2,2,2,48,1152]{7,6,5,4,3,2,1,0:T(8,128)(2,1)} %copy.268) | copy-start | bytes 10616836
  565.4 46.2 %copy-start.79 = (bf16[1,576,1536]{2,1,0:T(8,128)(2,1)S(1)}, bf16[1,576,1536]{2,1,0:T(8,128)(2,1)}, u32[]{:S(2)}) copy-start(bf16[1,576,1536]{2,1,0:T(8,128)(2,1)} %all-gather.26.cloned.1.call-done) | copy-start | bytes 5308420
  570.1 41.6 %copy-start.41 = (f32[1024,1152]{1,0:T(8,128)S(1)}, f32[1024,1152]{1,0:T(8,128)}, u32[]{:S(2)}) copy-start(f32[1024,1152]{1,0:T(8,128)} %copy-done.40) | copy-start | bytes 14155780
  619.7 41.0 %copy-start.57 = (bf16[1,192,1536]{2,1,0:T(8,128)(2,1)S(1)}, bf16[1,192,1536]{2,1,0:T(8,128)(2,1)}, u32[]{:S(2)}) copy-start(bf16[1,192,1536]{2,1,0:T(8,128)(2,1)} %all-gather.5) | copy-start | bytes 1769476
  669.1 3.8 collective-permute-start.4
  669.2 2.5 collective-permute-start.5
  689.5 224.2 %reduce-scatter.15.cloned.1.call-start = ((), (), s32[]{:S(2)}) async-start(), calls=%async_computation.18 | async-start | bytes 2457600 | tf_op jit(solution)/shard_map/reduce_scatter | solution.py:292
  694.1 40.6 %copy-start.78 = (bf16[1,576,1536]{2,1,0:T(8,128)(2,1)S(1)}, bf16[1,576,1536]{2,1,0:T(8,128)(2,1)}, u32[]{:S(2)}) copy-start(bf16[1,576,1536]{2,1,0:T(8,128)(2,1)} %all-gather.20.cloned.1.call-done) | copy-start | bytes 5308420
  745.6 41.3 %copy-start.55 = (bf16[1,192,1536]{2,1,0:T(8,128)(2,1)S(1)}, bf16[1,192,1536]{2,1,0:T(8,128)(2,1)}, u32[]{:S(2)}) copy-start(bf16[1,192,1536]{2,1,0:T(8,128)(2,1)} %copy-done.54) | copy-start | bytes 1769476
  796.7 26.5 %copy-start.36 = (f32[8,128,192]{1,2,0:T(8,128)S(1)}, f32[8,128,192]{1,2,0:T(8,128)}, u32[]{:S(2)}) copy-start(f32[8,128,192]{1,2,0:T(8,128)} %copy-done.35) | copy-start | bytes 2359300
  797.1 25.8 %collective-permute-start.6 = (f32[2,4,2,192]{3,1,2,0:T(4,128)S(1)}, f32[2,4,2,192]{3,1,2,0:T(4,128)S(1)}, u32[]{:S(2)}, u32[]{:S(2)}) collective-permute-start(f32[2,4,2,192]{3,1,2,0:T(4,128)S(1)} %copy.279), channel_id=1, source_target_pairs={{1,0},{0,1},{3,2},{2,3},{5,4},{4,5},{7,6},{6,7},{9,8},{8,9},{11,10... | collective-permute-start | bytes 36872 | tf_op jit(solution)/shard_map/ppermute | solution.py:310
  822.0 0.7 collective-permute-start.7
  838.1 147.8 %reduce-scatter.25.cloned.1.call-start = ((), (), s32[]{:S(2)}) async-start(), calls=%async_computation.23 | async-start | bytes 4423680 | tf_op jit(solution)/shard_map/reduce_scatter | solution.py:292
  847.3 166.4 %reduce-scatter.33.cloned.1.call-start = ((), (), s32[]{:S(2)}) async-start(), calls=%async_computation.33 | async-start | bytes 122880
  848.6 266.3 %reduce-scatter.31.cloned.1.call-start = ((), (), s32[]{:S(2)}) async-start(), calls=%async_computation.32 | async-start | bytes 811008
  881.6 312.0 %reduce-scatter.23.cloned.1.call-start = ((), (), s32[]{:S(2)}) async-start(), calls=%async_computation.22 | async-start | bytes 4423680 | tf_op jit(solution)/shard_map/reduce_scatter | solution.py:292
  891.2 335.0 %reduce-scatter.21.cloned.1.call-start = ((), (), s32[]{:S(2)}) async-start(), calls=%async_computation.21 | async-start | bytes 737280 | tf_op jit(solution)/shard_map/reduce_scatter | solution.py:447
  896.0 361.5 %reduce-scatter.19.cloned.1.call-start = ((), (), s32[]{:S(2)}) async-start(), calls=%async_computation.20 | async-start | bytes 737280 | tf_op jit(solution)/shard_map/reduce_scatter | solution.py:447
  899.7 407.6 %reduce-scatter.29.cloned.1.call-start = ((), (), s32[]{:S(2)}) async-start(), calls=%async_computation.25 | async-start | bytes 2211840 | tf_op jit(solution)/shard_map/reduce_scatter | solution.py:434
  904.3 12.7 all-to-all-start.5
  908.5 448.6 %reduce-scatter.27.cloned.1.call-start = ((), (), s32[]{:S(2)}) async-start(), calls=%async_computation.24 | async-start | bytes 2211840 | tf_op jit(solution)/shard_map/reduce_scatter | solution.py:434
  985.9 207.7 %all-to-all-start.7 = ((bf16[8,48,1152]{2,1,0:T(8,128)(2,1)}), bf16[8,48,1152]{2,1,0:T(8,128)(2,1)S(1)}, u32[]{:S(2)}, u32[]{:S(2)}) async-start(bf16[8,48,1152]{2,1,0:T(8,128)(2,1)} %bitcast.337), calls=%async_computation.13 | async-start | bytes 1769472 | tf_op jit(solution)/shard_map/all_to_all | solution.py:294
  1193.6 204.4 %all-to-all-start.6 = ((bf16[8,48,1152]{2,1,0:T(8,128)(2,1)}), bf16[8,48,1152]{2,1,0:T(8,128)(2,1)S(1)}, u32[]{:S(2)}, u32[]{:S(2)}) async-start(bf16[8,48,1152]{2,1,0:T(8,128)(2,1)} %bitcast.338), calls=%async_computation.11 | async-start | bytes 1769472 | tf_op jit(solution)/shard_map/all_to_all | solution.py:294
  1360.6 7.0 copy-start.61
  (64 other events, 197.8 us)
Sparse Core Ops, SparseCore 0:
  25.6 50.9 all-gather.15
  79.0 52.0 all-gather.21
  132.9 78.1 all-gather.17
  213.4 48.0 all-gather.19
  263.3 81.5 all-gather.23
  347.1 59.6 all-gather.25
  689.6 68.2 reduce-scatter.16
  838.3 69.1 reduce-scatter.14
  910.5 75.3 reduce-scatter.24
  989.1 24.6 reduce-scatter.32
  1020.3 94.6 reduce-scatter.30
  1118.2 75.4 reduce-scatter.22
  1197.3 28.8 reduce-scatter.20
  1229.5 27.9 reduce-scatter.18
  1261.2 46.0 reduce-scatter.28
  1311.0 46.0 reduce-scatter.26

commit v3 on v2

v3 whole, which is shorter than its diff:
```python
import functools
import itertools

import jax
import jax.numpy as jnp
from jax import lax
from jax.experimental import pallas as pl
from jax.experimental.pallas import tpu as pltpu
from jax.sharding import Mesh, PartitionSpec as P

EPSILON = 1e-05
TP = ("zl", "yl", "core")
DP = ("yh", "zh", "x")
ROW_AXES = ("yh", "yl", "core")
SEQ_AXES = ("zh", "zl", "x")
OWNERS = ROW_AXES + SEQ_AXES
BF16 = jnp.bfloat16
F32 = jnp.float32
MESH = pl.DeviceIdType.MESH
HALVES = 2
IN_NAMES = {
    "first": ("stream", "gain"),
    "fwd": ("partial", "stream", "gain"),
    "turn": ("partial", "stream", "grad"),
    "bwd": ("partial", "grad", "stream", "gain"),
    "last": ("partial", "grad", "stream", "gain"),
}
OUT_NAMES = {
    "first": ("whole",),
    "fwd": ("stream_next", "whole"),
    "turn": ("stream_next", "whole"),
    "bwd": ("grad_next", "gain_grad", "whole"),
    "last": ("grad_next", "gain_grad"),
}
COLLECTIVE_ID = {
    "first": 0, "fwd_ffn": 1, "fwd_conv": 2, "turn": 3, "bwd_ffn": 4, "bwd_conv": 5, "last": 6, "prepare": 7, "collect": 8,
}
FLIPS = ((1, 1, 1), (1, 1, 0), (1, 0, 1), (1, 0, 0), (0, 1, 1), (0, 1, 0), (0, 0, 1))
OTHERS = tuple(itertools.product((0, 1), repeat=5))[1:]
OTHER_AXES = ("yl", "core", "zh", "zl", "x")
SEMAPHORES = 64
LANES = 128


def rms_scale(values):
    return lax.rsqrt(jnp.mean(values * values, axis=-1, keepdims=True) + EPSILON)


class Place:
    def __init__(self, send, recv, local):
        self.zl, self.yl, self.core = (lax.axis_index(axis) for axis in TP)
        self.zh, self.x = lax.axis_index("zh"), lax.axis_index("x")
        self.send, self.recv, self.local = send, recv, local
        self.remote_count = self.local_count = 0
        self.sent = []

    def rank(self, flip_z, flip_y, flip_core):
        return self.flipped("zl", flip_z) * 4 + self.flipped("yl", flip_y) * 2 + self.flipped("core", flip_core)

    def flipped(self, axis, flip):
        return 1 - getattr(self, axis) if flip else getattr(self, axis)

    def member(self, flips):
        return {axis: 1 - getattr(self, axis) for axis, flip in zip(TP, flips) if flip}

    def beside(self, axis):
        return {axis: 1 - getattr(self, axis)}

    def owner(self, flips=(0,) * 5):
        index = 0
        for axis, flip in zip(OTHER_AXES, flips):
            index = index * 2 + self.flipped(axis, flip)
        return index

    def push(self, src, dst, device):
        index = self.remote_count
        self.remote_count += 1
        copy = pltpu.make_async_remote_copy(
            src_ref=src, dst_ref=dst, send_sem=self.send.at[index], recv_sem=self.recv.at[index],
            device_id=device, device_id_type=MESH,
        )
        self.sent.append(copy)
        return copy

    def copy(self, src, dst):
        index = self.local_count
        self.local_count += 1
        return pltpu.make_async_copy(src, dst, self.local.at[index])


def pieces_of(groups, width, group, low, high):
    main = width // LANES * LANES
    rest = width - main
    ranges = []
    if low < main:
        ranges.append((group * main + low, group * main + min(high, main)))
    if high > main:
        start = groups * main + group * rest - main
        ranges.append((start + max(low, main), start + high))
    return ranges


def shards_from(weights, out):
    width = weights[0].shape[1] // 8
    block = width // 4
    main = width // LANES * LANES
    rest = width - main
    for group, weight in enumerate(weights):
        for member in range(8):
            zl, others = member // 4, member % 4
            starts = [((others * 2 + zh) * 4 + zl * 2 + x) * block for zh in range(2) for x in range(2)]
            values = jnp.concatenate([weight[:, start : start + block] for start in starts], axis=1).astype(BF16)
            out[member, :, group * main : (group + 1) * main] = values[:, :main]
            if rest:
                low = len(weights) * main + group * rest
                out[member, :, low : low + rest] = values[:, main:]


def shards_to(shards, outs):
    groups, width = len(outs), shards.shape[2] // len(outs)
    block = width // 4
    for group, out in enumerate(outs):
        for others in range(4):
            for zh in range(2):
                values = []
                for zl in range(2):
                    for x in range(2):
                        low = (zh * 2 + x) * block
                        for start, end in pieces_of(groups, width, group, low, low + block):
                            values.append(shards[zl * 4 + others, :, start:end].astype(F32))
                start = (others * 2 + zh) * 4 * block
                out[:, start : start + 4 * block] = jnp.concatenate(values, axis=1)


def prepare_kernel(layers, small, in_proj, gate, up, out_proj, down, *refs):
    refs = list(refs)
    spread, *refs = refs
    outs, (send, recv, local) = refs[:-3], refs[-3:]
    place = Place(send, recv, local)
    barrier = pltpu.get_barrier_semaphore()
    for flips in OTHERS:
        device = {axis: place.flipped(axis, 1) for axis, flip in zip(OTHER_AXES, flips) if flip}
        pl.semaphore_signal(barrier, inc=1, device_id=device, device_id_type=MESH)
    pl.semaphore_wait(barrier, len(OTHERS))
    kept = place.copy(small, spread.at[place.owner()])
    kept.start()
    copies = []
    for flips in OTHERS:
        device = {axis: place.flipped(axis, 1) for axis, flip in zip(OTHER_AXES, flips) if flip}
        copies.append(place.push(small, spread.at[place.owner()], device))
        copies[-1].start()
    width = in_proj.shape[2] // 3
    for layer in range(layers):
        in_out, both_out, out_out, down_out = outs[4 * layer : 4 * layer + 4]
        shards_from([in_proj.at[layer, :, i * width : (i + 1) * width] for i in range(3)], in_out)
        shards_from([gate.at[layer], up.at[layer]], both_out)
        out_out[...] = out_proj[layer].astype(BF16)
        down_out[...] = down[layer].astype(BF16)
    kept.wait()
    for copy in copies:
        copy.wait()


def prepare(small, in_proj, gate, up, out_proj, down):
    layers, rows, columns = in_proj.shape
    width = gate.shape[2]
    shapes = []
    for _ in range(layers):
        shapes += [
            (8, rows, columns // 8), (8, rows, width // 4), out_proj.shape[1:], down.shape[1:],
        ]
    inside = pl.BlockSpec(memory_space=pltpu.VMEM)
    return pl.pallas_call(
        functools.partial(prepare_kernel, layers),
        out_shape=[jax.ShapeDtypeStruct((32,) + small.shape, F32)]
        + [jax.ShapeDtypeStruct(shape, BF16) for shape in shapes],
        in_specs=[inside] * 6,
        out_specs=[inside] * (1 + len(shapes)),
        scratch_shapes=[pltpu.SemaphoreType.DMA((SEMAPHORES,))] * 3,
        compiler_params=pltpu.CompilerParams(
            collective_id=COLLECTIVE_ID["prepare"], has_side_effects=True, vmem_limit_bytes=48 << 20
        ),
        name="prepare",
    )(small, in_proj, gate, up, out_proj, down)


def collect_kernel(slabs, out, landed, send, recv, local):
    place = Place(send, recv, local)
    barrier = pltpu.get_barrier_semaphore()
    for flips in OTHERS:
        device = {axis: place.flipped(axis, 1) for axis, flip in zip(OTHER_AXES, flips) if flip}
        pl.semaphore_signal(barrier, inc=1, device_id=device, device_id_type=MESH)
    pl.semaphore_wait(barrier, len(OTHERS))
    copies = []
    for i, flips in enumerate(OTHERS):
        device = {axis: place.flipped(axis, 1) for axis, flip in zip(OTHER_AXES, flips) if flip}
        copies.append(place.push(slabs.at[place.owner(flips)], landed.at[i], device))
        copies[-1].start()
    for copy in copies:
        copy.wait()
    out[...] = slabs[place.owner()] + jnp.sum(landed[...], axis=0)


def collect(slabs):
    inside = pl.BlockSpec(memory_space=pltpu.VMEM)
    return pl.pallas_call(
        collect_kernel,
        out_shape=jax.ShapeDtypeStruct(slabs.shape[1:], F32),
        in_specs=[inside],
        out_specs=inside,
        scratch_shapes=[pltpu.VMEM((len(OTHERS),) + slabs.shape[1:], F32)] + [pltpu.SemaphoreType.DMA((SEMAPHORES,))] * 3,
        compiler_params=pltpu.CompilerParams(collective_id=COLLECTIVE_ID["collect"], has_side_effects=True),
        name="collect",
    )(slabs)


class Gather:
    def __init__(self, place, mine, whole):
        self.columns = len(whole.shape) == 6
        self.chunks = whole.shape[0] if self.columns else 1
        self.mine, self.whole, self.place = mine, whole, place
        own, other = place.zh, 1 - place.zh
        self.along_z = [place.push(self.of_mine(c), self.at(c, own), place.beside("zh")) for c in range(self.chunks)]
        self.along_x = [place.push(self.of_mine(c), self.at(c, own), place.beside("x")) for c in range(self.chunks)]
        self.onward = [place.push(self.at(c, other), self.at(c, other), place.beside("x")) for c in range(self.chunks)]
        self.kept = [place.copy(self.of_mine(c), self.at(c, own)) for c in range(self.chunks)]

    def of_mine(self, c):
        return self.mine.at[c] if self.columns else self.mine

    def at(self, c, zh):
        return self.whole.at[c, zh, :, self.place.x] if self.columns else self.whole.at[zh, self.place.x]

    def start(self):
        for copies in (self.along_z, self.along_x, self.kept):
            for copy in copies:
                copy.start()

    def steps(self):
        def step(c):
            self.along_z[c].wait_recv()
            self.onward[c].start()
        return [functools.partial(step, c) for c in range(self.chunks)]

    def finish(self):
        for c in range(self.chunks):
            self.along_x[c].wait_recv()
            self.onward[c].wait_recv()
            self.kept[c].wait()


class Reduce:
    def __init__(self, place, total, outs, scratch):
        self.columns = len(total.shape) == 6
        self.place, self.total, self.outs = place, total, outs
        self.own, self.xin, self.zout, self.zin = scratch[:4]
        self.final, self.landed = scratch[4:] if self.columns else (None, None)
        self.chunks = 4 if self.columns else 1
        x, beside = place.x, place.beside
        pick = self.pick
        self.along_x = [place.push(pick(j, 1 - x), self.xin.at[j], beside("x")) for j in range(self.chunks)]
        self.kept = [place.copy(pick(j, x), self.own.at[j]) for j in range(self.chunks)]
        self.along_z = [place.push(self.zout.at[j], self.zin.at[j], beside("zh")) for j in range(self.chunks)]
        if self.columns:
            mine = place.rank(0, 0, 0)
            self.back = [
                [
                    place.push(self.final.at[j, fz], self.landed.at[mine], place.member((fz,) + self.flips(j)))
                    if (fz,) + self.flips(j) != (0, 0, 0)
                    else place.copy(self.final.at[j, fz], self.landed.at[mine])
                    for fz in (1, 0)
                ]
                for j in range(4)
            ]

    def flips(self, j):
        return ((1, 1), (1, 0), (0, 1), (0, 0))[j]

    def pick(self, j, x):
        if not self.columns:
            return self.total.at[:, x]
        flip_y, flip_core = self.flips(j)
        return self.total.at[self.place.flipped("yl", flip_y) * 2 + self.place.flipped("core", flip_core), :, :, x]

    def start(self):
        for j in range(self.chunks):
            self.along_x[j].start()
            self.kept[j].start()

    def steps(self):
        def first(j):
            self.kept[j].wait()
            self.along_x[j].wait_recv()
            there = 1 - self.place.zh
            self.zout[j] = (self.own[j, there].astype(F32) + self.xin[j, there].astype(F32)).astype(BF16)
            self.along_z[j].start()

        def second(j):
            self.along_z[j].wait_recv()
            here = self.place.zh
            total = self.own[j, here].astype(F32) + self.xin[j, here].astype(F32) + self.zin[j].astype(F32)
            if not self.columns:
                self.outs[0][...] = total
                return
            zl = self.place.zl
            for i, fz in enumerate((1, 0)):
                row = 1 - zl if fz else zl
                self.final[j, fz] = (
                    self.own[j, here, row].astype(F32) + self.xin[j, here, row].astype(F32) + self.zin[j, row].astype(F32)
                ).astype(BF16)
                self.back[j][i].start()

        steps = [functools.partial(first, 0)]
        for j in range(1, self.chunks):
            steps += [functools.partial(first, j), functools.partial(second, j - 1)]
        return steps + [functools.partial(second, self.chunks - 1)]

    def finish(self):
        if self.columns:
            for copies in self.back:
                for copy in copies:
                    if copy is self.back[3][1]:
                        copy.wait()
                    else:
                        copy.wait_recv()
            shards_to(self.landed, self.outs)


def exchange_kernel(kind, plan, *refs):
    reduces, gathers = kind != "first", kind != "last"
    refs = list(refs)

    def take(count):
        taken = refs[:count]
        del refs[:count]
        return taken

    ref = dict(zip(IN_NAMES[kind], take(len(IN_NAMES[kind]))))
    shard_refs, mine_refs, total_refs = (take(plan[name]) for name in ("shards", "mine", "totals"))
    ref.update(zip(OUT_NAMES[kind], take(len(OUT_NAMES[kind]))))
    shard_outs, whole_outs = (take(plan[name]) for name in ("shards", "wholes"))
    total_outs = [take(count) for count in plan["groups"]]
    near, sib, yin, yout, zin, zout, mine, send, recv, local = take(10)
    place = Place(send, recv, local)
    tokens = mine.shape[0]
    half = tokens // HALVES
    to_sibling, to_y, to_z = (place.beside(axis) for axis in ("core", "yl", "zl"))
    rank, push = place.rank, place.push

    def part(h):
        return pl.ds(h * half, half)

    chips = ((1, 1), (0, 1), (1, 0), (0, 0))
    if reduces:
        near_copies = [place.copy(ref["partial"].at[rank(*chip, 0)], near.at[i]) for i, chip in enumerate(chips)]
        for copy in near_copies:
            copy.start()
    if kind == "first":
        stream = ref["stream"][...]
        mine[...] = (stream * rms_scale(stream) * ref["gain"][...]).astype(BF16)
    if kind == "turn":
        mine[...] = ref["grad"][...].astype(BF16)

    partners = [place.member(flips) for flips in FLIPS] if shard_refs or total_refs else [to_sibling, to_y, to_z]
    if whole_outs or total_refs:
        partners += [place.beside("zh"), place.beside("x")]
    barrier = pltpu.get_barrier_semaphore()
    for partner in partners:
        pl.semaphore_signal(barrier, inc=1, device_id=partner, device_id_type=MESH)
    pl.semaphore_wait(barrier, len(partners))

    scattered = []
    for shards, out in zip(shard_refs, shard_outs):
        here = out.at[place.yl * 2 + place.core, place.zl]
        scattered.append(
            [push(shards.at[rank(*flips)], here, place.member(flips)) for flips in FLIPS]
            + [place.copy(shards.at[rank(0, 0, 0)], here)]
        )
    gather_list = [Gather(place, own, whole) for own, whole in zip(shard_outs[:1] + mine_refs, whole_outs)]
    reduce_list = []
    for total, out in zip(total_refs, total_outs):
        reduce_list.append(Reduce(place, total, out, take(6 if len(total.shape) == 6 else 4)))
    steps = []

    def do_steps(count):
        for step in steps[:count]:
            step()
        del steps[:count]

    for item in reduce_list:
        item.start()
        steps += item.steps()
    for item in gather_list[1:] if scattered else gather_list:
        item.start()
    for copy in scattered[0] if scattered else ():
        copy.start()

    if gathers:
        whole = ref["whole"]
        own, beside_z, beside_y, corner = (rank(*chip, 0) for chip in ((0, 0), (1, 0), (0, 1), (1, 1)))
        halves = [part(h) for h in range(HALVES)]

        def sends(src, at, device):
            return [push(src.at[at, rows] if src is whole else src.at[rows], whole.at[at, rows], device) for rows in halves]

        own_places = [place.copy(mine.at[rows], whole.at[own, rows]) for rows in halves]
        own_to_core = sends(mine, own, to_sibling)
        from_z, from_y = sends(mine, own, to_z), sends(mine, own, to_y)
        from_corner = sends(whole, beside_z, to_y)
        z_to_core, y_to_core, corner_to_core = (sends(whole, at, to_sibling) for at in (beside_z, beside_y, corner))

    def send_mine(h):
        for copies in (from_z, from_y, own_to_core, own_places):
            copies[h].start()

    if kind in ("first", "turn"):
        for h in range(HALVES):
            send_mine(h)
    for copies in scattered[1:]:
        for copy in copies:
            copy.start()
    if scattered:
        for copy in scattered[0][:-1]:
            copy.wait_recv()
        scattered[0][-1].wait()
        gather_list[0].start()
    for item in gather_list:
        steps += item.steps()
    step_count = len(steps)

    if reduces:
        sib_copies = [push(ref["partial"].at[rank(*chip, 1)], sib.at[i], to_sibling) for i, chip in enumerate(chips)]
        for copy in sib_copies:
            copy.start()
        y_copies = [[push(yout.at[i, part(h)], yin.at[i, part(h)], to_y) for h in range(HALVES)] for i in range(2)]
        z_copies = [push(zout.at[part(h)], zin.at[part(h)], to_z) for h in range(HALVES)]

        def chip_sum(i, h):
            return near[i, part(h)].astype(F32) + sib[i, part(h)].astype(F32)

        for i in range(2):
            near_copies[i].wait()
            sib_copies[i].wait_recv()
            for h in range(HALVES):
                yout[i, part(h)] = chip_sum(i, h).astype(BF16)
                y_copies[i][h].start()
        near_copies[2].wait()
        sib_copies[2].wait_recv()
        for h in range(HALVES):
            y_copies[0][h].wait_recv()
            zout[part(h)] = (chip_sum(2, h) + yin[0, part(h)].astype(F32)).astype(BF16)
            z_copies[h].start()
        do_steps(step_count // 4)
        near_copies[3].wait()
        sib_copies[3].wait_recv()
        for h in range(HALVES):
            rows = part(h)
            y_copies[1][h].wait_recv()
            z_copies[h].wait_recv()
            total = chip_sum(3, h) + yin[1, rows].astype(F32) + zin[rows].astype(F32)
            stream = ref["stream"][rows]
            if kind in ("fwd", "turn"):
                stream = stream + total
                ref["stream_next"][rows] = stream
            if kind == "fwd":
                mine[rows] = (stream * rms_scale(stream) * ref["gain"][...]).astype(BF16)
                send_mine(h)
            if kind in ("bwd", "last"):
                scale = rms_scale(stream)
                gain_grad = jnp.sum(total * stream * scale, axis=0, keepdims=True)
                ref["gain_grad"][...] = gain_grad if h == 0 else ref["gain_grad"][...] + gain_grad
                scaled = total * ref["gain"][...]
                grad = (
                    ref["grad"][rows]
                    + scale * scaled
                    - stream * (scale * scale * scale) * jnp.mean(scaled * stream, axis=-1, keepdims=True)
                )
                ref["grad_next"][rows] = grad
                if kind == "bwd":
                    mine[rows] = grad.astype(BF16)
                    send_mine(h)
        do_steps(step_count // 4)

    if gathers:
        for h in range(HALVES):
            from_z[h].wait_recv()
            from_corner[h].start()
            z_to_core[h].start()
        do_steps(step_count // 4)
        for h in range(HALVES):
            from_y[h].wait_recv()
            y_to_core[h].start()
        for h in range(HALVES):
            from_corner[h].wait_recv()
            corner_to_core[h].start()
        for copy in own_places:
            copy.wait()
    do_steps(step_count)
    if gathers:
        for copy in own_to_core + z_to_core + y_to_core + corner_to_core:
            copy.wait_recv()
    for copies in scattered[1:]:
        for copy in copies[:-1]:
            copy.wait_recv()
        copies[-1].wait()
    for item in gather_list + reduce_list:
        item.finish()
    for copy in place.sent:
        copy.wait_send()


def exchange(kind, operands, use="", shards=(), mine=(), totals=(), groups=()):
    tokens, features = operands[IN_NAMES[kind].index("stream")].shape
    shapes = {
        "whole": ((8, tokens, features), BF16),
        "stream_next": ((tokens, features), F32),
        "grad_next": ((tokens, features), F32),
        "gain_grad": ((1, features), F32),
    }
    anywhere = pl.BlockSpec(memory_space=pl.ANY)
    inside = pl.BlockSpec(memory_space=pltpu.VMEM)
    block = (tokens, features)
    outs = [shapes[name] + (anywhere if name == "whole" else inside,) for name in OUT_NAMES[kind]]
    outs += [((4, 2) + array.shape[1:], BF16, anywhere) for array in shards]
    for array in [jax.ShapeDtypeStruct((4, 2) + array.shape[1:], BF16) for array in shards[:1]] + list(mine):
        if len(array.shape) == 4:
            outs.append(((4, 2, 2, 2) + array.shape[2:], BF16, anywhere))
        else:
            outs.append(((2, 2) + array.shape, BF16, anywhere))
    scratch = [
        pltpu.VMEM((4,) + block, BF16),
        pltpu.VMEM((4,) + block, BF16),
        pltpu.VMEM((2,) + block, BF16),
        pltpu.VMEM((2,) + block, BF16),
        pltpu.VMEM(block, BF16),
        pltpu.VMEM(block, BF16),
        pltpu.VMEM(block, BF16),
        pltpu.SemaphoreType.DMA((SEMAPHORES,)),
        pltpu.SemaphoreType.DMA((SEMAPHORES,)),
        pltpu.SemaphoreType.DMA((SEMAPHORES,)),
    ]
    for array, count in zip(totals, groups):
        if array.ndim == 6:
            rows = array.shape[4:]
            outs += [((rows[0], rows[1] // count * 8), F32, inside)] * count
            quarter = (4, 2) + rows
            scratch += [pltpu.VMEM((4, 2, 2) + rows, BF16)] * 2 + [pltpu.VMEM(quarter, BF16)] * 3
            scratch.append(pltpu.VMEM((8,) + rows, BF16))
        else:
            rows = array.shape[2:]
            outs.append((rows, F32, inside))
            scratch += [pltpu.VMEM((1, 2) + rows, BF16)] * 2 + [pltpu.VMEM((1,) + rows, BF16)] * 2
    plan = {
        "shards": len(shards), "mine": len(mine), "totals": len(totals), "wholes": len(shards[:1]) + len(mine),
        "groups": groups,
    }
    name = kind + use
    return pl.pallas_call(
        functools.partial(exchange_kernel, kind, plan),
        out_shape=tuple(jax.ShapeDtypeStruct(shape, dtype) for shape, dtype, _ in outs),
        in_specs=[anywhere if name == "partial" else inside for name in IN_NAMES[kind]]
        + [anywhere] * (len(shards) + len(mine) + len(totals)),
        out_specs=tuple(spec for _, _, spec in outs),
        scratch_shapes=scratch,
        compiler_params=pltpu.CompilerParams(
            collective_id=COLLECTIVE_ID[name], has_side_effects=True, vmem_limit_bytes=48 << 20
        ),
        cost_estimate=pl.CostEstimate(flops=10**7, bytes_accessed=150 * 10**6, transcendentals=0),
        name="exchange_" + name,
    )(*operands, *shards, *mine, *totals)


def matmul(left, right):
    return jnp.dot(left, right, preferred_element_type=F32)


def inner_rows(left, right):
    return lax.dot_general(left, right, (((0,), (0,)), ((), ())), preferred_element_type=F32)


def outer_cols(left, right):
    return lax.dot_general(left, right, (((1,), (1,)), ((), ())), preferred_element_type=F32)


def sizes_of(axes):
    return tuple(lax.axis_size(axis) for axis in axes)


def split_owners(array, dim):
    owners = sizes_of(OWNERS)
    count = 1
    for size in owners:
        count *= size
    shape = array.shape
    return array.reshape(shape[:dim] + owners + (shape[dim] // count,) + shape[dim + 1 :])


def column_shards(weights):
    rows = weights[0].shape[0]
    mains, rests = [], []
    for weight in weights:
        parts = split_owners(weight, 1).transpose(5, 2, 3, 0, 1, 4, 6, 7).reshape(8, rows, -1)
        main = parts.shape[2] // LANES * LANES
        mains.append(parts[:, :, :main])
        rests.append(parts[:, :, main:])
    return jnp.concatenate(mains + rests, axis=2)


def column_groups(values, groups):
    width = values.shape[-1] // groups
    return [
        jnp.concatenate([values[..., a:b] for a, b in pieces_of(groups, width, group, 0, width)], axis=-1)
        for group in range(groups)
    ]


def group_columns(groups):
    main = groups[0].shape[-1] // LANES * LANES
    return jnp.concatenate([g[..., :main] for g in groups] + [g[..., main:] for g in groups], axis=-1)


def column_whole(shards, groups):
    rows = shards.shape[1]
    yh, yl, core, zh, zl, x = sizes_of(OWNERS)
    return [
        part.reshape(zl, yl, core, rows, yh, zh, x, -1).transpose(3, 4, 1, 2, 5, 0, 6, 7).reshape(rows, -1)
        for part in column_groups(shards, groups)
    ]


def gather_columns(shards):
    mine = lax.all_to_all(shards, TP, split_axis=0, concat_axis=0, tiled=True)
    whole = lax.all_gather(mine, DP, axis=0, tiled=False)
    yh, yl, core, zh, zl, x = sizes_of(OWNERS)
    rows, columns = shards.shape[1:]
    whole = whole.reshape(yh, zh, x, zl, yl, core, rows, columns)
    return whole.transpose(0, 4, 5, 1, 3, 2, 6, 7).reshape(-1, columns)


def scatter_columns(total):
    yh, yl, core, zh, zl, x = sizes_of(OWNERS)
    columns = total.shape[1]
    parts = split_owners(total, 0).transpose(0, 3, 5, 4, 1, 2, 6, 7)
    parts = parts.reshape(yh * zh * x, -1, columns)
    mine = lax.psum_scatter(parts, DP, scatter_dimension=0, tiled=False)
    mine = mine.reshape(8, -1, columns)
    return lax.all_to_all(mine, TP, split_axis=0, concat_axis=0, tiled=True)


def tails_before(tails):
    x_size, zh_size = lax.axis_size("x"), lax.axis_size("zh")
    tails = tails.reshape((2, 4) + tails.shape[1:])
    beside = lax.ppermute(tails, "x", [(i, (i + 1) % x_size) for i in range(x_size)])
    pairs = [(i * x_size + x_size - 1, (i + 1) * x_size) for i in range(zh_size - 1)]
    below = lax.ppermute(tails[1], ("zh", "x"), pairs)
    first = jnp.stack([below, beside[0]])
    return jnp.where(lax.axis_index("x") == 0, first, beside).reshape((8,) + tails.shape[2:])


def heads_after(heads):
    x_size, zh_size = lax.axis_size("x"), lax.axis_size("zh")
    heads = heads.reshape((2, 4) + heads.shape[1:])
    beside = lax.ppermute(heads, "x", [((i + 1) % x_size, i) for i in range(x_size)])
    pairs = [((i + 1) * x_size, i * x_size + x_size - 1) for i in range(zh_size - 1)]
    above = lax.ppermute(heads[0], ("zh", "x"), pairs)
    final = jnp.stack([beside[1], above])
    return jnp.where(lax.axis_index("x") == x_size - 1, final, beside).reshape((8,) + heads.shape[2:])


def tap_masks(starts, token_count):
    zh, x, x_size = lax.axis_index("zh"), lax.axis_index("x"), lax.axis_size("x")
    blocks = (zh * 2 + jnp.arange(2, dtype=jnp.int32)) * x_size + x
    places = blocks[:, None] * token_count + jnp.arange(token_count, dtype=jnp.int32)

    def segment_of(where):
        return jnp.sum((starts[None, :, None, :] <= where[:, None, :, None]).astype(jnp.int32), axis=3)

    own_segment = segment_of(places)
    keep_one = (segment_of(places - 1) == own_segment).astype(F32)
    keep_two = (segment_of(places - 2) == own_segment).astype(F32)
    return keep_one.reshape(8, token_count, 1), keep_two.reshape(8, token_count, 1)


def conv_forward(joint, taps, keep_one, keep_two):
    positions = joint.shape[1]
    b_part, c_part, x_part = column_groups(joint, 3)
    carried = b_part * x_part
    previous = tails_before(carried[:, positions - 2 :])
    padded = jnp.concatenate([previous, carried], axis=1)
    mixed = (
        taps[:, 0] * padded[:, :positions] * keep_two
        + taps[:, 1] * padded[:, 1 : positions + 1] * keep_one
        + taps[:, 2] * carried
    )
    return (c_part * mixed).astype(BF16), mixed, padded


def conv_backward(grad_gated, joint, mixed, padded, taps, keep_one, keep_two):
    rows, positions, width = grad_gated.shape
    b_part, c_part, x_part = column_groups(joint, 3)
    grad_c = grad_gated * mixed
    grad_mixed = grad_gated * c_part
    first_tap = grad_mixed * keep_two
    second_tap = grad_mixed * keep_one
    grad_taps = jnp.stack(
        [
            jnp.sum(first_tap * padded[:, :positions], axis=(0, 1)),
            jnp.sum(second_tap * padded[:, 1 : positions + 1], axis=(0, 1)),
            jnp.sum(grad_mixed * padded[:, 2:], axis=(0, 1)),
        ],
        axis=0,
    )
    one = jnp.zeros((rows, 1, width), F32)
    two = jnp.zeros((rows, 2, width), F32)
    grad_padded = jnp.concatenate([first_tap * taps[:, 0], two], axis=1) + jnp.concatenate(
        [one, second_tap * taps[:, 1], one], axis=1
    )
    returned = heads_after(grad_padded[:, :2])
    arriving = jnp.concatenate([jnp.zeros((rows, positions - 2, width), F32), returned], axis=1)
    grad_carried = grad_padded[:, 2:] + grad_mixed * taps[:, 2] + arriving
    return group_columns([grad_carried * x_part, grad_c, grad_carried * b_part]).astype(BF16), grad_taps


def local(stream_in, doc_starts, norm_mix, in_proj, conv_taps, out_proj, norm_ffn, w_gate, w_up, w_down, grad_out):
    _, token_count, features = stream_in.shape
    layers = norm_mix.shape[0]
    def blocks(array):
        return array.reshape(8, token_count, -1)

    def flat(array):
        return array.reshape(8 * token_count, -1)

    own_kernels = sizes_of(DP) == (1, 2, 2)
    stream = stream_in.reshape(-1, features)
    grad_stream = grad_out.reshape(-1, features)
    small = jnp.concatenate([norm_mix[:, None], norm_ffn[:, None], conv_taps.transpose(0, 2, 1)], axis=1)
    small = small.astype(BF16).astype(F32)
    owned = small.shape[2]
    in_w, both_w, out_w, down_w = ([None] * layers for _ in range(4))
    if own_kernels:
        packed = jnp.zeros((16, LANES), F32).at[: 5 * layers, :owned].set(small.reshape(-1, owned))
        packed = packed.at[15, : doc_starts.shape[1]].set(doc_starts[0].astype(F32))
        spread, *results = prepare(packed, in_proj, w_gate, w_up, out_proj, w_down)
        shards, out_own, down_own = [], [], []
        for layer in range(layers):
            shards += results[4 * layer : 4 * layer + 2]
            out_own.append(results[4 * layer + 2])
            down_own.append(results[4 * layer + 3])
        params = spread[:, : 5 * layers, :owned].transpose(1, 0, 2)
        gains = params.reshape(layers, 5, 1, -1)[:, :2]
        params = params.reshape(layers, 5, 4, 2, 2, 2, owned)[:, 2:]
        others = lax.axis_index("yl") * 2 + lax.axis_index("core")
        params = lax.dynamic_index_in_dim(params, others, 2, False)
        taps_all = lax.dynamic_index_in_dim(params, lax.axis_index("zl"), 3, False)
        taps_all = taps_all.reshape(layers, 3, -1).transpose(0, 2, 1)
        starts = spread.reshape(4, 8, 16, LANES)[:, 0, 15, : doc_starts.shape[1]].astype(jnp.int32)
        normed, *results = exchange("first", (stream, gains[0, 0]), shards=shards, mine=(out_own[0], down_own[0]))
        mine, results = results[: len(shards)], results[len(shards) :]
        in_w[0], out_w[0], down_w[0] = results
    else:
        starts = lax.all_gather(doc_starts, ("yl", "core"), axis=0, tiled=True)
        small = small.astype(BF16)
        gains = lax.all_gather(small[:, :2], OWNERS, axis=2, tiled=True).astype(F32)[:, :, None]
        taps_all = lax.all_gather(small[:, 2:], DP, axis=2, tiled=True).astype(F32).transpose(0, 2, 1)
        (normed,) = exchange("first", (stream, gains[0, 0]))
        for layer in range(layers):
            in_w[layer] = gather_columns(column_shards(jnp.split(in_proj[layer].astype(BF16), 3, axis=1)))
            both_w[layer] = gather_columns(column_shards([w_gate[layer].astype(BF16), w_up[layer].astype(BF16)]))
            out_w[layer] = lax.all_gather(out_proj[layer].astype(BF16), DP, axis=0, tiled=True)
            down_w[layer] = lax.all_gather(w_down[layer].astype(BF16), DP, axis=0, tiled=True)
    keep_one, keep_two = tap_masks(starts, token_count)

    def rows_of(weight):
        return weight.reshape(-1, weight.shape[-1])

    saved = []
    for layer in range(layers):
        taps = taps_all[layer]
        normed = flat(normed)
        joint = blocks(matmul(normed, rows_of(in_w[layer])))
        gated, mixed, padded = conv_forward(joint, taps, keep_one, keep_two)
        gated = flat(gated)
        partial = blocks(matmul(gated, rows_of(out_w[layer])).astype(BF16))
        moved = (mine[2 * layer + 1],) if own_kernels else ()
        middle, normed_ffn, *results = exchange("fwd", (partial, stream, gains[layer, 1]), "_ffn", mine=moved)
        if own_kernels:
            (both_w[layer],) = results
        normed_ffn = flat(normed_ffn)
        gate_up = matmul(normed_ffn, rows_of(both_w[layer]))
        gate, up = column_groups(gate_up, 2)
        hidden = (jax.nn.silu(gate) * up).astype(BF16)
        saved.append((stream, normed, joint, mixed, padded, gated, middle, normed_ffn, gate, up, hidden))
        partial = blocks(matmul(hidden, rows_of(down_w[layer])).astype(BF16))
        if layer + 1 < layers:
            moved = (mine[2 * layer + 2], out_own[layer + 1], down_own[layer + 1]) if own_kernels else ()
            stream, normed, *results = exchange("fwd", (partial, middle, gains[layer + 1, 0]), "_conv", mine=moved)
            if own_kernels:
                in_w[layer + 1], out_w[layer + 1], down_w[layer + 1] = results
        else:
            stream, down_in = exchange("turn", (partial, middle, grad_stream))

    def by_owner(grad):
        return grad.astype(BF16).reshape(4, 2, 2, 2, -1, grad.shape[1])

    def by_part(grad):
        return grad.astype(BF16).reshape(2, 2, -1, grad.shape[1])

    pieces = [None] * layers
    for layer in reversed(range(layers)):
        source, normed, joint, mixed, padded, gated, middle, normed_ffn, gate, up, hidden = saved[layer]
        taps = taps_all[layer]
        down_in = flat(down_in)
        grad_hidden = outer_cols(down_in, rows_of(down_w[layer]))
        sigmoid = jax.nn.sigmoid(gate)
        grad_gate_up = group_columns(
            [grad_hidden * up * sigmoid * (1.0 + gate * (1.0 - sigmoid)), grad_hidden * gate * sigmoid]
        ).astype(BF16)
        partial = blocks(outer_cols(grad_gate_up, rows_of(both_w[layer])).astype(BF16))
        grad_down = inner_rows(hidden, down_in)
        grad_both = inner_rows(normed_ffn, grad_gate_up)
        totals = (by_owner(grad_both),) if own_kernels else ()
        grad_middle, grad_gain_ffn, mix_in, *results = exchange(
            "bwd", (partial, grad_stream, middle, gains[layer, 1]), "_ffn", totals=totals, groups=(2,)[: len(totals)]
        )
        if own_kernels:
            grad_gate, grad_up = results
        else:
            grad_gate, grad_up = column_whole(scatter_columns(grad_both.astype(BF16)).astype(F32), 2)
        mix_in = flat(mix_in)
        grad_gated = blocks(outer_cols(mix_in, rows_of(out_w[layer])))
        grad_joint, grad_taps = conv_backward(grad_gated, joint, mixed, padded, taps, keep_one, keep_two)
        grad_joint = flat(grad_joint)
        partial = blocks(outer_cols(grad_joint, rows_of(in_w[layer])).astype(BF16))
        grad_out_w, grad_in_w = inner_rows(gated, mix_in), inner_rows(normed, grad_joint)
        totals = (by_owner(grad_in_w), by_part(grad_out_w), by_part(grad_down)) if own_kernels else ()
        operands, groups = (partial, grad_middle, source, gains[layer, 0]), (3, 1, 1)[: len(totals)]
        if layer > 0:
            grad_stream, grad_gain_mix, down_in, *results = exchange("bwd", operands, "_conv", totals=totals, groups=groups)
        else:
            grad_stream, grad_gain_mix, *results = exchange("last", operands, totals=totals, groups=groups)
        if own_kernels:
            *grad_in_w, grad_out_w, grad_down = results
        else:
            grad_in_w = column_whole(scatter_columns(grad_in_w.astype(BF16)).astype(F32), 3)
            grad_out_w, grad_down = (
                lax.psum_scatter(grad.astype(BF16), DP, scatter_dimension=0, tiled=True).astype(F32)
                for grad in (grad_out_w, grad_down)
            )
        grad_in_w = jnp.concatenate(grad_in_w, axis=1)
        pieces[layer] = (grad_gain_mix, grad_in_w, grad_taps, grad_out_w, grad_gain_ffn, grad_gate, grad_up, grad_down)
    gain_grads = jnp.stack([jnp.concatenate([p[0], p[4]]) for p in pieces])
    tap_grads = jnp.stack([p[2] for p in pieces])
    if own_kernels:
        slabs = gain_grads.reshape(2 * layers, 32, owned).transpose(1, 0, 2)
        lanes = ((0, 0), (0, 0), (0, LANES - owned))
        taps = tap_grads.reshape(3 * layers, 2, 1, 2, owned).transpose(1, 2, 3, 0, 4)
        taps = jnp.pad(taps, ((0, 0), (0, 0), (0, 0), (0, 0), (0, LANES - owned)))
        same = (jnp.arange(4) == others)[:, None, None, None, None, None]
        same = same & (jnp.arange(2) == lax.axis_index("zl"))[None, None, :, None, None, None]
        taps = jnp.where(same, taps[None], 0.0).reshape(32, 3 * layers, LANES)
        rows = 16 - 5 * layers
        slabs = jnp.concatenate([jnp.pad(slabs, lanes), taps, jnp.zeros((32, rows, LANES), F32)], axis=1)
        sums = collect(slabs)[:, :owned]
        gain_grads = sums[: 2 * layers].reshape(layers, 2, owned)
        tap_grads = sums[2 * layers : 5 * layers].reshape(layers, 3, owned)
    else:
        gain_grads = lax.psum_scatter(gain_grads, OWNERS, scatter_dimension=2, tiled=True)
        tap_grads = lax.psum_scatter(tap_grads, DP, scatter_dimension=2, tiled=True)
    return (
        stream[None],
        grad_stream[None],
        gain_grads[:, 0],
        jnp.stack([p[1] for p in pieces]),
        tap_grads.transpose(0, 2, 1),
        jnp.stack([p[3] for p in pieces]),
        gain_grads[:, 1],
        jnp.stack([p[5] for p in pieces]),
        jnp.stack([p[6] for p in pieces]),
        jnp.stack([p[7] for p in pieces]),
    )


def solution(mesh):
    dp, seq = mesh.shape["dp"], mesh.shape["seq"]
    side = dp // 2
    split = Mesh(mesh.devices.reshape(side // 2, 2, 2, seq // side // 2, 2, side), OWNERS)
    token = P(ROW_AXES, SEQ_AXES, None)
    vector = P(None, OWNERS)
    matrix = P(None, OWNERS, None)
    return jax.shard_map(
        local,
        mesh=split,
        in_specs=(token, P(ROW_AXES, None), vector, matrix, matrix, matrix, vector, matrix, matrix, matrix, token),
        out_specs=(token, token, vector, matrix, matrix, matrix, vector, matrix, matrix, matrix),
        check_vma=False,
    )
```

time: 1440 us -> 970 us (0.67)
  waiting for transfers between devices: 426 us -> 0.32 us
  Pallas kernels: 370 us -> 698 us
  blocking collectives: 253 us -> 0 us
  local copies, waits for them, and re-layouts: 182 us -> 103 us
  starting transfers between devices: 46.7 us -> 8.49 us
  matrix products: 92 us -> 118 us
    pallas_call x9 -> x11, Pallas kernels: 370 us -> 698 us  [the longest x9 656 us: exchange(): pl.pallas_call(functools.partial(exchange_kernel, kind, plan), out_shape=...]
    reduce_scatter x8 -> x0, waiting for transfers between devices: 289 us -> none  [the longest x4 133 us: scatter_columns(): mine = lax.psum_scatter(parts, DP, scatter_dimension=0, tiled=False)]
    all_gather x5 -> x0, blocking collectives: 179 us -> none  [the longest x1 77.1 us: local(): lax.all_gather(small[:, :, :2], OWNERS, axis=1, tiled=True).astype(F32)]
    unnamed x18 -> x0, waiting for transfers between devices: 125 us -> none
    all_to_all x4 -> x0, blocking collectives: 74.2 us -> none  [the longest x3 60.2 us: gather_columns(): mine = lax.all_to_all(shards, TP, split_axis=0, concat_axis=0, tiled=True)]
    slice x12 -> x21, local copies, waits for them, and re-layouts: 42.9 us -> 11.3 us  [the longest x8 4.36 us: column_groups(): values[..., a:b]]
    transpose x12 -> x2, local copies, waits for them, and re-layouts: 27.4 us -> 0.07 us  [local(): params = spread[:, :5 * layers, :owned].transpose(1, 0, 2)]
    reshape x14 -> x7, local copies, waits for them, and re-layouts: 23.9 us -> 0.46 us  [the longest x2 0.14 us: local(): slabs = gain_grads.reshape(2 * layers, 32, owned).transpose(1, 0, 2)]
  transfers between devices with their start and end apart: 28 -> 8, of which waited for: 11 -> 1; matrix products, arithmetic and copies ran while one was open for 17% -> 2% of each run, Pallas kernels for 20% -> 0%
where the time goes in v3:
time: 970 us; the launch traced here: 961 us
  Pallas kernels  698 us (72%)
  matrix products  118 us (12%)
  local copies, waits for them, and re-layouts  103 us (11%)
  other arithmetic  30.7 us (3%)
    pallas_call x9, Pallas kernels, exchange(): pl.pallas_call(functools.partial(exchange_kernel, kind, plan), out_shape=...  656 us
    dot_general x8, matrix products, outer_cols(): lax.dot_general(left, right, (((1,), (1,)), ((), ())), preferred_element_...  42.4 us
    dot_general x8, matrix products, matmul(): return jnp.dot(left, right, preferred_element_type=F32)  38.9 us
    dot_general x8, matrix products, inner_rows(): lax.dot_general(left, right, (((0,), (0,)), ((), ())), preferred_element_...  36.7 us
    unnamed x289, local copies, waits for them, and re-layouts  29.4 us
    concatenate x12, local copies, waits for them, and re-layouts, group_columns(): jnp.concatenate([g[..., :main] for g in groups] + [g[..., main:] for g in...  25.4 us
    pallas_call x1, Pallas kernels, collect(): pl.pallas_call(collect_kernel, out_shape=jax.ShapeDtypeStruct(slabs.shape...  23.5 us
  transfers between devices with their start and end apart: 8, of which 1 were waited for; matrix products, arithmetic and copies ran while one was open for 2% of the time, Pallas kernels for 0%

profile of v3, /device:TPU:0, one launch (start us, length us, event | category | flops | bytes accessed | tf_op | source)
XLA Modules:
  0.0 960.8 jit_solution(12611025648403731468)
XLA Ops:
  3.9 18.4 %prepare.1 = (f32[32,16,128]{2,1,0:T(8,128)S(1)}, bf16[8,48,576]{2,1,0:T(8,128)(2,1)S(1)}, bf16[8,48,1152]{2,1,0:T(8,128)(2,1)S(1)}, bf16[48,1536]{1,0:T(8,128)(...) custom-call(f32[16,128]{1,0:T(8,128)S(1)} %scatter.14.small, ...), custom_call_target="tpu_custom_call" | custom-call | tf_op jit(solution)/shard_map/prepare/pallas_call | solution.py:173
  33.5 75.9 %exchange_first.1 = (bf16[8,128,1536]{2,1,0:T(8,128)(2,1)}, bf16[4,2,48,576]{3,2,1,0:T(8,128)(2,1)}, bf16[4,2,48,1152]{3,2,1,0:T(8,128)(2,1)S(1)}, bf16[4,2,48,5...) custom-call(f32[128,1536]{1,0:T(8,128)S(1)} %bitcast.216, ...), custom_call_target="tpu_custom_call" | custom-call | flops 10000000 | bytes 150000000 | tf_op jit(solution)/shard_map/exchange_first/pallas_call | solution.py:558
  109.4 4.9 fusion.39
  120.6 1.9 slice.409
  127.7 4.2 multiply_convert_fusion.7
  132.0 2.7 convolution_convert_fusion.7
  134.7 85.9 %exchange_fwd_ffn.2 = (f32[128,1536]{1,0:T(8,128)S(1)}, bf16[8,128,1536]{2,1,0:T(8,128)(2,1)S(1)}, bf16[4,2,2,2,48,1152]{5,4,3,2,1,0:T(8,128)(2,1)}) custom-call(bf16[8,128,1536]{2,1,0:T(8,128)(2,1)} %bitcast.247, f32[128,1536]{1,0:T(8,128)S(1)} %bitcast.217, f32[1,1536]{1,0:T(1,128)S(1)} %get-tuple-element.247.refs_2_.refs_3_, ...), custom_call_target="tpu_custom_call" | custom-call | flops 10000000 | bytes 150000000 | tf_op jit(solution)/shard_map/exchange_fwd_ffn/pallas_call | solution.py:558
  220.6 7.6 fusion.40
  231.9 4.1 convolution_convert_fusion.6
  236.0 84.3 %exchange_fwd_conv.1 = (f32[128,1536]{1,0:T(8,128)S(1)}, bf16[8,128,1536]{2,1,0:T(8,128)(2,1)}, bf16[4,2,2,2,48,576]{5,4,3,2,1,0:T(8,128)(2,1)}, bf16[2,2,48,153...) custom-call(bf16[8,128,1536]{2,1,0:T(8,128)(2,1)} %bitcast.267, f32[128,1536]{1,0:T(8,128)S(1)} %get-tuple-element.102.refs_1_.refs_2_, ...), custom_call_target="tpu_custom_call" | custom-call | flops 10000000 | bytes 150000000 | tf_op jit(solution)/shard_map/exchange_fwd_conv/pallas_call | solution.py:558
  320.4 5.4 fusion.41
  335.8 4.0 multiply_convert_fusion.6
  339.8 2.7 convolution_convert_fusion.5
  342.5 78.4 %exchange_fwd_ffn.3 = (f32[128,1536]{1,0:T(8,128)S(1)}, bf16[8,128,1536]{2,1,0:T(8,128)(2,1)S(1)}, bf16[4,2,2,2,48,1152]{5,4,3,2,1,0:T(8,128)(2,1)}) custom-call(bf16[8,128,1536]{2,1,0:T(8,128)(2,1)} %bitcast.246, f32[128,1536]{1,0:T(8,128)S(1)} %get-tuple-element.109.refs_1_.refs_2_, f32[1,1536]{1,0:T(1,128)S(1)} %get-tuple-element.245.refs_2_.refs_3_, ...), custom_call_target="tpu_custom_call" | custom-call | flops 10000000 | bytes 150000000 | tf_op jit(solution)/shard_map/exchange_fwd_ffn/pallas_call | solution.py:558
  420.9 7.4 fusion.42
  430.6 4.1 convolution_convert_fusion.4
  434.6 40.0 %exchange_turn.1 = (f32[128,1536]{1,0:T(8,128)S(1)}, bf16[8,128,1536]{2,1,0:T(8,128)(2,1)S(1)}) custom-call(bf16[8,128,1536]{2,1,0:T(8,128)(2,1)} %bitcast.262, f32[128,1536]{1,0:T(8,128)S(1)} %get-tuple-element.114.refs_1_.refs_2_, f32[128,1536]{1,0:T(8,128)S(1)} %bitcast.219), custom_call_target="tpu_custom_call" | custom-call | flops 10000000 | bytes 150000000 | tf_op jit(solution)/shard_map/exchange_turn/pallas_call | solution.py:558
  474.6 3.2 convolution_convert_fusion.11
  477.9 3.1 multiply_convert_fusion.2
  484.5 4.8 concatenate.144
  489.3 8.9 convolution_convert_fusion.1
  498.2 5.8 convolution_convert_fusion.9
  504.0 62.2 %exchange_bwd_ffn.2 = (f32[128,1536]{1,0:T(8,128)S(1)}, f32[1,1536]{1,0:T(1,128)S(1)}, bf16[8,128,1536]{2,1,0:T(8,128)(2,1)}, f32[48,4608]{1,0:T(8,128)S(1)}, f32[48,4608]{1,0:T(8,128)S(1)}) custom-call(bf16[8,128,1536]{2,1,0:T(8,128)(2,1)} %bitcast.261, f32[128,1536]{1,0:T(8,128)S(1)} %bitcast.220, f32[128,1536]{1,0:T(8,128)S(1)} %get-tuple-element.114.refs_1_.refs_2_, ...), custom_call_target="tpu_custom_call" | custom-call | flops 10000000 | bytes 150000000 | tf_op jit(solution)/shard_map/exchange_bwd_ffn/pallas_call | solution.py:558
  566.3 4.9 multiply_multiply_fusion.3
  578.6 2.7 fusion
  584.5 2.4 fusion.10
  589.7 3.3 bitcast_convert_fusion.1
  593.0 3.9 copy.151
  598.0 1.8 copy.180
  601.8 3.5 concatenate.154
  605.3 6.3 convolution_convert_fusion.3
  611.6 85.6 %exchange_bwd_conv.1 = (f32[128,1536]{1,0:T(8,128)S(1)}, f32[1,1536]{1,0:T(1,128)S(1)}, bf16[8,128,1536]{2,1,0:T(8,128)(2,1)}, f32[48,1536]{1,0:T(8,128)S(1)}, f...) custom-call(bf16[8,128,1536]{2,1,0:T(8,128)(2,1)} %bitcast.258, ...), custom_call_target="tpu_custom_call" | custom-call | flops 10000000 | bytes 150000000 | tf_op jit(solution)/shard_map/exchange_bwd_conv/pallas_call | solution.py:558
  697.3 5.8 convolution_convert_fusion.10
  703.2 4.9 multiply_convert_fusion
  709.3 4.8 concatenate.156
  714.1 8.9 convolution_convert_fusion
  723.0 5.8 convolution_convert_fusion.8
  728.8 64.8 %exchange_bwd_ffn.3 = (f32[128,1536]{1,0:T(8,128)S(1)}, f32[1,1536]{1,0:T(1,128)S(1)}, bf16[8,128,1536]{2,1,0:T(8,128)(2,1)}, f32[48,4608]{1,0:T(8,128)S(1)}, f32[48,4608]{1,0:T(8,128)S(1)}) custom-call(bf16[8,128,1536]{2,1,0:T(8,128)(2,1)} %bitcast.260, f32[128,1536]{1,0:T(8,128)S(1)} %copy-done.19, f32[128,1536]{1,0:T(8,128)S(1)} %copy-done.3, ...), custom_call_target="tpu_custom_call" | custom-call | flops 10000000 | bytes 150000000 | tf_op jit(solution)/shard_map/exchange_bwd_ffn/pallas_call | solution.py:558
  793.8 5.4 multiply_reduce_fusion.2
  808.1 2.8 pad_maximum_fusion.10
  816.8 2.5 fusion.14
  823.2 3.1 bitcast_convert_fusion
  826.3 3.9 copy.166
  831.4 1.7 copy.183
  835.2 3.5 concatenate.166
  838.7 6.3 convolution_convert_fusion.2
  845.1 78.9 %exchange_last.1 = (f32[128,1536]{1,0:T(8,128)S(1)}, f32[1,1536]{1,0:T(1,128)S(1)}, f32[48,1536]{1,0:T(8,128)S(1)}, f32[48,1536]{1,0:T(8,128)S(1)}, f32[48,1536]...) custom-call(bf16[8,128,1536]{2,1,0:T(8,128)(2,1)} %bitcast.259, f32[128,1536]{1,0:T(8,128)S(1)} %copy-done.15, ...), custom_call_target="tpu_custom_call" | custom-call | flops 10000000 | bytes 150000000 | tf_op jit(solution)/shard_map/exchange_last/pallas_call | solution.py:558
  928.7 23.5 %collect.1 = f32[16,128]{1,0:T(8,128)} custom-call(f32[32,16,128]{2,1,0:T(8,128)} %fusion.20.slabs), custom_call_target="tpu_custom_call" | custom-call | tf_op jit(solution)/shard_map/collect/pallas_call | solution.py:206
  (428 shorter events, 97.4 us)
Async XLA Ops:
  3.9 25.6 %copy-start = (f32[1,128,1536]{2,1,0:T(8,128)S(1)}, f32[1,128,1536]{2,1,0:T(8,128)}, u32[]{:S(2)}) copy-start(f32[1,128,1536]{2,1,0:T(8,128)} %param.15) | copy-start | bytes 2359300
  29.4 84.9 %copy-start.57 = (f32[1,1536]{1,0:T(1,128)}, f32[1,1536]{1,0:T(1,128)S(1)}, u32[]{:S(2)}) copy-start(f32[1,1536]{1,0:T(1,128)S(1)} %get-tuple-element.248.refs_1_.refs_3_) | copy-start | bytes 18436
  109.4 22.6 %copy-start.25 = (bf16[2,2,48,1536]{3,2,1,0:T(8,128)(2,1)}, bf16[2,2,48,1536]{3,2,1,0:T(8,128)(2,1)S(1)}, u32[]{:S(2)}) copy-start(bf16[2,2,48,1536]{3,2,1,0:T(8,128)(2,1)S(1)} %get-tuple-element.97) | copy-start | bytes 1769476
  119.8 6.7 collective-permute-start.1
  122.5 2.8 collective-permute-start
  125.1 6.9 copy-start.122
  125.1 210.7 %copy-start.124 = (f32[192,1]{0,1:T(1,128)}, f32[192,1]{0,1:T(1,128)S(1)}, u32[]{:S(2)}) copy-start(f32[192,1]{0,1:T(1,128)S(1)} %get-tuple-element.252) | copy-start | bytes 2308
  125.1 210.7 %copy-start.126 = (f32[192,1]{0,1:T(1,128)}, f32[192,1]{0,1:T(1,128)S(1)}, u32[]{:S(2)}) copy-start(f32[192,1]{0,1:T(1,128)S(1)} %get-tuple-element.251) | copy-start | bytes 2308
  125.1 210.7 %copy-start.128 = (f32[192,1]{0,1:T(1,128)}, f32[192,1]{0,1:T(1,128)S(1)}, u32[]{:S(2)}) copy-start(f32[192,1]{0,1:T(1,128)S(1)} %get-tuple-element.253) | copy-start | bytes 2308
  220.6 7.7 copy-start.59
  220.6 15.4 %copy-start.2 = (f32[128,1536]{1,0:T(8,128)}, f32[128,1536]{1,0:T(8,128)S(1)}, u32[]{:S(2)}) copy-start(f32[128,1536]{1,0:T(8,128)S(1)} %get-tuple-element.102.refs_1_.refs_2_) | copy-start | bytes 2359300
  320.3 19.4 %copy-start.4 = (bf16[2,2,48,1536]{3,2,1,0:T(8,128)(2,1)}, bf16[2,2,48,1536]{3,2,1,0:T(8,128)(2,1)S(1)}, u32[]{:S(2)}) copy-start(bf16[2,2,48,1536]{3,2,1,0:T(8,128)(2,1)S(1)} %get-tuple-element.108) | copy-start | bytes 1769476
  330.8 3.8 collective-permute-start.3
  330.8 2.2 collective-permute-start.2
  420.9 7.4 copy-start.60
  489.3 8.9 copy-start.105
  489.3 8.9 copy-start.132
  504.0 62.3 %copy-start.5 = (bf16[2,2,48,1536]{3,2,1,0:T(8,128)(2,1)S(1)}, bf16[2,2,48,1536]{3,2,1,0:T(8,128)(2,1)}, u32[]{:S(2)}) copy-start(bf16[2,2,48,1536]{3,2,1,0:T(8,128)(2,1)} %copy-done.4) | copy-start | bytes 1769476
  504.0 62.3 %copy-start.81 = (f32[8,128,128]{1,2,0:T(8,128)S(1)}, f32[8,128,128]{1,2,0:T(8,128)}, u32[]{:S(2)}) copy-start(f32[8,128,128]{1,2,0:T(8,128)} %get-tuple-element.233) | copy-start | bytes 1572868
  504.0 62.3 %copy-start.127 = (f32[192,1]{0,1:T(1,128)S(1)}, f32[192,1]{0,1:T(1,128)}, u32[]{:S(2)}) copy-start(f32[192,1]{0,1:T(1,128)} %copy-done.126) | copy-start | bytes 2308
  571.2 13.4 %copy-start.73 = (f32[8,128,192]{1,2,0:T(8,128)}, f32[8,128,192]{1,2,0:T(8,128)S(1)}, u32[]{:S(2)}) copy-start(f32[8,128,192]{1,2,0:T(8,128)S(1)} %get-tuple-element.214) | copy-start | bytes 2359300
  572.2 6.4 copy-start.80
  575.8 7.5 collective-permute-start.4
  577.1 5.0 collective-permute-start.5
  605.3 6.3 copy-start.17
  611.6 85.7 %copy-start.114 = (bf16[1024,576]{1,0:T(8,128)(2,1)S(1)}, bf16[1024,576]{1,0:T(8,128)(2,1)}, u32[]{:S(2)}) copy-start(bf16[1024,576]{1,0:T(8,128)(2,1)} %copy-done.113) | copy-start | bytes 3538948
  697.2 5.9 copy-start.18
  714.1 8.9 copy-start.106
  714.1 8.9 copy-start.131
  728.8 64.9 %copy-start.26 = (bf16[2,2,48,1536]{3,2,1,0:T(8,128)(2,1)S(1)}, bf16[2,2,48,1536]{3,2,1,0:T(8,128)(2,1)}, u32[]{:S(2)}) copy-start(bf16[2,2,48,1536]{3,2,1,0:T(8,128)(2,1)} %copy-done.25) | copy-start | bytes 1769476
  728.8 65.0 %copy-start.64 = (f32[8,128,192]{1,2,0:T(8,128)S(1)}, f32[8,128,192]{1,2,0:T(8,128)}, u32[]{:S(2)}) copy-start(f32[8,128,192]{1,2,0:T(8,128)} %copy-done.63) | copy-start | bytes 2359300
  728.8 65.0 %copy-start.66 = (f32[8,128,192]{1,2,0:T(8,128)S(1)}, f32[8,128,192]{1,2,0:T(8,128)}, u32[]{:S(2)}) copy-start(f32[8,128,192]{1,2,0:T(8,128)} %copy-done.65) | copy-start | bytes 2359300
  728.8 65.0 %copy-start.74 = (f32[8,128,192]{1,2,0:T(8,128)S(1)}, f32[8,128,192]{1,2,0:T(8,128)}, u32[]{:S(2)}) copy-start(f32[8,128,192]{1,2,0:T(8,128)} %copy-done.73) | copy-start | bytes 2359300
  728.8 65.0 %copy-start.90 = (f32[2,4,2,192]{2,3,1,0:T(8,128)S(1)}, f32[2,4,2,192]{2,3,1,0:T(8,128)}, u32[]{:S(2)}) copy-start(f32[2,4,2,192]{2,3,1,0:T(8,128)} %copy.129) | copy-start | bytes 36868
  728.8 65.0 %copy-start.91 = (f32[2,4,2,192]{2,3,1,0:T(8,128)S(1)}, f32[2,4,2,192]{2,3,1,0:T(8,128)}, u32[]{:S(2)}) copy-start(f32[2,4,2,192]{2,3,1,0:T(8,128)} %copy.135) | copy-start | bytes 36868
  728.8 65.0 %copy-start.107 = (f32[8,128,128]{1,2,0:T(8,128)S(1)}, f32[8,128,128]{1,2,0:T(8,128)}, u32[]{:S(2)}) copy-start(f32[8,128,128]{1,2,0:T(8,128)} %get-tuple-element.239) | copy-start | bytes 1572868
  728.8 65.0 %copy-start.116 = (f32[8,128,64]{1,2,0:T(8,128)S(1)}, f32[8,128,64]{1,2,0:T(8,128)}, u32[]{:S(2)}) copy-start(f32[8,128,64]{1,2,0:T(8,128)} %get-tuple-element.242) | copy-start | bytes 786436
  804.3 6.6 copy-start.7
  805.9 9.7 %collective-permute-start.6 = (f32[2,4,2,192]{3,1,2,0:T(4,128)S(1)}, f32[2,4,2,192]{3,1,2,0:T(4,128)S(1)}, u32[]{:S(2)}, u32[]{:S(2)}) collective-permute-start(f32[2,4,2,192]{3,1,2,0:T(4,128)S(1)} %copy.154), channel_id=1, source_target_pairs={{1,0},{0,1},{3,2},{2,3},{5,4},{4,5},{7,6},{6,7},{9,8},{8,9},{11,10... | collective-permute-start | bytes 36872 | tf_op jit(solution)/shard_map/ppermute | solution.py:663
  806.4 8.0 collective-permute-start.7
  826.3 6.8 copy-start.120
  826.3 7.6 copy-start.118
  826.3 8.5 copy-start.117
  838.7 6.4 copy-start.15
  838.7 6.4 copy-start.58
  845.1 82.9 %copy-start.121 = (f32[32,6,128]{2,1,0:T(8,128)S(1)}, f32[32,6,128]{2,1,0:T(8,128)}, u32[]{:S(2)}) copy-start(f32[32,6,128]{2,1,0:T(8,128)} %bitcast_select_fusion) | copy-start | bytes 294916
  927.9 28.3 %copy-start.50 = (f32[48,1536]{1,0:T(8,128)S(1)}, f32[48,1536]{1,0:T(8,128)}, u32[]{:S(2)}) copy-start(f32[48,1536]{1,0:T(8,128)} %copy-done.49) | copy-start | bytes 884740
  927.9 28.3 %copy-start.52 = (f32[48,1536]{1,0:T(8,128)S(1)}, f32[48,1536]{1,0:T(8,128)}, u32[]{:S(2)}) copy-start(f32[48,1536]{1,0:T(8,128)} %copy-done.51) | copy-start | bytes 884740
  (97 other events, 278.7 us)

commit v4 on v3

v4 whole, which is shorter than its diff:
```python
import functools
import itertools

import jax
import jax.numpy as jnp
from jax import lax
from jax.experimental import pallas as pl
from jax.experimental.pallas import tpu as pltpu
from jax.sharding import Mesh, PartitionSpec as P

EPSILON = 1e-05
TP = ("zl", "yl", "core")
DP = ("yh", "zh", "x")
ROW_AXES = ("yh", "yl", "core")
SEQ_AXES = ("zh", "zl", "x")
OWNERS = ROW_AXES + SEQ_AXES
BF16 = jnp.bfloat16
F32 = jnp.float32
MESH = pl.DeviceIdType.MESH
HALVES = 2
OWN_IN = {
    "conv": ("mine", "stream", "gain", "taps", "keep"),
    "ffn": ("mine", "stream", "gain"),
    "conv_back": ("mine", "grad", "stream", "gain", "taps", "keep"),
    "ffn_back": ("mine", "grad", "stream", "gain"),
}
GROUP_IN = {
    "conv": ("in_w", "out_w"),
    "ffn": ("both_w", "down_w"),
    "conv_back": ("in_w", "out_w", "whole", "joint", "carried", "mixed", "gated"),
    "ffn_back": ("both_w", "down_w", "whole", "gate_up", "hidden"),
}
OWN_OUT = {
    "conv": ("stream_next", "next"),
    "ffn": ("stream_next", "next"),
    "conv_back": ("grad_next", "gain_grad", "next", "grad_taps"),
    "ffn_back": ("grad_next", "gain_grad", "next"),
}
GROUP_OUT = {
    "conv": ("whole", "joint", "carried", "mixed", "gated"),
    "ffn": ("whole", "gate_up", "hidden"),
    "conv_back": ("grad_in_w", "grad_out_w"),
    "ffn_back": ("grad_both_w", "grad_down_w"),
}
COLLECTIVE_ID = {
    name: i
    for i, name in enumerate(
        ("prepare", "finish", "conv", "ffn", "ffn_moving", "conv_back", "ffn_back", "ffn_back_moving")
    )
}
FLIPS = ((1, 1, 1), (1, 1, 0), (1, 0, 1), (1, 0, 0), (0, 1, 1), (0, 1, 0), (0, 0, 1))
OTHERS = tuple(itertools.product((0, 1), repeat=5))[1:]
OTHER_AXES = ("yl", "core", "zh", "zl", "x")
SEMAPHORES = 112
LANES = 128
TILE = 256
HALO = 8


def rms_scale(values):
    return lax.rsqrt(jnp.mean(values * values, axis=-1, keepdims=True) + EPSILON)


class Place:
    def __init__(self, send, recv, local):
        self.zl, self.yl, self.core = (lax.axis_index(axis) for axis in TP)
        self.zh, self.x = lax.axis_index("zh"), lax.axis_index("x")
        self.send, self.recv, self.local = send, recv, local
        self.remote_count = self.local_count = 0
        self.sent = []

    def rank(self, flip_z, flip_y, flip_core):
        return self.flipped("zl", flip_z) * 4 + self.flipped("yl", flip_y) * 2 + self.flipped("core", flip_core)

    def flipped(self, axis, flip):
        return 1 - getattr(self, axis) if flip else getattr(self, axis)

    def member(self, flips):
        return {axis: 1 - getattr(self, axis) for axis, flip in zip(TP, flips) if flip}

    def beside(self, axis):
        return {axis: 1 - getattr(self, axis)}

    def owner(self, flips=(0,) * 5):
        index = 0
        for axis, flip in zip(OTHER_AXES, flips):
            index = index * 2 + self.flipped(axis, flip)
        return index

    def push(self, src, dst, device, kept=True):
        index = self.remote_count
        self.remote_count += 1
        copy = pltpu.make_async_remote_copy(
            src_ref=src, dst_ref=dst, send_sem=self.send.at[index], recv_sem=self.recv.at[index],
            device_id=device, device_id_type=MESH,
        )
        if kept:
            self.sent.append(copy)
        return copy

    def copy(self, src, dst):
        index = self.local_count
        self.local_count += 1
        return pltpu.make_async_copy(src, dst, self.local.at[index])


def pieces_of(groups, width, group, low, high):
    main = width // LANES * LANES
    rest = width - main
    ranges = []
    if low < main:
        ranges.append((group * main + low, group * main + min(high, main)))
    if high > main:
        start = groups * main + group * rest - main
        ranges.append((start + max(low, main), start + high))
    return ranges


def shards_from(weights, out):
    width = weights[0].shape[1] // 8
    block = width // 4
    main = width // LANES * LANES
    rest = width - main
    for group, weight in enumerate(weights):
        for member in range(8):
            zl, others = member // 4, member % 4
            starts = [((others * 2 + zh) * 4 + zl * 2 + x) * block for zh in range(2) for x in range(2)]
            values = jnp.concatenate([weight[:, start : start + block] for start in starts], axis=1).astype(BF16)
            out[member, :, group * main : (group + 1) * main] = values[:, :main]
            if rest:
                low = len(weights) * main + group * rest
                out[member, :, low : low + rest] = values[:, main:]
    pad = out.shape[2] - len(weights) * width
    if pad:
        out[:, :, len(weights) * width :] = jnp.zeros((8, out.shape[1], pad), BF16)


def shards_to(shards, outs):
    groups, width = len(outs), outs[0].shape[1] // 8
    block = width // 4
    for group, out in enumerate(outs):
        for others in range(4):
            for zh in range(2):
                values = []
                for zl in range(2):
                    for x in range(2):
                        low = (zh * 2 + x) * block
                        for start, end in pieces_of(groups, width, group, low, low + block):
                            values.append(shards[zl * 4 + others, :, start:end].astype(F32))
                start = (others * 2 + zh) * 4 * block
                out[:, start : start + 4 * block] = jnp.concatenate(values, axis=1)


def every_other(place):
    return [
        ({axis: place.flipped(axis, 1) for axis, flip in zip(OTHER_AXES, flips) if flip}, flips) for flips in OTHERS
    ]


def prepare_kernel(layers, small, in_proj, gate, up, out_proj, down, *refs):
    refs = list(refs)

    def take(count):
        taken = refs[:count]
        del refs[:count]
        return taken

    (spread,), mine, rounded, wholes = take(1), take(2 * layers), take(2 * layers), take(3)
    shards, (send, recv, local) = take(2 * layers), take(3)
    place = Place(send, recv, local)
    barrier = pltpu.get_barrier_semaphore()
    for device, _ in every_other(place):
        pl.semaphore_signal(barrier, inc=1, device_id=device, device_id_type=MESH)
    width = in_proj.shape[2] // 3

    def cut(layer, which):
        if which == 0:
            shards_from([in_proj.at[layer, :, i * width : (i + 1) * width] for i in range(3)], shards[2 * layer])
        else:
            shards_from([gate.at[layer], up.at[layer]], shards[2 * layer + 1])

    def scatter(index):
        here = mine[index].at[place.yl * 2 + place.core, place.zl]
        copies = [place.push(shards[index].at[place.rank(*flips)], here, place.member(flips)) for flips in FLIPS]
        copies.append(place.copy(shards[index].at[place.rank(0, 0, 0)], here))
        for copy in copies:
            copy.start()
        return copies

    def landed(copies):
        for copy in copies[:-1]:
            copy.wait_recv()
        copies[-1].wait()

    cut(0, 0)
    for layer in range(layers):
        rounded[2 * layer][...] = out_proj[layer].astype(BF16)
        rounded[2 * layer + 1][...] = down[layer].astype(BF16)
    pl.semaphore_wait(barrier, len(OTHERS))
    kept = place.copy(small, spread.at[place.owner()])
    kept.start()
    spreads = [place.push(small, spread.at[place.owner()], device) for device, _ in every_other(place)]
    first = scatter(0)
    for copy in spreads:
        copy.start()
    gathers = [Gather(place, own, whole) for own, whole in zip([mine[0]] + list(rounded[:2]), wholes)]
    for gather in gathers[1:]:
        gather.start()
    cut(0, 1)
    landed(first)
    gathers[0].start()
    others = [scatter(1)]
    for layer in range(1, layers):
        for which in range(2):
            cut(layer, which)
            others.append(scatter(2 * layer + which))
    for gather in gathers[1:] + gathers[:1]:
        for step in gather.steps():
            step()
    for copies in others:
        landed(copies)
    kept.wait()
    for copy in spreads:
        copy.wait_recv()
    for gather in gathers:
        gather.finish()
    for copy in place.sent:
        copy.wait_send()


def whole_shape(mine):
    return (4, 2, 2, 2) + mine[2:] if len(mine) == 4 else (2, 2) + mine


def prepare(small, in_proj, gate, up, out_proj, down):
    layers, rows, columns = in_proj.shape
    widths = (-(-columns // 8 // LANES) * LANES, gate.shape[2] // 4)
    inside = pl.BlockSpec(memory_space=pltpu.VMEM)
    anywhere = pl.BlockSpec(memory_space=pl.ANY)
    mine = [(4, 2, rows, width) for _ in range(layers) for width in widths]
    rounded = [array.shape[1:] for _ in range(layers) for array in (out_proj, down)]
    wholes = [whole_shape(shape) for shape in [mine[0]] + rounded[:2]]
    outs = pl.pallas_call(
        functools.partial(prepare_kernel, layers),
        out_shape=[jax.ShapeDtypeStruct((32,) + small.shape, F32)]
        + [jax.ShapeDtypeStruct(shape, BF16) for shape in mine + rounded + wholes],
        in_specs=[inside] * 6,
        out_specs=[anywhere] * (1 + len(mine)) + [inside] * len(rounded) + [anywhere] * 3,
        scratch_shapes=[pltpu.VMEM((8, rows, width), BF16) for _ in range(layers) for width in widths]
        + [pltpu.SemaphoreType.DMA((SEMAPHORES,))] * 3,
        compiler_params=pltpu.CompilerParams(
            collective_id=COLLECTIVE_ID["prepare"], has_side_effects=True, vmem_limit_bytes=48 << 20
        ),
        name="prepare",
    )(small, in_proj, gate, up, out_proj, down)
    spread, outs = outs[0], outs[1:]
    return spread, outs[: len(mine)], outs[len(mine) : -3], outs[-3:]


def finish_kernel(counts, slabs, *refs):
    refs = list(refs)

    def take(count):
        taken = refs[:count]
        del refs[:count]
        return taken

    totals = take(len(counts))
    (out,) = take(1)
    outs = [take(count) for count in counts]
    (landed,) = take(1)
    scratch = [take(6 if len(total.shape) == 6 else 4) for total in totals]
    place = Place(*take(3))
    barrier = pltpu.get_barrier_semaphore()
    for device, _ in every_other(place):
        pl.semaphore_signal(barrier, inc=1, device_id=device, device_id_type=MESH)
    pl.semaphore_wait(barrier, len(OTHERS))
    reduces = [Reduce(place, *group) for group in zip(totals, outs, scratch)]
    for item in reduces:
        item.start()
    copies = []
    for i, (device, flips) in enumerate(every_other(place)):
        copies.append(place.push(slabs.at[place.owner(flips)], landed.at[i], device))
        copies[-1].start()
    for step in interleaved([item.steps() for item in reduces]):
        step()
    for copy in copies:
        copy.wait_recv()
    out[...] = slabs[place.owner()] + jnp.sum(landed[...], axis=0)
    for item in reduces:
        item.finish()
    for copy in place.sent:
        copy.wait_send()


def finish(slabs, totals, groups):
    inside = pl.BlockSpec(memory_space=pltpu.VMEM)
    anywhere = pl.BlockSpec(memory_space=pl.ANY)
    outs, scratch = reduce_shapes(totals, groups)
    return pl.pallas_call(
        functools.partial(finish_kernel, groups),
        out_shape=[jax.ShapeDtypeStruct(slabs.shape[1:], F32)] + outs,
        in_specs=[inside] + [anywhere] * len(totals),
        out_specs=[inside] * (1 + len(outs)),
        scratch_shapes=[pltpu.VMEM((len(OTHERS),) + slabs.shape[1:], F32)]
        + scratch
        + [pltpu.SemaphoreType.DMA((SEMAPHORES,))] * 3,
        compiler_params=pltpu.CompilerParams(
            collective_id=COLLECTIVE_ID["finish"], has_side_effects=True, vmem_limit_bytes=48 << 20
        ),
        name="finish",
    )(slabs, *totals)


def interleaved(lists):
    keyed = [((i + 1) / len(items), n, item) for n, items in enumerate(lists) for i, item in enumerate(items)]
    return [item for _, _, item in sorted(keyed, key=lambda entry: entry[:2])]


def reduce_shapes(totals, groups):
    outs, scratch = [], []
    for array, count in zip(totals, groups):
        if array.ndim == 6:
            rows = array.shape[4:]
            width = rows[1] // LANES * LANES if count == 2 else rows[1] - LANES // 2
            outs += [jax.ShapeDtypeStruct((rows[0], width // count * 8), F32)] * count
            quarter = (4, 2) + rows
            scratch += [pltpu.VMEM((4, 2, 2) + rows, BF16)] * 2 + [pltpu.VMEM(quarter, BF16)] * 3
            scratch.append(pltpu.VMEM((8,) + rows, BF16))
        else:
            rows = array.shape[2:]
            outs.append(jax.ShapeDtypeStruct(rows, F32))
            scratch += [pltpu.VMEM((1, 2) + rows, BF16)] * 2 + [pltpu.VMEM((1,) + rows, BF16)] * 2
    return outs, scratch


class Gather:
    def __init__(self, place, mine, whole):
        self.columns = len(whole.shape) == 6
        self.chunks = whole.shape[0] if self.columns else 1
        self.mine, self.whole, self.place = mine, whole, place
        own, other = place.zh, 1 - place.zh
        self.along_z = [place.push(self.of_mine(c), self.at(c, own), place.beside("zh")) for c in range(self.chunks)]
        self.along_x = [place.push(self.of_mine(c), self.at(c, own), place.beside("x")) for c in range(self.chunks)]
        self.onward = [place.push(self.at(c, other), self.at(c, other), place.beside("x")) for c in range(self.chunks)]
        self.kept = [place.copy(self.of_mine(c), self.at(c, own)) for c in range(self.chunks)]

    def of_mine(self, c):
        return self.mine.at[c] if self.columns else self.mine

    def at(self, c, zh):
        return self.whole.at[c, zh, :, self.place.x] if self.columns else self.whole.at[zh, self.place.x]

    def start(self):
        for copies in (self.along_z, self.along_x, self.kept):
            for copy in copies:
                copy.start()

    def steps(self):
        def step(c):
            self.along_z[c].wait_recv()
            self.onward[c].start()
        return [functools.partial(step, c) for c in range(self.chunks)]

    def finish(self):
        for c in range(self.chunks):
            self.along_x[c].wait_recv()
            self.onward[c].wait_recv()
            self.kept[c].wait()


class Reduce:
    def __init__(self, place, total, outs, scratch):
        self.columns = len(total.shape) == 6
        self.place, self.total, self.outs = place, total, outs
        self.own, self.xin, self.zout, self.zin = scratch[:4]
        self.final, self.landed = scratch[4:] if self.columns else (None, None)
        self.chunks = 4 if self.columns else 1
        x, beside = place.x, place.beside
        pick = self.pick
        self.along_x = [place.push(pick(j, 1 - x), self.xin.at[j], beside("x")) for j in range(self.chunks)]
        self.kept = [place.copy(pick(j, x), self.own.at[j]) for j in range(self.chunks)]
        self.along_z = [place.push(self.zout.at[j], self.zin.at[j], beside("zh")) for j in range(self.chunks)]
        if self.columns:
            mine = place.rank(0, 0, 0)
            self.back = [
                [
                    place.push(self.final.at[j, fz], self.landed.at[mine], place.member((fz,) + self.flips(j)))
                    if (fz,) + self.flips(j) != (0, 0, 0)
                    else place.copy(self.final.at[j, fz], self.landed.at[mine])
                    for fz in (1, 0)
                ]
                for j in range(4)
            ]

    def flips(self, j):
        return ((1, 1), (1, 0), (0, 1), (0, 0))[j]

    def pick(self, j, x):
        if not self.columns:
            return self.total.at[:, x]
        flip_y, flip_core = self.flips(j)
        return self.total.at[self.place.flipped("yl", flip_y) * 2 + self.place.flipped("core", flip_core), :, :, x]

    def start(self):
        for j in range(self.chunks):
            self.along_x[j].start()
            self.kept[j].start()

    def steps(self):
        def first(j):
            self.kept[j].wait()
            self.along_x[j].wait_recv()
            there = 1 - self.place.zh
            self.zout[j] = (self.own[j, there].astype(F32) + self.xin[j, there].astype(F32)).astype(BF16)
            self.along_z[j].start()

        def second(j):
            self.along_z[j].wait_recv()
            here = self.place.zh
            total = self.own[j, here].astype(F32) + self.xin[j, here].astype(F32) + self.zin[j].astype(F32)
            if not self.columns:
                self.outs[0][...] = total
                return
            zl = self.place.zl
            for i, fz in enumerate((1, 0)):
                row = 1 - zl if fz else zl
                self.final[j, fz] = (
                    self.own[j, here, row].astype(F32) + self.xin[j, here, row].astype(F32) + self.zin[j, row].astype(F32)
                ).astype(BF16)
                self.back[j][i].start()

        steps = [functools.partial(first, 0)]
        for j in range(1, self.chunks):
            steps += [functools.partial(first, j), functools.partial(second, j - 1)]
        return steps + [functools.partial(second, self.chunks - 1)]

    def finish(self):
        if self.columns:
            for copies in self.back:
                for copy in copies:
                    if copy is self.back[3][1]:
                        copy.wait()
                    else:
                        copy.wait_recv()
            shards_to(self.landed, self.outs)


def loop(count, body):
    def step(i, carry):
        body(i)
        return carry

    lax.fori_loop(0, count, step, 0)


def tile(i, width=TILE):
    return pl.ds(pl.multiple_of(i * width, width), width)


def dot(left, right):
    return jnp.dot(left, right, preferred_element_type=F32)


def dot_cols(left, right):
    return lax.dot_general(left, right, (((1,), (1,)), ((), ())), preferred_element_type=F32)


def dot_rows(left, right):
    return lax.dot_general(left, right, (((0,), (0,)), ((), ())), preferred_element_type=F32)


def swap_half(values):
    return pltpu.roll(values, LANES // 2, 1)


class Halo:
    def __init__(self, place, buffer, edge, halo, forward):
        x, zh, count = place.x, place.zh, lax.axis_size("x")
        first, final = x == 0, x == count - 1
        low, high = pl.ds(0, 4), pl.ds(4, 4)
        lead = len(buffer.shape) - 3
        lead = (slice(None),) * lead

        def at(blocks, rows):
            return buffer.at[lead + (blocks, rows)]

        every = pl.ds(0, 8)
        step = lax.rem(x + 1, count) if forward else lax.rem(x + count - 1, count)
        if forward:
            within, turn, beyond = jnp.logical_not(final), final, jnp.logical_and(final, zh == 0)
            into, turned, entered = jnp.logical_not(first), first, jnp.logical_and(first, zh == 1)
            sent, landing = low, high
        else:
            within, turn, beyond = jnp.logical_not(first), first, jnp.logical_and(first, zh == 1)
            into, turned, entered = jnp.logical_not(final), final, jnp.logical_and(final, zh == 0)
            sent, landing = high, low
        copies = [
            place.push(at(every, edge), at(every, halo), {"x": step}, False),
            place.push(at(sent, edge), at(landing, halo), {"x": step}, False),
            place.push(at(landing, edge), at(sent, halo), {"x": step, "zh": 1 - zh}, False),
        ]
        self.sends = list(zip((within, turn, beyond), copies))
        self.lands = list(zip((into, turned, entered), copies))
        self.unreached = jnp.logical_and(turned, jnp.logical_not(entered))
        self.open_end = lead + (sent, halo)
        self.buffer = buffer

    def start(self):
        for condition, copy in self.sends:
            pl.when(condition)(copy.start)

        @pl.when(self.unreached)
        def _():
            shape = self.buffer.at[self.open_end].shape
            self.buffer[self.open_end] = jnp.zeros(shape, self.buffer.dtype)

    def wait_recv(self):
        for condition, copy in self.lands:
            pl.when(condition)(copy.wait_recv)

    def wait_send(self):
        for condition, copy in self.sends:
            pl.when(condition)(copy.wait_send)


def phase_kernel(kind, plan, *refs):
    back = kind in ("ffn_back", "conv_back")
    conv = kind in ("conv", "conv_back")
    refs = list(refs)

    def take(count):
        taken = refs[:count]
        del refs[:count]
        return taken

    ref = dict(zip(OWN_IN[kind], take(len(OWN_IN[kind]))))
    loads = dict(zip(GROUP_IN[kind], take(len(GROUP_IN[kind]))))
    mine_refs, total_refs = take(plan["mine"]), take(len(plan["groups"]))
    ref.update(zip(OWN_OUT[kind], take(len(OWN_OUT[kind]))))
    saves = dict(zip(GROUP_OUT[kind], take(len(GROUP_OUT[kind]))))
    whole_outs = take(plan["mine"])
    total_outs = [take(count) for count in plan["groups"]]
    buffer = dict(zip(plan["buffers"], take(len(plan["buffers"]))))
    whole, part, sib, yin, yout, zin, zout = take(7)
    scratch = [take(6 if len(total.shape) == 6 else 4) for total in total_refs]
    place = Place(*take(3))
    rank, push = place.rank, place.push
    mine = ref["mine"]
    tokens, features = mine.shape
    half = tokens // HALVES
    halves = [pl.ds(h * half, half) for h in range(HALVES)]
    to_sibling, to_y, to_z = (place.beside(axis) for axis in ("core", "yl", "zl"))
    chips = ((0, 0), (1, 0), (0, 1), (1, 1))
    own, beside_z, beside_y, corner = (rank(*chip, 0) for chip in chips)

    loading = {}
    for name, source in loads.items():
        target = buffer[name]
        if target.shape != source.shape:
            target[source.shape[0] :] = jnp.zeros((target.shape[0] - source.shape[0],) + target.shape[1:], BF16)
            target = target.at[: source.shape[0]]
        loading[name] = place.copy(source, target)
        loading[name].start()
    saving = []

    def save(name, source):
        saving.append(place.copy(source, saves[name]))
        saving[-1].start()

    def loaded(*names):
        for name in names:
            loading[name].wait()

    barrier = pltpu.get_barrier_semaphore()
    partners = [to_sibling, to_y, to_z]
    if whole_outs or total_refs:
        partners += [place.beside("zh"), place.beside("x")]
    if any(len(total.shape) == 6 for total in total_refs):
        partners += [place.member(flips) for flips in FLIPS if sum(flips) > 1]
    x, zh, x_size = place.x, place.zh, lax.axis_size("x")
    expected = len(partners)
    if conv:
        partners += [{"x": lax.rem(x + 1, x_size)}, {"x": lax.rem(x + x_size - 1, x_size)}]
        at_turn = jnp.logical_or(
            jnp.logical_and(x == x_size - 1, zh == 0), jnp.logical_and(x == 0, zh == 1)
        )
        across = {"x": jnp.where(x == 0, x_size - 1, 0), "zh": 1 - zh}

        @pl.when(at_turn)
        def _():
            pl.semaphore_signal(barrier, inc=1, device_id=across, device_id_type=MESH)

        expected = len(partners) + jnp.where(at_turn, 1, 0)
    for partner in partners:
        pl.semaphore_signal(barrier, inc=1, device_id=partner, device_id_type=MESH)
    pl.semaphore_wait(barrier, expected)

    def sends(src, at, device):
        return [push(src.at[at, rows] if src is whole else src.at[rows], whole.at[at, rows], device) for rows in halves]

    from_z, from_y, own_to_core = sends(mine, own, to_z), sends(mine, own, to_y), sends(mine, own, to_sibling)
    from_corner = sends(whole, beside_z, to_y)
    z_to_core, y_to_core, corner_to_core = (sends(whole, at, to_sibling) for at in (beside_z, beside_y, corner))
    own_place = place.copy(mine, whole.at[own])
    own_place.start()
    for h in range(HALVES):
        for copies in (from_z, from_y, own_to_core):
            copies[h].start()

    gather_list = [Gather(place, *group) for group in zip(mine_refs, whole_outs)]
    reduce_list = [Reduce(place, *group) for group in zip(total_refs, total_outs, scratch)]
    for item in gather_list + reduce_list:
        item.start()
    steps = interleaved([item.steps() for item in gather_list + reduce_list])
    done = [0, len(steps)]

    def steps_until(share):
        while done[0] < int(share * done[1]):
            steps[done[0]]()
            done[0] += 1

    def landed(copies):
        for copy in copies:
            copy.wait_recv()

    def pair(chip):
        return pl.ds(rank(*chip, 0) - place.core, 2)

    def rows_of(values):
        return values.reshape(2 * tokens, values.shape[-1])

    def blocks_of(values):
        return values.reshape(2, tokens, values.shape[-1])

    def conv_first(chip):
        at = pair(chip)

        def columns(j):
            buffer["joint"][at, :, tile(j)] = blocks_of(dot(rows_of(whole[at]), buffer["in_w"][:, tile(j)]))

        loop(2, columns)
        low = 2 * TILE
        buffer["joint"][at, :, low:] = blocks_of(dot(rows_of(whole[at]), buffer["in_w"][:, low:]))
        joint = buffer["joint"]
        here = pl.ds(HALO, tokens)
        buffer["carried"][at, here, :LANES] = joint[at, :, :LANES] * joint[at, :, 2 * LANES : 3 * LANES]
        buffer["carried"][at, here, LANES:] = joint[at, :, 3 * LANES : 4 * LANES] * joint[at, :, 4 * LANES :]

    def conv_second(chip, j):
        at = pair(chip)
        return dot(rows_of(buffer["gated"][at]), buffer["out_w"][:, tile(j)])

    def c_columns(b, lane):
        if lane == 0:
            return buffer["joint"][b, :, LANES : 2 * LANES]
        return swap_half(buffer["joint"][b, :, 3 * LANES : 4 * LANES])

    def conv_between():
        carried = buffer["carried"]
        halo = Halo(place, carried, pl.ds(tokens, HALO), pl.ds(0, HALO), True)
        halo.start()
        save("joint", buffer["joint"])
        save("whole", whole)
        halo.wait_recv()
        taps = ref["taps"]

        def block(b):
            keep_one, keep_two = ref["keep"][0, b], ref["keep"][1, b]
            for lane in (0, LANES):
                lanes = slice(lane, lane + LANES)
                mixed = (
                    taps[0:1, lanes] * carried[b, HALO - 2 : HALO - 2 + tokens, lanes] * keep_two
                    + taps[1:2, lanes] * carried[b, HALO - 1 : HALO - 1 + tokens, lanes] * keep_one
                    + taps[2:3, lanes] * carried[b, HALO : HALO + tokens, lanes]
                )
                buffer["mixed"][b, :, lanes] = mixed
                buffer["gated"][b, :, lanes] = (c_columns(b, lane) * mixed).astype(BF16)

        loop(8, block)
        halo.wait_send()
        for name in ("carried", "mixed", "gated"):
            save(name, buffer[name])

    def ffn_first(chip):
        at = pair(chip)
        main = buffer["gate_up"].shape[2] // (2 * LANES) * LANES

        def columns(j):
            gate = dot(rows_of(whole[at]), buffer["both_w"][:, tile(j)])
            up = dot(rows_of(whole[at]), buffer["both_w"][:, pl.ds(pl.multiple_of(main + j * TILE, TILE), TILE)])
            buffer["gate_up"][at, :, tile(j)] = blocks_of(gate)
            buffer["gate_up"][at, :, pl.ds(pl.multiple_of(main + j * TILE, TILE), TILE)] = blocks_of(up)
            buffer["hidden"][at, :, tile(j)] = blocks_of((gate * jax.nn.sigmoid(gate) * up).astype(BF16))

        loop(main // TILE, columns)
        both = dot(rows_of(whole[at]), buffer["both_w"][:, 2 * main :])
        buffer["gate_up"][at, :, 2 * main :] = blocks_of(both)
        lane = lax.broadcasted_iota(jnp.int32, both.shape, 1)
        hidden = jnp.where(lane < LANES // 2, both * jax.nn.sigmoid(both) * swap_half(both), 0.0)
        buffer["hidden"][at, :, main:] = blocks_of(hidden.astype(BF16))

    def ffn_second(chip, j):
        return dot(rows_of(buffer["hidden"][pair(chip)]), buffer["down_w"][:, tile(j)])

    def ffn_back_first(chip):
        at = pair(chip)
        main = buffer["gate_up"].shape[2] // (2 * LANES) * LANES

        def grads(grad_hidden, gate, up):
            sigmoid = jax.nn.sigmoid(gate)
            return grad_hidden * up * sigmoid * (1.0 + gate * (1.0 - sigmoid)), grad_hidden * gate * sigmoid

        def columns(j):
            ups = pl.ds(pl.multiple_of(main + j * TILE, TILE), TILE)
            grad_hidden = dot_cols(rows_of(whole[at]), buffer["down_w"][tile(j), :])
            gate, up = (rows_of(buffer["gate_up"][at, :, lanes]) for lanes in (tile(j), ups))
            grad_gate, grad_up = grads(grad_hidden, gate, up)
            buffer["grad_gate_up"][at, :, tile(j)] = blocks_of(grad_gate.astype(BF16))
            buffer["grad_gate_up"][at, :, ups] = blocks_of(grad_up.astype(BF16))

        loop(main // TILE, columns)
        grad_hidden = dot_cols(rows_of(whole[at]), buffer["down_w"][main:, :])
        both = rows_of(buffer["gate_up"][at, :, 2 * main :])
        grad_gate, grad_up = grads(grad_hidden, both, swap_half(both))
        buffer["grad_gate_up"][at, :, 2 * main :] = blocks_of((grad_gate + swap_half(grad_up)).astype(BF16))

    def ffn_back_second(chip, j):
        return dot_cols(rows_of(buffer["grad_gate_up"][pair(chip)]), buffer["both_w"][tile(j), :])

    def all_rows(values):
        return values.reshape(8 * tokens, values.shape[-1])

    def ffn_back_grads():
        def both_rows(j):
            left = all_rows(buffer["whole"][:, :, tile(j)])
            buffer["grad_both_w"][tile(j), :] = dot_rows(left, all_rows(buffer["grad_gate_up"][...])).astype(BF16)

        def down_rows(j):
            left = all_rows(buffer["hidden"][:, :, tile(j, LANES)])
            buffer["grad_down_w"][tile(j, LANES), :] = dot_rows(left, all_rows(whole[...])).astype(BF16)

        loop(features // TILE, both_rows)
        save("grad_both_w", buffer["grad_both_w"])
        loop(buffer["grad_down_w"].shape[0] // LANES, down_rows)
        save("grad_down_w", buffer["grad_down_w"].at[: saves["grad_down_w"].shape[0]])

    def conv_back_first(chip):
        at = pair(chip)
        buffer["grad_gated"][at] = blocks_of(dot_cols(rows_of(whole[at]), buffer["out_w"][...]))

    def conv_back_between():
        edges, carried, joint = buffer["edges"], buffer["carried"], buffer["joint"]
        taps = ref["taps"]
        grad_taps = ref["grad_taps"]
        grad_taps[...] = jnp.zeros_like(grad_taps)

        def block(b):
            keep_one, keep_two = ref["keep"][0, b], ref["keep"][1, b]
            for lane in (0, LANES):
                lanes = slice(lane, lane + LANES)
                grad_mixed = buffer["grad_gated"][b, :, lanes] * c_columns(b, lane)
                first_tap, second_tap = grad_mixed * keep_two, grad_mixed * keep_one
                edges[0, b, :tokens, lanes] = second_tap * taps[1:2, lanes]
                edges[1, b, :tokens, lanes] = first_tap * taps[0:1, lanes]
                buffer["grad_carried"][b, :, lanes] = grad_mixed * taps[2:3, lanes]
                for row, grad, back_by in ((0, first_tap, 2), (1, second_tap, 1), (2, grad_mixed, 0)):
                    tap_in = carried[b, HALO - back_by : HALO - back_by + tokens, lanes]
                    grad_taps[row : row + 1, lanes] += jnp.sum(grad * tap_in, axis=0, keepdims=True)

        loop(8, block)
        halo = Halo(place, edges, pl.ds(0, HALO), pl.ds(tokens, HALO), False)
        halo.start()
        halo.wait_recv()
        grad_joint = buffer["grad_joint"]

        def block_after(b):
            for lane in (0, LANES):
                lanes = slice(lane, lane + LANES)
                grad_carried = (
                    buffer["grad_carried"][b, :, lanes]
                    + edges[0, b, 1 : 1 + tokens, lanes]
                    + edges[1, b, 2 : 2 + tokens, lanes]
                )
                grad_c = buffer["grad_gated"][b, :, lanes] * buffer["mixed"][b, :, lanes]
                if lane == 0:
                    grad_joint[b, :, :LANES] = (grad_carried * joint[b, :, 2 * LANES : 3 * LANES]).astype(BF16)
                    grad_joint[b, :, LANES : 2 * LANES] = grad_c.astype(BF16)
                    grad_joint[b, :, 2 * LANES : 3 * LANES] = (grad_carried * joint[b, :, :LANES]).astype(BF16)
                else:
                    grad_b = grad_carried * joint[b, :, 4 * LANES :]
                    grad_joint[b, :, 3 * LANES : 4 * LANES] = (grad_b + swap_half(grad_c)).astype(BF16)
                    grad_joint[b, :, 4 * LANES :] = (grad_carried * joint[b, :, 3 * LANES : 4 * LANES]).astype(BF16)

        loop(8, block_after)
        halo.wait_send()

    def conv_back_second(chip, j):
        return dot_cols(rows_of(buffer["grad_joint"][pair(chip)]), buffer["in_w"][tile(j), :])

    def conv_back_grads():
        def in_rows(j):
            left = all_rows(buffer["whole"][:, :, tile(j)])
            buffer["grad_in_w"][tile(j), :] = dot_rows(left, all_rows(buffer["grad_joint"][...])).astype(BF16)

        def out_rows(j):
            left = all_rows(buffer["gated"][:, :, tile(j, LANES)])
            buffer["grad_out_w"][tile(j, LANES), :] = dot_rows(left, all_rows(whole[...])).astype(BF16)

        loop(features // TILE, in_rows)
        save("grad_in_w", buffer["grad_in_w"])
        loop(buffer["grad_out_w"].shape[0] // LANES, out_rows)
        save("grad_out_w", buffer["grad_out_w"].at[: saves["grad_out_w"].shape[0]])

    first = {"conv": conv_first, "ffn": ffn_first, "conv_back": conv_back_first, "ffn_back": ffn_back_first}[kind]
    second = {"conv": conv_second, "ffn": ffn_second, "conv_back": conv_back_second, "ffn_back": ffn_back_second}[kind]
    weight_names = ("in_w", "out_w") if conv else ("both_w", "down_w")

    own_place.wait()
    landed(own_to_core)
    loaded(*weight_names)
    if kind == "ffn_back":
        loaded("gate_up")
    first(chips[0])
    for h in range(HALVES):
        from_z[h].wait_recv()
        from_corner[h].start()
        z_to_core[h].start()
    for h in range(HALVES):
        from_y[h].wait_recv()
        y_to_core[h].start()
    landed(z_to_core)
    first(chips[1])
    landed(y_to_core)
    first(chips[2])
    steps_until(0.25)
    for h in range(HALVES):
        from_corner[h].wait_recv()
        corner_to_core[h].start()
    landed(corner_to_core)
    first(chips[3])
    if kind == "conv":
        conv_between()
    if kind == "conv_back":
        loaded("joint", "carried", "mixed")
        conv_back_between()
    if kind == "ffn":
        save("whole", whole)
        save("gate_up", buffer["gate_up"])
        save("hidden", buffer["hidden"])

    order = (chips[3], chips[2], chips[1], chips[0])
    sib_copies = [push(part.at[i, 1 - place.core], sib.at[i], to_sibling) for i in range(4)]
    y_copies = [[push(yout.at[i, rows], yin.at[i, rows], to_y) for rows in halves] for i in range(2)]
    z_copies = [push(zout.at[rows], zin.at[rows], to_z) for rows in halves]

    def multiply(i):
        def columns(j):
            part[i, :, :, tile(j)] = blocks_of(second(order[i], j).astype(BF16))

        loop(features // TILE, columns)
        sib_copies[i].start()

    def chip_sum(i, rows):
        return part[i, place.core, rows].astype(F32) + sib[i, rows].astype(F32)

    def to_y_side(i):
        sib_copies[i].wait_recv()
        for h, rows in enumerate(halves):
            yout[i, rows] = chip_sum(i, rows).astype(BF16)
            y_copies[i][h].start()

    multiply(0)
    multiply(1)
    to_y_side(0)
    multiply(2)
    to_y_side(1)
    multiply(3)
    steps_until(0.5)
    sib_copies[2].wait_recv()
    for h, rows in enumerate(halves):
        y_copies[0][h].wait_recv()
        zout[rows] = (chip_sum(2, rows) + yin[0, rows].astype(F32)).astype(BF16)
        z_copies[h].start()
    if kind == "ffn_back":
        loaded("whole", "hidden")
        ffn_back_grads()
    if kind == "conv_back":
        loaded("whole", "gated")
        conv_back_grads()
    steps_until(0.75)
    sib_copies[3].wait_recv()
    for h, rows in enumerate(halves):
        y_copies[1][h].wait_recv()
        z_copies[h].wait_recv()
        total = chip_sum(3, rows) + yin[1, rows].astype(F32) + zin[rows].astype(F32)
        stream = ref["stream"][rows]
        if not back:
            stream = stream + total
            ref["stream_next"][rows] = stream
            ref["next"][rows] = (stream * rms_scale(stream) * ref["gain"][...]).astype(BF16)
        else:
            scale = rms_scale(stream)
            gain_grad = jnp.sum(total * stream * scale, axis=0, keepdims=True)
            ref["gain_grad"][...] = gain_grad if h == 0 else ref["gain_grad"][...] + gain_grad
            scaled = total * ref["gain"][...]
            grad = (
                ref["grad"][rows]
                + scale * scaled
                - stream * (scale * scale * scale) * jnp.mean(scaled * stream, axis=-1, keepdims=True)
            )
            ref["grad_next"][rows] = grad
            ref["next"][rows] = grad.astype(BF16)
    steps_until(1)
    for item in gather_list + reduce_list:
        item.finish()
    for copy in saving:
        copy.wait()
    for copy in place.sent:
        copy.wait_send()


def phase(kind, own_in, group_in, use="", mine=(), totals=(), groups=()):
    tokens, features = own_in[0].shape
    inside = pl.BlockSpec(memory_space=pltpu.VMEM)
    anywhere = pl.BlockSpec(memory_space=pl.ANY)
    conv = kind in ("conv", "conv_back")
    names = dict(zip(GROUP_IN[kind], group_in))
    wide, tall = (names["in_w"], names["out_w"]) if conv else (names["both_w"], names["down_w"])
    columns, rows = wide.shape[1], tall.shape[0]
    rows_padded = -(-rows // LANES) * LANES
    block = (tokens, features)
    forms = {
        "in_w": (wide.shape, BF16),
        "both_w": (wide.shape, BF16),
        "out_w": ((rows_padded, features), BF16),
        "down_w": ((rows_padded, features), BF16),
        "whole": ((8,) + block, BF16),
        "joint": ((8, tokens, columns), F32),
        "gate_up": ((8, tokens, columns), F32),
        "carried": ((8, tokens + HALO, rows_padded), F32),
        "mixed": ((8, tokens, rows_padded), F32),
        "gated": ((8, tokens, rows_padded), BF16),
        "hidden": ((8, tokens, rows_padded), BF16),
        "stream_next": (block, F32),
        "grad_next": (block, F32),
        "next": (block, BF16),
        "gain_grad": ((1, features), F32),
        "grad_taps": ((HALO, rows_padded), F32),
        "grad_in_w": (wide.shape, BF16),
        "grad_both_w": (wide.shape, BF16),
        "grad_out_w": ((rows_padded, features), BF16),
        "grad_down_w": ((rows_padded, features), BF16),
        "grad_gated": ((8, tokens, rows_padded), F32),
        "grad_carried": ((8, tokens, rows_padded), F32),
        "edges": ((2, 8, tokens + HALO, rows_padded), F32),
        "grad_joint": ((8, tokens, columns), BF16),
        "grad_gate_up": ((8, tokens, columns), BF16),
    }
    buffers = {
        "conv": ("in_w", "out_w", "joint", "carried", "mixed", "gated"),
        "ffn": ("both_w", "down_w", "gate_up", "hidden"),
        "conv_back": GROUP_IN[kind] + ("grad_gated", "grad_carried", "edges", "grad_joint", "grad_in_w", "grad_out_w"),
        "ffn_back": GROUP_IN[kind] + ("grad_gate_up", "grad_both_w", "grad_down_w"),
    }[kind]
    reduced, reduce_scratch = reduce_shapes(totals, groups)
    outs = [(jax.ShapeDtypeStruct(*forms[name]), inside) for name in OWN_OUT[kind]]
    for name in GROUP_OUT[kind]:
        shape, dtype = forms[name]
        if name in ("grad_out_w", "grad_down_w"):
            shape = tall.shape
        outs.append((jax.ShapeDtypeStruct(shape, dtype), anywhere))
    outs += [(jax.ShapeDtypeStruct(whole_shape(array.shape), BF16), anywhere) for array in mine]
    outs += [(shape, inside) for shape in reduced]
    plan = {"mine": len(mine), "groups": groups, "buffers": buffers}
    name = kind + use
    return pl.pallas_call(
        functools.partial(phase_kernel, kind, plan),
        out_shape=[shape for shape, _ in outs],
        in_specs=[inside] * len(own_in) + [anywhere] * (len(group_in) + len(mine) + len(totals)),
        out_specs=[spec for _, spec in outs],
        scratch_shapes=[pltpu.VMEM(*forms[buffer]) for buffer in buffers]
        + [pltpu.VMEM((8,) + block, BF16), pltpu.VMEM((4, 2) + block, BF16), pltpu.VMEM((4,) + block, BF16)]
        + [pltpu.VMEM((2,) + block, BF16)] * 2
        + [pltpu.VMEM(block, BF16)] * 2
        + reduce_scratch
        + [pltpu.SemaphoreType.DMA((SEMAPHORES,))] * 3,
        compiler_params=pltpu.CompilerParams(
            collective_id=COLLECTIVE_ID[name], has_side_effects=True, vmem_limit_bytes=60 << 20
        ),
        name=name,
    )(*own_in, *group_in, *mine, *totals)


def sizes_of(axes):
    return tuple(lax.axis_size(axis) for axis in axes)


def split_owners(array, dim):
    owners = sizes_of(OWNERS)
    count = 1
    for size in owners:
        count *= size
    shape = array.shape
    return array.reshape(shape[:dim] + owners + (shape[dim] // count,) + shape[dim + 1 :])


def column_shards(weights):
    rows = weights[0].shape[0]
    mains, rests = [], []
    for weight in weights:
        parts = split_owners(weight, 1).transpose(5, 2, 3, 0, 1, 4, 6, 7).reshape(8, rows, -1)
        main = parts.shape[2] // LANES * LANES
        mains.append(parts[:, :, :main])
        rests.append(parts[:, :, main:])
    shards = jnp.concatenate(mains + rests, axis=2)
    return jnp.pad(shards, ((0, 0), (0, 0), (0, -shards.shape[2] % LANES)))


def column_whole(shards, groups, width):
    rows = shards.shape[1]
    yh, yl, core, zh, zl, x = sizes_of(OWNERS)
    wholes = []
    for group in range(groups):
        part = jnp.concatenate(
            [shards[..., a:b] for a, b in pieces_of(groups, width, group, 0, width)], axis=-1
        ).reshape(zl, yl, core, rows, yh, zh, x, -1)
        wholes.append(part.transpose(3, 4, 1, 2, 5, 0, 6, 7).reshape(rows, -1))
    return wholes


def gather_columns(shards):
    mine = lax.all_to_all(shards, TP, split_axis=0, concat_axis=0, tiled=True)
    whole = lax.all_gather(mine, DP, axis=0, tiled=False)
    yh, yl, core, zh, zl, x = sizes_of(OWNERS)
    rows, columns = shards.shape[1:]
    whole = whole.reshape(yh, zh, x, zl, yl, core, rows, columns)
    return whole.transpose(0, 4, 5, 1, 3, 2, 6, 7).reshape(-1, columns)


def scatter_columns(total):
    yh, yl, core, zh, zl, x = sizes_of(OWNERS)
    columns = total.shape[1]
    parts = split_owners(total, 0).transpose(0, 3, 5, 4, 1, 2, 6, 7)
    parts = parts.reshape(yh * zh * x, -1, columns)
    mine = lax.psum_scatter(parts, DP, scatter_dimension=0, tiled=False)
    mine = mine.reshape(8, -1, columns)
    return lax.all_to_all(mine, TP, split_axis=0, concat_axis=0, tiled=True)


def tap_masks(starts, token_count):
    zh, x, x_size = lax.axis_index("zh"), lax.axis_index("x"), lax.axis_size("x")
    blocks = (zh * 2 + jnp.arange(2, dtype=jnp.int32)) * x_size + x
    places = blocks[:, None] * token_count + jnp.arange(token_count, dtype=jnp.int32)

    def segment_of(where):
        return jnp.sum((starts[None, :, None, :] <= where[:, None, :, None]).astype(jnp.int32), axis=3)

    own_segment = segment_of(places)
    keep_one = (segment_of(places - 1) == own_segment).astype(F32)
    keep_two = (segment_of(places - 2) == own_segment).astype(F32)
    return keep_one.reshape(8, token_count, 1), keep_two.reshape(8, token_count, 1)


def local(stream_in, doc_starts, norm_mix, in_proj, conv_taps, out_proj, norm_ffn, w_gate, w_up, w_down, grad_out):
    _, token_count, features = stream_in.shape
    layers = norm_mix.shape[0]
    own_kernels = sizes_of(DP) == (1, 2, 2)
    stream = stream_in.reshape(-1, features)
    grad_stream = grad_out.reshape(-1, features)
    small = jnp.concatenate([norm_mix[:, None], norm_ffn[:, None], conv_taps.transpose(0, 2, 1)], axis=1)
    small = small.astype(BF16).astype(F32)
    owned = small.shape[2]
    in_w, both_w, out_w, down_w = ([None] * layers for _ in range(4))

    def rows_of(weight):
        return weight.reshape(-1, weight.shape[-1])

    if own_kernels:
        packed = jnp.zeros((16, LANES), F32).at[: 5 * layers, :owned].set(small.reshape(-1, owned))
        packed = packed.at[15, : doc_starts.shape[1]].set(doc_starts[0].astype(F32))
        spread, mine, rounded, wholes = prepare(packed, in_proj, w_gate, w_up, out_proj, w_down)
        in_w[0], out_w[0], down_w[0] = (rows_of(whole) for whole in wholes)
        params = spread[:, : 5 * layers, :owned].transpose(1, 0, 2)
        gains = params.reshape(layers, 5, 1, -1)[:, :2]
        params = params.reshape(layers, 5, 4, 2, 2, 2, owned)[:, 2:]
        others = lax.axis_index("yl") * 2 + lax.axis_index("core")
        params = lax.dynamic_index_in_dim(params, others, 2, False)
        taps_all = lax.dynamic_index_in_dim(params, lax.axis_index("zl"), 3, False).reshape(layers, 3, -1)
        starts = spread.reshape(4, 8, 16, LANES)[:, 0, 15, : doc_starts.shape[1]].astype(jnp.int32)
    else:
        starts = lax.all_gather(doc_starts, ("yl", "core"), axis=0, tiled=True)
        small = small.astype(BF16)
        gains = lax.all_gather(small[:, :2], OWNERS, axis=2, tiled=True).astype(F32)[:, :, None]
        taps_all = lax.all_gather(small[:, 2:], DP, axis=2, tiled=True).astype(F32)
        for layer in range(layers):
            in_w[layer] = gather_columns(column_shards(jnp.split(in_proj[layer].astype(BF16), 3, axis=1)))
            both_w[layer] = gather_columns(column_shards([w_gate[layer].astype(BF16), w_up[layer].astype(BF16)]))
            out_w[layer] = lax.all_gather(out_proj[layer].astype(BF16), DP, axis=0, tiled=True)
            down_w[layer] = lax.all_gather(w_down[layer].astype(BF16), DP, axis=0, tiled=True)
    channels = taps_all.shape[2]
    taps_all = jnp.pad(taps_all, ((0, 0), (0, HALO - 3), (0, -channels % LANES)))
    keep = jnp.stack(tap_masks(starts, token_count))

    saved = []
    normed = (stream * rms_scale(stream) * gains[0, 0]).astype(BF16)
    for layer in range(layers):
        moved = (mine[2 * layer + 1],) if own_kernels else ()
        middle, normed, *kept, = phase(
            "conv", (normed, stream, gains[layer, 1], taps_all[layer], keep), (in_w[layer], out_w[layer]), mine=moved
        )
        if own_kernels:
            both_w[layer] = rows_of(kept.pop())
        if layer + 1 < layers and own_kernels:
            moved, use = (mine[2 * layer + 2], rounded[2 * layer + 2], rounded[2 * layer + 3]), "_moving"
        else:
            moved, use = (), ""
        gain = gains[min(layer + 1, layers - 1), 0]
        after, normed, *kept_ffn = phase("ffn", (normed, middle, gain), (both_w[layer], down_w[layer]), use, mine=moved)
        if moved:
            in_w[layer + 1], out_w[layer + 1], down_w[layer + 1] = (rows_of(whole) for whole in kept_ffn[3:])
        saved.append((stream, middle, kept, kept_ffn[:3]))
        stream = after

    def by_owner(grad):
        return grad.reshape(4, 2, 2, 2, -1, grad.shape[1])

    def by_part(grad):
        return grad.reshape(2, 2, -1, grad.shape[1])

    pieces = [None] * layers
    waiting, groups = (), ()
    sums = [[] for _ in range(layers)]
    rounded_grad = grad_stream.astype(BF16)
    for layer in reversed(range(layers)):
        source, middle, kept, kept_ffn = saved[layer]
        grad_middle, grad_gain_ffn, rounded_grad, grad_both, grad_down, *results = phase(
            "ffn_back", (rounded_grad, grad_stream, middle, gains[layer, 1]), (both_w[layer], down_w[layer], *kept_ffn),
            "_moving" if waiting else "", totals=waiting, groups=groups,
        )
        if waiting:
            sums[layer + 1] += results
        waiting, groups = ((by_owner(grad_both),), (2,)) if own_kernels else ((), ())
        grad_stream, grad_gain_mix, rounded_grad, grad_taps, grad_in, grad_out, *results = phase(
            "conv_back", (rounded_grad, grad_middle, source, gains[layer, 0], taps_all[layer], keep),
            (in_w[layer], out_w[layer], *kept), totals=waiting, groups=groups,
        )
        if own_kernels:
            sums[layer] += results
            waiting, groups = (by_owner(grad_in), by_part(grad_out), by_part(grad_down)), (3, 1, 1)
        else:
            sums[layer] = column_whole(scatter_columns(grad_both).astype(F32), 2, down_w[layer].shape[0])
            sums[layer] += column_whole(scatter_columns(grad_in).astype(F32), 3, out_w[layer].shape[0])
            sums[layer] += [
                lax.psum_scatter(grad, DP, scatter_dimension=0, tiled=True).astype(F32) for grad in (grad_out, grad_down)
            ]
        pieces[layer] = (grad_gain_mix, grad_gain_ffn, grad_taps[:3, :channels])
    gain_grads = jnp.stack([jnp.concatenate(p[:2]) for p in pieces])
    tap_grads = jnp.stack([p[2] for p in pieces])
    if own_kernels:
        slabs = gain_grads.reshape(2 * layers, 32, owned).transpose(1, 0, 2)
        slabs = jnp.pad(slabs, ((0, 0), (0, 0), (0, LANES - owned)))
        taps = tap_grads.reshape(3 * layers, 2, 1, 2, owned).transpose(1, 2, 3, 0, 4)
        taps = jnp.pad(taps, ((0, 0), (0, 0), (0, 0), (0, 0), (0, LANES - owned)))
        same = (jnp.arange(4) == others)[:, None, None, None, None, None]
        same = same & (jnp.arange(2) == lax.axis_index("zl"))[None, None, :, None, None, None]
        taps = jnp.where(same, taps[None], 0.0).reshape(32, 3 * layers, LANES)
        slabs = jnp.concatenate([slabs, taps, jnp.zeros((32, 16 - 5 * layers, LANES), F32)], axis=1)
        small_sums, *results = finish(slabs, waiting, groups)
        sums[0] += results
        small_sums = small_sums[:, :owned]
        gain_grads = small_sums[: 2 * layers].reshape(layers, 2, owned)
        tap_grads = small_sums[2 * layers : 5 * layers].reshape(layers, 3, owned)
    else:
        gain_grads = lax.psum_scatter(gain_grads, OWNERS, scatter_dimension=2, tiled=True)
        gain_grads = gain_grads.reshape(layers, 2, -1)
        tap_grads = lax.psum_scatter(tap_grads, DP, scatter_dimension=2, tiled=True)
    return (
        stream[None],
        grad_stream[None],
        gain_grads[:, 0],
        jnp.stack([jnp.concatenate(s[2:5], axis=1) for s in sums]),
        tap_grads.transpose(0, 2, 1),
        jnp.stack([s[5] for s in sums]),
        gain_grads[:, 1],
        jnp.stack([s[0] for s in sums]),
        jnp.stack([s[1] for s in sums]),
        jnp.stack([s[6] for s in sums]),
    )


def solution(mesh):
    dp, seq = mesh.shape["dp"], mesh.shape["seq"]
    side = dp // 2
    split = Mesh(mesh.devices.reshape(side // 2, 2, 2, seq // side // 2, 2, side), OWNERS)
    token = P(ROW_AXES, SEQ_AXES, None)
    vector = P(None, OWNERS)
    matrix = P(None, OWNERS, None)
    return jax.shard_map(
        local,
        mesh=split,
        in_specs=(token, P(ROW_AXES, None), vector, matrix, matrix, matrix, vector, matrix, matrix, matrix, token),
        out_specs=(token, token, vector, matrix, matrix, matrix, vector, matrix, matrix, matrix),
        check_vma=False,
    )
```

time: 970 us -> 804 us (0.83)
  matrix products: 118 us -> 0 us
  local copies, waits for them, and re-layouts: 103 us -> 14.4 us
  Pallas kernels: 698 us -> 770 us
  other arithmetic: 30.7 us -> 12.5 us
    dot_general x24 -> x0, matrix products: 118 us -> none  [the longest x8 42.4 us: outer_cols(): lax.dot_general(left, right, (((1,), (1,)), ((), ())), preferred_element_...]
    pallas_call x1, Pallas kernels: 18.4 us -> 78.6 us  [prepare(): pl.pallas_call(functools.partial(prepare_kernel, layers), out_shape=[jax....]
    concatenate x12 -> x0, local copies, waits for them, and re-layouts: 25.4 us -> none  [group_columns(): jnp.concatenate([g[..., :main] for g in groups] + [g[..., main:] for g in...]
    slice x33 -> x2, local copies, waits for them, and re-layouts: 19.3 us -> 0.01 us  [the longest x1 0.01 us: local(): tap_grads = small_sums[2 * layers:5 * layers].reshape(layers, 3, owned)]
    unnamed x289 -> x55, local copies, waits for them, and re-layouts: 29.4 us -> 10.6 us
    pallas_call x10 -> x9, Pallas kernels: 680 us -> 691 us  [the longest x8 606 us: phase(): pl.pallas_call(functools.partial(phase_kernel, kind, plan), out_shape=[sh...]
  transfers between devices with their start and end apart: 8 -> 0, of which waited for: 1 -> 0; matrix products, arithmetic and copies ran while one was open for 2% -> 0% of each run, Pallas kernels for 0% -> 0%
where the time goes in v4:
time: 804 us; the launch traced here: 798 us
  Pallas kernels  770 us (96%)
  local copies, waits for them, and re-layouts  14.4 us (2%)
  other arithmetic  12.5 us (2%)
    pallas_call x8, Pallas kernels, phase(): pl.pallas_call(functools.partial(phase_kernel, kind, plan), out_shape=[sh...  606 us
    pallas_call x1, Pallas kernels, finish(): pl.pallas_call(functools.partial(finish_kernel, groups), out_shape=[jax.S...  84.9 us
    pallas_call x1, Pallas kernels, prepare(): pl.pallas_call(functools.partial(prepare_kernel, layers), out_shape=[jax....  78.6 us

profile of v4, /device:TPU:0, one launch (start us, length us, event | category | flops | bytes accessed | tf_op | source)
XLA Modules:
  0.0 798.0 jit_solution(1359174094937177458)
XLA Ops:
  0.6 0.7 convert_bitcast_fusion.1
  1.3 0.7 convert_bitcast_fusion.2
  2.1 0.7 convert_element_type.66
  2.8 1.1 copy-done.4
  3.9 78.6 %prepare.1 = (f32[32,16,128]{2,1,0:T(8,128)S(1)}, bf16[4,2,48,640]{3,2,1,0:T(8,128)(2,1)}, bf16[4,2,48,1152]{3,2,1,0:T(8,128)(2,1)S(1)}, bf16[4,2,48,640]{3,2,1,...) custom-call(f32[16,128]{1,0:T(8,128)S(1)} %scatter.14.small, ...), custom_call_target="tpu_custom_call" | custom-call | tf_op jit(solution)/shard_map/prepare/pallas_call | solution.py:243
  82.5 0.8 copy-done
  83.3 0.9 copy-done.2
  84.2 0.9 copy-done.3
  85.1 0.8 copy-done.6
  85.9 0.8 copy-done.7
  86.7 0.6 copy-done.8
  87.4 0.1 reshape.337
  87.5 0.6 slice_bitcast_fusion.6
  88.2 0.3 copy-done.9
  88.4 0.1 multiply_reduce_fusion
  88.6 0.9 multiply_convert_fusion.refs_0_
  89.6 0.6 fusion.2
  90.3 0.1 convert_reduce_fusion.2
  90.4 0.5 copy.59
  90.9 1.1 stack.69.refs_4_.refs_5_
  92.0 72.1 %conv.2 = (f32[128,1536]{1,0:T(8,128)}, bf16[128,1536]{1,0:T(8,128)(2,1)}, bf16[8,128,1536]{2,1,0:T(8,128)(2,1)}, f32[8,128,640]{2,1,0:T(8,128)}, f32[8,136,256]...) custom-call(bf16[128,1536]{1,0:T(8,128)(2,1)} %multiply_convert_fusi, ...), custom_call_target="tpu_custom_call" | custom-call | tf_op jit(solution)/shard_map/conv/pallas_call | solution.py:977
  164.1 82.4 %ffn_moving.1 = (f32[128,1536]{1,0:T(8,128)}, bf16[128,1536]{1,0:T(8,128)(2,1)}, bf16[8,128,1536]{2,1,0:T(8,128)(2,1)}, f32[8,128,1152]{2,1,0:T(8,128)}, bf16[8,...) custom-call(bf16[128,1536]{1,0:T(8,128)(2,1)} %get-tuple-element.111, ...), custom_call_target="tpu_custom_call" | custom-call | tf_op jit(solution)/shard_map/ffn_moving/pallas_call | solution.py:977
  246.5 76.4 %conv.3 = (f32[128,1536]{1,0:T(8,128)}, bf16[128,1536]{1,0:T(8,128)(2,1)}, bf16[8,128,1536]{2,1,0:T(8,128)(2,1)}, f32[8,128,640]{2,1,0:T(8,128)}, f32[8,136,256]...) custom-call(bf16[128,1536]{1,0:T(8,128)(2,1)} %get-tuple-element.118, ...), custom_call_target="tpu_custom_call" | custom-call | tf_op jit(solution)/shard_map/conv/pallas_call | solution.py:977
  322.9 52.8 %ffn.1 = (f32[128,1536]{1,0:T(8,128)}, bf16[128,1536]{1,0:T(8,128)(2,1)}, bf16[8,128,1536]{2,1,0:T(8,128)(2,1)}, f32[8,128,1152]{2,1,0:T(8,128)}, bf16[8,128,640]{2,1,0:T(8,128)(2,1)}) custom-call(bf16[128,1536]{1,0:T(8,128)(2,1)} %get-tuple-element.123.refs_0_, f32[128,1536]{1,0:T(8,128)} %get-tuple-element.124.refs_1_.refs_2_, ...), custom_call_target="tpu_custom_call" | custom-call | tf_op jit(solution)/shard_map/ffn/pallas_call | solution.py:977
  375.7 0.8 bitcast_convert_fusion.refs_0_
  376.5 52.0 %ffn_back.1 = (f32[128,1536]{1,0:T(8,128)}, f32[1,1536]{1,0:T(1,128)}, bf16[128,1536]{1,0:T(8,128)(2,1)}, bf16[1536,1152]{1,0:T(8,128)(2,1)}, bf16[576,1536]{1,0:T(8,128)(2,1)}) custom-call(bf16[128,1536]{1,0:T(8,128)(2,1)} %bitcast_convert_fusion.refs_0_, f32[128,1536]{1,0:T(8,128)} %bitcast.114, f32[128,1536]{1,0:T(8,128)} %get-tuple-element.124.refs_1_.refs_2_, ...), custom_call_target="tpu_custom_call" | custom-call | tf_op jit(solution)/shard_map/ffn_back/pallas_call | solution.py:977
  428.5 93.5 %conv_back.2 = (f32[128,1536]{1,0:T(8,128)}, f32[1,1536]{1,0:T(1,128)}, bf16[128,1536]{1,0:T(8,128)(2,1)}, f32[8,256]{1,0:T(8,128)}, bf16[1536,640]{1,0:T(8,128)...) custom-call(bf16[128,1536]{1,0:T(8,128)(2,1)} %get-tuple-element.131.refs_0_, ...), custom_call_target="tpu_custom_call" | custom-call | tf_op jit(solution)/shard_map/conv_back/pallas_call | solution.py:977
  522.0 81.9 %ffn_back_moving.1 = (f32[128,1536]{1,0:T(8,128)}, f32[1,1536]{1,0:T(1,128)}, bf16[128,1536]{1,0:T(8,128)(2,1)}, bf16[1536,1152]{1,0:T(8,128)(2,1)}, bf16[576,15...) custom-call(bf16[128,1536]{1,0:T(8,128)(2,1)} %get-tuple-element.139, ...), custom_call_target="tpu_custom_call" | custom-call | tf_op jit(solution)/shard_map/ffn_back_moving/pallas_call | solution.py:977
  604.0 95.4 %conv_back.3 = (f32[128,1536]{1,0:T(8,128)}, f32[1,1536]{1,0:T(1,128)}, bf16[128,1536]{1,0:T(8,128)(2,1)}, f32[8,256]{1,0:T(8,128)}, bf16[1536,640]{1,0:T(8,128)...) custom-call(bf16[128,1536]{1,0:T(8,128)(2,1)} %get-tuple-element.147.refs_0_, ...), custom_call_target="tpu_custom_call" | custom-call | tf_op jit(solution)/shard_map/conv_back/pallas_call | solution.py:977
  699.4 0.7 maximum_bitcast_fusion.2
  700.1 0.1 reshape.355
  700.3 0.7 slice_bitcast_fusion.5
  701.3 0.1 broadcast_in_dim.61
  701.4 0.1 bitcast_select_fusion
  701.6 1.1 copy-done.5
  702.7 84.9 %finish.1 = (f32[16,128]{1,0:T(8,128)S(1)}, f32[48,1536]{1,0:T(8,128)S(1)}, f32[48,1536]{1,0:T(8,128)S(1)}, f32[48,1536]{1,0:T(8,128)S(1)}, f32[48,1536]{1,0:T(8,128)S(1)}, /*index=5*/f32[144,1536]{1,0:T(8,128)S(1)}) custom-call(f32[32,16,128]{2,1,0:T(8,128)S(1)} %fusion.slabs, bf16[4,2,2,2,48,640]{5,4,3,2,1,0:T(8,128)(2,1)} %bitcast.117, ...), custom_call_target="tpu_custom_call" | custom-call | tf_op jit(solution)/shard_map/finish/pallas_call | solution.py:300
  787.6 0.6 fusion.6
  788.3 1.3 pad_maximum_fusion
  789.6 0.6 copy.64
  790.2 0.9 pad_maximum_fusion.4
  791.1 1.3 pad_maximum_fusion.1
  792.4 0.1 copy-done.11
  792.5 0.6 copy-done.14
  793.2 1.3 pad_maximum_fusion.2
  794.5 0.1 copy-done.13
  794.6 1.3 pad_maximum_fusion.3
  796.0 0.9 copy.74
  796.9 0.9 copy.75
  (76 shorter events, 1.1 us)
Async XLA Ops:
  2.8 1.1 copy-start.4
  82.5 0.8 copy-start
  83.3 0.9 copy-start.2
  84.2 0.9 copy-start.3
  85.1 0.8 copy-start.6
  85.9 0.8 copy-start.7
  86.7 0.6 copy-start.8
  87.3 1.1 copy-start.9
  322.9 52.8 %copy-start.10 = (f32[1,128,1536]{2,1,0:T(8,128)S(1)}, f32[1,128,1536]{2,1,0:T(8,128)}, u32[]{:S(2)}) copy-start(f32[1,128,1536]{2,1,0:T(8,128)} %param.25) | copy-start | bytes 2359300
  603.9 95.4 %copy-start.22 = (f32[1,1536]{1,0:T(1,128)S(1)}, f32[1,1536]{1,0:T(1,128)}, u32[]{:S(2)}) copy-start(f32[1,1536]{1,0:T(1,128)} %get-tuple-element.159) | copy-start | bytes 18436
  603.9 95.4 %copy-start.23 = (f32[1,1536]{1,0:T(1,128)S(1)}, f32[1,1536]{1,0:T(1,128)}, u32[]{:S(2)}) copy-start(f32[1,1536]{1,0:T(1,128)} %get-tuple-element.158) | copy-start | bytes 18436
  603.9 95.4 %copy-start.24 = (f32[1,1536]{1,0:T(1,128)S(1)}, f32[1,1536]{1,0:T(1,128)}, u32[]{:S(2)}) copy-start(f32[1,1536]{1,0:T(1,128)} %get-tuple-element.157) | copy-start | bytes 18436
  603.9 96.3 %copy-start.25 = (f32[8,256]{1,0:T(8,128)S(1)}, f32[8,256]{1,0:T(8,128)}, u32[]{:S(2)}) copy-start(f32[8,256]{1,0:T(8,128)} %get-tuple-element.161) | copy-start | bytes 24580
  604.0 97.6 %copy-start.1 = (bf16[576,1536]{1,0:T(8,128)(2,1)S(1)}, bf16[576,1536]{1,0:T(8,128)(2,1)}, u32[]{:S(2)}) copy-start(bf16[576,1536]{1,0:T(8,128)(2,1)} %get-tuple-element.164) | copy-start | bytes 5308420
  701.6 1.1 copy-start.5
  702.7 85.5 %copy-start.18 = (f32[48,1536]{1,0:T(8,128)S(1)}, f32[48,1536]{1,0:T(8,128)}, u32[]{:S(2)}) copy-start(f32[48,1536]{1,0:T(8,128)} %get-tuple-element.169) | copy-start | bytes 884740
  702.7 85.5 %copy-start.19 = (f32[48,1536]{1,0:T(8,128)S(1)}, f32[48,1536]{1,0:T(8,128)}, u32[]{:S(2)}) copy-start(f32[48,1536]{1,0:T(8,128)} %get-tuple-element.170) | copy-start | bytes 884740
  702.7 85.5 %copy-start.20 = (f32[48,1536]{1,0:T(8,128)S(1)}, f32[48,1536]{1,0:T(8,128)}, u32[]{:S(2)}) copy-start(f32[48,1536]{1,0:T(8,128)} %get-tuple-element.171) | copy-start | bytes 884740
  788.3 2.0 copy-start.21
  788.3 2.8 copy-start.12
  789.6 1.5 copy-start.15
  791.1 1.5 copy-start.11
  791.1 2.1 copy-start.14
  793.2 1.5 copy-start.13
  794.6 1.4 copy-start.16
  794.6 2.3 copy-start.17

commit v5 on v1

v5 whole, which is shorter than its diff:
```python
import functools
import itertools

import jax
import jax.numpy as jnp
from jax import lax
from jax.experimental import pallas as pl
from jax.experimental.pallas import tpu as pltpu
from jax.sharding import Mesh, PartitionSpec as P

EPSILON = 1e-05
TP = ("zl", "yl", "core")
DP = ("yh", "zh", "x")
ROW_AXES = ("yh", "yl", "core")
SEQ_AXES = ("zh", "zl", "x")
OWNERS = ROW_AXES + SEQ_AXES
BF16 = jnp.bfloat16
F32 = jnp.float32
MESH = pl.DeviceIdType.MESH
HALVES = 2
COLLECTIVE_ID = {"prepare": 0, "forward": 1, "backward": 2}
FLIPS = ((1, 1, 1), (1, 1, 0), (1, 0, 1), (1, 0, 0), (0, 1, 1), (0, 1, 0), (0, 0, 1))
OTHERS = tuple(itertools.product((0, 1), repeat=5))[1:]
OTHER_AXES = ("yl", "core", "zh", "zl", "x")
SEMAPHORES = 288
FLYING = 2
LANES = 128
TILE = 256
HALO = 8


def rms_scale(values):
    return lax.rsqrt(jnp.mean(values * values, axis=-1, keepdims=True) + EPSILON)


class Place:
    def __init__(self, send, recv, local):
        self.zl, self.yl, self.core = (lax.axis_index(axis) for axis in TP)
        self.zh, self.x = lax.axis_index("zh"), lax.axis_index("x")
        self.send, self.recv, self.local = send, recv, local
        self.remote_count = self.local_count = 0
        self.sent = []

    def rank(self, flip_z, flip_y, flip_core):
        return self.flipped("zl", flip_z) * 4 + self.flipped("yl", flip_y) * 2 + self.flipped("core", flip_core)

    def flipped(self, axis, flip):
        return 1 - getattr(self, axis) if flip else getattr(self, axis)

    def member(self, flips):
        return {axis: 1 - getattr(self, axis) for axis, flip in zip(TP, flips) if flip}

    def beside(self, axis):
        return {axis: 1 - getattr(self, axis)}

    def owner(self, flips=(0,) * 5):
        index = 0
        for axis, flip in zip(OTHER_AXES, flips):
            index = index * 2 + self.flipped(axis, flip)
        return index

    def push(self, src, dst, device, kept=True):
        index = self.remote_count
        self.remote_count += 1
        assert index < SEMAPHORES
        copy = pltpu.make_async_remote_copy(
            src_ref=src, dst_ref=dst, send_sem=self.send.at[index], recv_sem=self.recv.at[index],
            device_id=device, device_id_type=MESH,
        )
        if kept:
            self.sent.append(copy)
        return copy

    def copy(self, src, dst):
        index = self.local_count
        self.local_count += 1
        return pltpu.make_async_copy(src, dst, self.local.at[index])


def pieces_of(groups, width, group, low, high):
    main = width // LANES * LANES
    rest = width - main
    ranges = []
    if low < main:
        ranges.append((group * main + low, group * main + min(high, main)))
    if high > main:
        start = groups * main + group * rest - main
        ranges.append((start + max(low, main), start + high))
    return ranges


def shards_from(weights, out):
    width = weights[0].shape[1] // 8
    block = width // 4
    main = width // LANES * LANES
    rest = width - main
    for group, weight in enumerate(weights):
        for member in range(8):
            zl, others = member // 4, member % 4
            starts = [((others * 2 + zh) * 4 + zl * 2 + x) * block for zh in range(2) for x in range(2)]
            values = jnp.concatenate([weight[:, start : start + block] for start in starts], axis=1).astype(BF16)
            out[member, :, group * main : (group + 1) * main] = values[:, :main]
            if rest:
                low = len(weights) * main + group * rest
                out[member, :, low : low + rest] = values[:, main:]
    pad = out.shape[2] - len(weights) * width
    if pad:
        out[:, :, len(weights) * width :] = jnp.zeros((8, out.shape[1], pad), BF16)


def shards_to(shards, outs):
    groups, width = len(outs), outs[0].shape[1] // 8
    block = width // 4
    for group, out in enumerate(outs):
        for others in range(4):
            for zh in range(2):
                values = []
                for zl in range(2):
                    for x in range(2):
                        low = (zh * 2 + x) * block
                        for start, end in pieces_of(groups, width, group, low, low + block):
                            values.append(shards[zl * 4 + others, :, start:end].astype(F32))
                start = (others * 2 + zh) * 4 * block
                out[:, start : start + 4 * block] = jnp.concatenate(values, axis=1)


def every_other(place):
    return [
        ({axis: place.flipped(axis, 1) for axis, flip in zip(OTHER_AXES, flips) if flip}, flips) for flips in OTHERS
    ]


def prepare_kernel(layers, small, in_proj, gate, up, out_proj, down, *refs):
    refs = list(refs)

    def take(count):
        taken = refs[:count]
        del refs[:count]
        return taken

    (spread,), mine, rounded, wholes = take(1), take(2 * layers), take(2 * layers), take(2)
    shards, (send, recv, local) = take(2 * layers), take(3)
    place = Place(send, recv, local)
    barrier = pltpu.get_barrier_semaphore()
    for device, _ in every_other(place):
        pl.semaphore_signal(barrier, inc=1, device_id=device, device_id_type=MESH)
    width = in_proj.shape[2] // 3

    def cut(layer, which):
        if which == 0:
            shards_from([in_proj.at[layer, :, i * width : (i + 1) * width] for i in range(3)], shards[2 * layer])
        else:
            shards_from([gate.at[layer], up.at[layer]], shards[2 * layer + 1])

    def scatter(index):
        here = mine[index].at[place.yl * 2 + place.core, place.zl]
        copies = [place.push(shards[index].at[place.rank(*flips)], here, place.member(flips)) for flips in FLIPS]
        copies.append(place.copy(shards[index].at[place.rank(0, 0, 0)], here))
        for copy in copies:
            copy.start()
        return copies

    def landed(copies):
        for copy in copies[:-1]:
            copy.wait_recv()
        copies[-1].wait()

    cut(0, 0)
    for layer in range(layers):
        rounded[2 * layer][...] = out_proj[layer].astype(BF16)
        rounded[2 * layer + 1][...] = down[layer].astype(BF16)
    pl.semaphore_wait(barrier, len(OTHERS))
    kept = place.copy(small, spread.at[place.owner()])
    kept.start()
    spreads = [place.push(small, spread.at[place.owner()], device) for device, _ in every_other(place)]
    first = scatter(0)
    for copy in spreads:
        copy.start()
    gathers = [Gather(place, own, whole) for own, whole in zip((mine[0], rounded[0]), wholes)]
    for gather in gathers[1:]:
        for launch, _ in gather.pairs():
            launch()
    cut(0, 1)
    landed(first)
    for launch, _ in gathers[0].pairs():
        launch()
    others = [scatter(1)]
    for layer in range(1, layers):
        for which in range(2):
            cut(layer, which)
            others.append(scatter(2 * layer + which))
    for gather in gathers[1:] + gathers[:1]:
        for _, land in gather.pairs():
            land()
    for copies in others:
        landed(copies)
    kept.wait()
    for copy in spreads:
        copy.wait_recv()
    for gather in gathers:
        gather.finish()
    for copy in place.sent:
        copy.wait_send()


def whole_shape(mine):
    return (4, 2, 2, 2) + mine[2:] if len(mine) == 4 else (2, 2) + mine


def prepare(small, in_proj, gate, up, out_proj, down):
    layers, rows, columns = in_proj.shape
    widths = (-(-columns // 8 // LANES) * LANES, gate.shape[2] // 4)
    inside = pl.BlockSpec(memory_space=pltpu.VMEM)
    anywhere = pl.BlockSpec(memory_space=pl.ANY)
    mine = [(4, 2, rows, width) for _ in range(layers) for width in widths]
    rounded = [array.shape[1:] for _ in range(layers) for array in (out_proj, down)]
    wholes = [whole_shape(shape) for shape in (mine[0], rounded[0])]
    outs = pl.pallas_call(
        functools.partial(prepare_kernel, layers),
        out_shape=[jax.ShapeDtypeStruct((32,) + small.shape, F32)]
        + [jax.ShapeDtypeStruct(shape, BF16) for shape in mine + rounded + wholes],
        in_specs=[inside] * 6,
        out_specs=[anywhere] * (1 + len(mine)) + [inside] * len(rounded) + [anywhere] * 2,
        scratch_shapes=[pltpu.VMEM((8, rows, width), BF16) for _ in range(layers) for width in widths]
        + [pltpu.SemaphoreType.DMA((SEMAPHORES,))] * 3,
        compiler_params=pltpu.CompilerParams(
            collective_id=COLLECTIVE_ID["prepare"], has_side_effects=True, vmem_limit_bytes=48 << 20
        ),
        name="prepare",
    )(small, in_proj, gate, up, out_proj, down)
    spread, outs = outs[0], outs[1:]
    return spread, outs[: len(mine)], outs[len(mine) : -2], outs[-2:]


class Gather:
    def __init__(self, place, mine, whole):
        x, own, other = place.x, place.zh, 1 - place.zh
        if len(whole.shape) == 6:
            parts = [
                (mine.at[c, zl], whole.at[c, own, zl, x], whole.at[c, other, zl, x])
                for c in range(4)
                for zl in range(2)
            ]
        else:
            count = whole.shape[2]
            size = 48 if count % 48 == 0 else count
            parts = [
                (mine.at[rows], whole.at[own, x, rows], whole.at[other, x, rows])
                for rows in (pl.ds(low, size) for low in range(0, count, size))
            ]
        self.along_z = [place.push(src, here, place.beside("zh")) for src, here, _ in parts]
        self.along_x = [place.push(src, here, place.beside("x")) for src, here, _ in parts]
        self.onward = [place.push(there, there, place.beside("x")) for _, _, there in parts]
        self.kept = [place.copy(src, here) for src, here, _ in parts]

    def pairs(self):
        def launch(c):
            self.along_z[c].start()
            self.along_x[c].start()
            self.kept[c].start()

        def land(c):
            self.along_z[c].wait_recv()
            self.onward[c].start()

        return [(functools.partial(launch, c), functools.partial(land, c)) for c in range(len(self.kept))]

    def finish(self):
        for c in range(len(self.kept)):
            self.along_x[c].wait_recv()
            self.onward[c].wait_recv()
            self.kept[c].wait()


class Reduce:
    def __init__(self, place, total, landing, deliver):
        self.columns = len(total.shape) == 6
        self.place, self.total, self.deliver = place, total, deliver
        self.xin, self.zout, self.zin, self.final = landing[:4]
        self.landed = landing[4] if self.columns else None
        x, zh, beside = place.x, place.zh, place.beside
        self.flips = FLIPS + ((0, 0, 0),)
        self.chunks = self.zin.shape[0]
        self.along_x = [
            [
                place.push(self.part(j, to_zh, 1 - x), self.xin.at[j, i], beside("x"), False)
                for i, to_zh in enumerate((1 - zh, zh))
            ]
            for j in range(self.chunks)
        ]
        self.along_z = [place.push(self.zout.at[j], self.zin.at[j], beside("zh"), False) for j in range(self.chunks)]
        if self.columns:
            here = self.landed.at[place.rank(0, 0, 0)]
            self.back = [place.push(self.final.at[j], here, place.member(flips), False) for j, flips in enumerate(FLIPS)]
            self.back.append(place.copy(self.final.at[7], here))

    def part(self, j, zh, x):
        if self.columns:
            flip_z, flip_y, flip_core = self.flips[j]
            place = self.place
            chunk = place.flipped("yl", flip_y) * 2 + place.flipped("core", flip_core)
            return self.total.at[chunk, zh, place.flipped("zl", flip_z), x]
        count = self.zin.shape[1]
        low = ((zh * 2 + x) * self.chunks + j) * count
        return self.total.at[pl.ds(pl.multiple_of(low, 16), count)]

    def start(self):
        for copies in self.along_x:
            for copy in copies:
                copy.start()

    def pairs(self):
        x, zh = self.place.x, self.place.zh

        def launch(j):
            for copy in self.along_x[j]:
                copy.wait_recv()
            self.zout[j] = (self.part(j, 1 - zh, x)[...].astype(F32) + self.xin[j, 0].astype(F32)).astype(BF16)
            self.along_z[j].start()

        def land(j):
            self.along_z[j].wait_recv()
            total = self.part(j, zh, x)[...].astype(F32) + self.xin[j, 1].astype(F32) + self.zin[j].astype(F32)
            if self.columns:
                self.final[j] = total.astype(BF16)
                self.back[j].start()
            else:
                count = self.zin.shape[1]
                self.final[j * count : (j + 1) * count] = total

        return [(functools.partial(launch, j), functools.partial(land, j)) for j in range(self.chunks)]

    def finish(self):
        if self.columns:
            for copy in self.back[:-1]:
                copy.wait_recv()
            self.back[-1].wait()
        sent = [copy for copies in self.along_x for copy in copies] + self.along_z
        for copy in sent + (self.back[:-1] if self.columns else []):
            copy.wait_send()
        self.deliver(self.landed if self.columns else self.final)


def landing_shapes(total):
    if len(total) == 6:
        rows = total[4:]
        return [((8, 2) + rows, BF16)] + [((8,) + rows, BF16)] * 4
    count = total[0] // 4
    size = 48 if count % 48 == 0 else count
    rows = (size,) + total[1:]
    chunks = (count // size,)
    return [(chunks + (2,) + rows, BF16), (chunks + rows, BF16), (chunks + rows, BF16), ((count,) + total[1:], F32)]


def loop(count, body):
    def step(i, carry):
        body(i)
        return carry

    lax.fori_loop(0, count, step, 0)


def tile(i, width=TILE):
    return pl.ds(pl.multiple_of(i * width, width), width)


def dot(left, right):
    return jnp.dot(left, right, preferred_element_type=F32)


def dot_cols(left, right):
    return lax.dot_general(left, right, (((1,), (1,)), ((), ())), preferred_element_type=F32)


def dot_rows(left, right):
    return lax.dot_general(left, right, (((0,), (0,)), ((), ())), preferred_element_type=F32)


def swap_half(values):
    return pltpu.roll(values, LANES // 2, 1)


class Halo:
    def __init__(self, place, buffer, edge, landing, forward):
        x, zh, count = place.x, place.zh, lax.axis_size("x")
        first, final = x == 0, x == count - 1
        low, high, every = pl.ds(0, 4), pl.ds(4, 4), pl.ds(0, 8)
        lead = (slice(None),) * (len(buffer.shape) - 3)
        step = lax.rem(x + 1, count) if forward else lax.rem(x + count - 1, count)
        if forward:
            within, turn, beyond = jnp.logical_not(final), final, jnp.logical_and(final, zh == 0)
            into, turned, entered = jnp.logical_not(first), first, jnp.logical_and(first, zh == 1)
            sent, landed = low, high
        else:
            within, turn, beyond = jnp.logical_not(first), first, jnp.logical_and(first, zh == 1)
            into, turned, entered = jnp.logical_not(final), final, jnp.logical_and(final, zh == 0)
            sent, landed = high, low

        def push(src, dst, device):
            return place.push(buffer.at[lead + (src, edge)], landing.at[lead + (dst,)], device, False)

        copies = [
            push(every, every, {"x": step}),
            push(sent, landed, {"x": step}),
            push(landed, sent, {"x": step, "zh": 1 - zh}),
        ]
        self.sends = list(zip((within, turn, beyond), copies))
        self.lands = list(zip((into, turned, entered), copies))
        self.unreached = jnp.logical_and(turned, jnp.logical_not(entered))
        self.landing, self.open_end = landing, lead + (sent,)

    def start(self):
        for condition, copy in self.sends:
            pl.when(condition)(copy.start)

        @pl.when(self.unreached)
        def _():
            shape = self.landing.at[self.open_end].shape
            self.landing[self.open_end] = jnp.zeros(shape, self.landing.dtype)

    def wait_recv(self):
        for condition, copy in self.lands:
            pl.when(condition)(copy.wait_recv)

    def wait_send(self):
        for condition, copy in self.sends:
            pl.when(condition)(copy.wait_send)


SAVED = ("conv_whole", "joint", "carried", "mixed", "gated", "ffn_whole", "gate_up", "hidden")
WEIGHTS = ("in_w", "out_w", "both_w", "down_w")


def forms_of(tokens, features, wide, tall, layers):
    channels, units = (-(-rows // LANES) * LANES for rows in tall)
    block = (tokens, features)
    return {
        "in_w": ((features, wide[0]), BF16),
        "both_w": ((features, wide[1]), BF16),
        "out_w": ((tall[0], features), BF16),
        "down_w": ((tall[1], features), BF16),
        "conv_whole": ((8,) + block, BF16),
        "ffn_whole": ((8,) + block, BF16),
        "joint": ((8, tokens, wide[0]), F32),
        "gate_up": ((8, tokens, wide[1]), F32),
        "carried": ((8, tokens + HALO, channels), F32),
        "mixed": ((8, tokens, channels), F32),
        "gated": ((8, tokens, channels), BF16),
        "hidden": ((8, tokens, units), BF16),
        "tall_w": ((units, features), BF16),
        "grad_rows": ((8, tokens, wide[1]), BF16),
        "grad_gated": ((8, tokens, channels), F32),
        "edges": ((2, 8, tokens + HALO, channels), F32),
        "heads": ((layers, 2, 8, HALO, channels), F32),
        "tails": ((layers, 8, HALO, channels), F32),
        "stream": (block, F32),
        "next": (block, BF16),
        "whole": ((2, 8) + block, BF16),
        "part": ((4, 2) + block, BF16),
        "sib": ((4,) + block, BF16),
        "yin": ((2,) + block, BF16),
        "yout": ((2,) + block, BF16),
        "zin": (block, BF16),
        "zout": (block, BF16),
        "grad_in_w": ((4, 2, 2, 2, features // 32, wide[0]), BF16),
        "grad_both_w": ((4, 2, 2, 2, features // 32, wide[1]), BF16),
        "grad_out_w": ((channels, features), BF16),
        "grad_down_w": ((units, features), BF16),
    }


class Pass:
    def __init__(self, place, buffers):
        self.place, self.buffers = place, buffers
        self.tokens, self.features = buffers["zin"].shape
        half = self.tokens // HALVES
        self.halves = [pl.ds(h * half, half) for h in range(HALVES)]
        self.chips = ((0, 0), (1, 0), (0, 1), (1, 1))
        self.phases = 0
        self.items, self.queue, self.flying = [], [], []
        self.saving, self.loading = [], {}

    def enter(self, more, barrier_all):
        place = self.place
        barrier = pltpu.get_barrier_semaphore()
        if barrier_all:
            partners = [device for device, _ in every_other(place)]
            expected = len(partners)
        else:
            x, zh, x_size = place.x, place.zh, lax.axis_size("x")
            partners = [place.beside(axis) for axis in ("core", "yl", "zl")] + more
            partners += [{"x": lax.rem(x + 1, x_size)}, {"x": lax.rem(x + x_size - 1, x_size)}]
            at_turn = jnp.logical_or(jnp.logical_and(x == x_size - 1, zh == 0), jnp.logical_and(x == 0, zh == 1))
            across = {"x": jnp.where(x == 0, x_size - 1, 0), "zh": 1 - zh}

            @pl.when(at_turn)
            def _():
                pl.semaphore_signal(barrier, inc=1, device_id=across, device_id_type=MESH)

            expected = len(partners) + jnp.where(at_turn, 1, 0)
        for partner in partners:
            pl.semaphore_signal(barrier, inc=1, device_id=partner, device_id_type=MESH)
        pl.semaphore_wait(barrier, expected)

    def begin(self, items):
        for item in items:
            item.left = len(item.pairs())
            self.queue += [(item,) + pair for pair in item.pairs()]
            self.items.append(item)

    def launch(self, count):
        for item, launch, land in self.queue[:count]:
            launch()
            self.flying.append((item, land))
        del self.queue[:count]

    def land(self, count):
        for item, land in self.flying[:count]:
            land()
            item.left -= 1
        del self.flying[:count]

    def step(self):
        if len(self.flying) >= FLYING:
            self.land(1)
        self.launch(1)

    def settle(self, items):
        for item in items:
            while any(queued is item for queued, _, _ in self.queue):
                self.launch(1)
            while item.left:
                self.land(1)
            item.finish()
            self.items.remove(item)

    def load(self, name, source, target):
        if target.shape != source.shape:
            rows = target.shape[0] - source.shape[0]
            target[source.shape[0] :] = jnp.zeros((rows,) + target.shape[1:], BF16)
            target = target.at[: source.shape[0]]
        self.loading[name] = self.place.copy(source, target)
        self.loading[name].start()

    def loaded(self, *names):
        for name in names:
            self.loading.pop(name).wait()

    def save(self, source, target):
        self.saving.append(self.place.copy(source, target))
        self.saving[-1].start()

    def saved(self):
        for copy in self.saving:
            copy.wait()
        self.saving = []

    def pair(self, chip):
        return pl.ds(self.place.rank(*chip, 0) - self.place.core, 2)

    def rows_of(self, values):
        return values.reshape(2 * self.tokens, values.shape[-1])

    def blocks_of(self, values):
        return values.reshape(2, self.tokens, values.shape[-1])

    def all_rows(self, values):
        return values.reshape(8 * self.tokens, values.shape[-1])

    def phase(self, mine, first, second, after, before_first=None, before_second=None, between=None, aside=None):
        place, buffers, halves, chips = self.place, self.buffers, self.halves, self.chips
        rank, sent = place.rank, []
        whole = buffers["whole"].at[self.phases % 2]
        self.phases += 1
        part, sib, yin, yout, zin, zout = (buffers[name] for name in ("part", "sib", "yin", "yout", "zin", "zout"))
        to_sibling, to_y, to_z = (place.beside(axis) for axis in ("core", "yl", "zl"))
        own, beside_z, beside_y, corner = (rank(*chip, 0) for chip in chips)

        def push(src, dst, device):
            sent.append(place.push(src, dst, device, False))
            return sent[-1]

        def sends(src, at, device):
            return [push(mine.at[rows] if src is None else src.at[at, rows], whole.at[at, rows], device) for rows in halves]

        def landed(copies):
            for copy in copies:
                copy.wait_recv()

        from_z, from_y, own_to_core = sends(None, own, to_z), sends(None, own, to_y), sends(None, own, to_sibling)
        from_corner = sends(whole, beside_z, to_y)
        z_to_core, y_to_core, corner_to_core = (sends(whole, at, to_sibling) for at in (beside_z, beside_y, corner))
        own_place = place.copy(mine, whole.at[own])
        own_place.start()
        for h in range(HALVES):
            for copies in (from_z, from_y, own_to_core):
                copies[h].start()
        self.step()
        if before_first is not None:
            before_first()
        own_place.wait()
        landed(own_to_core)
        first(whole, chips[0])
        for h in range(HALVES):
            from_z[h].wait_recv()
            from_corner[h].start()
            z_to_core[h].start()
        self.step()
        for h in range(HALVES):
            from_y[h].wait_recv()
            y_to_core[h].start()
        landed(z_to_core)
        first(whole, chips[1])
        self.step()
        landed(y_to_core)
        first(whole, chips[2])
        self.step()
        for h in range(HALVES):
            from_corner[h].wait_recv()
            corner_to_core[h].start()
        landed(corner_to_core)
        first(whole, chips[3])
        self.step()
        if between is not None:
            between(whole)
        if before_second is not None:
            before_second()

        order = (chips[3], chips[2], chips[1], chips[0])
        sib_copies = [push(part.at[i, 1 - place.core], sib.at[i], to_sibling) for i in range(4)]
        y_copies = [[push(yout.at[i, rows], yin.at[i, rows], to_y) for rows in halves] for i in range(2)]
        z_copies = [push(zout.at[rows], zin.at[rows], to_z) for rows in halves]

        def multiply(i):
            def columns(j):
                part[i, :, :, tile(j)] = self.blocks_of(second(order[i], j).astype(BF16))

            loop(self.features // TILE, columns)
            sib_copies[i].start()

        def chip_sum(i, rows):
            return part[i, place.core, rows].astype(F32) + sib[i, rows].astype(F32)

        def to_y_side(i):
            sib_copies[i].wait_recv()
            for h, rows in enumerate(halves):
                yout[i, rows] = chip_sum(i, rows).astype(BF16)
                y_copies[i][h].start()

        multiply(0)
        multiply(1)
        to_y_side(0)
        self.step()
        multiply(2)
        to_y_side(1)
        multiply(3)
        self.step()
        sib_copies[2].wait_recv()
        for h, rows in enumerate(halves):
            y_copies[0][h].wait_recv()
            zout[rows] = (chip_sum(2, rows) + yin[0, rows].astype(F32)).astype(BF16)
            z_copies[h].start()
        self.step()
        if aside is not None:
            aside(whole)
        self.step()
        sib_copies[3].wait_recv()
        for copy in sent:
            copy.wait_send()
        for h, rows in enumerate(halves):
            y_copies[1][h].wait_recv()
            z_copies[h].wait_recv()
            if h == HALVES - 1:
                self.step()
            after(h, rows, chip_sum(3, rows) + yin[1, rows].astype(F32) + zin[rows].astype(F32))
        self.step()


def c_columns(joint, b, lane):
    if lane == 0:
        return joint[b, :, LANES : 2 * LANES]
    return swap_half(joint[b, :, 3 * LANES : 4 * LANES])


def both_lanes():
    return [(lane, slice(lane, lane + LANES)) for lane in (0, LANES)]


def forward_kernel(plan, *refs):
    refs = list(refs)
    layers, moving, buffer_names = plan["layers"], plan["moving"], plan["buffers"]

    def take(count):
        taken = refs[:count]
        del refs[:count]
        return taken

    stream_in, gains, taps_ref, keep = take(4)
    weights = [dict(zip(WEIGHTS, take(2 if moving else 4))) for _ in range(1 if moving else layers)]
    mine = [take(4 if layer else 2) for layer in range(layers)] if moving else None
    stream_out, middles, sources = take(1)[0], take(layers), take(layers - 1)
    saves = [dict(zip(SAVED, take(len(SAVED)))) for _ in range(layers)]
    flat = []
    if moving:
        for layer in range(layers):
            names = WEIGHTS if layer else WEIGHTS[2:]
            wholes = dict(zip(names, take(len(names))))
            if layer:
                weights.append({})
            weights[layer].update(wholes)
    buffers = dict(zip(buffer_names, take(len(buffer_names))))
    place = Place(*take(3))
    run = Pass(place, buffers)
    tokens, features = run.tokens, run.features
    rows_of, blocks_of, pair = run.rows_of, run.blocks_of, run.pair
    joint, carried, mixed, gated = (buffers[name] for name in ("joint", "carried", "mixed", "gated"))
    gate_up, hidden = buffers["gate_up"], buffers["hidden"]
    in_w, out_w, both_w, down_w = (buffers["vmem_" + name] for name in WEIGHTS)
    main = gate_up.shape[2] // (2 * LANES) * LANES
    next_ref = buffers["next"]

    coming = {}

    def moves(layer, names):
        own = dict(zip(WEIGHTS if layer else WEIGHTS[2:], mine[layer]))
        for name in names:
            coming[layer, name] = Gather(place, own[name], weights[layer][name])
            run.begin([coming[layer, name]])

    def load(layer, names):
        for name in names:
            if (layer, name) in coming:
                run.settle([coming.pop((layer, name))])
            source, target = weights[layer][name], buffers["vmem_" + name]
            if len(source.shape) == 2:
                run.load(name, source, target)
                continue
            copies = []
            rows = source.shape[-2]
            lead = source.shape[:-2]
            for n, index in enumerate(itertools.product(*(range(size) for size in lead))):
                copies.append(place.copy(source.at[index], target.at[pl.ds(n * rows, rows)]))
                copies[-1].start()
            filled = rows * len(copies)
            if filled < target.shape[0]:
                target[filled:] = jnp.zeros((target.shape[0] - filled, target.shape[1]), BF16)
            run.loading[name] = Several(copies)

    def rounded(values, gain):
        return (values * rms_scale(values) * gain).astype(BF16)

    def conv(layer, stream):
        def before_first():
            load(layer, ("in_w",))
            run.loaded("in_w")

        def first(whole, chip):
            at = pair(chip)

            def columns(j):
                joint[at, :, tile(j)] = blocks_of(dot(rows_of(whole[at]), in_w[:, tile(j)]))

            loop(2, columns)
            joint[at, :, 2 * TILE :] = blocks_of(dot(rows_of(whole[at]), in_w[:, 2 * TILE :]))
            here = pl.ds(HALO, tokens)
            carried[at, here, :LANES] = joint[at, :, :LANES] * joint[at, :, 2 * LANES : 3 * LANES]
            carried[at, here, LANES:] = joint[at, :, 3 * LANES : 4 * LANES] * joint[at, :, 4 * LANES :]

        def between(whole):
            halo = Halo(place, carried, pl.ds(tokens, HALO), buffers["tails"].at[layer], True)
            halo.start()
            run.saved()
            run.save(joint, saves[layer]["joint"])
            run.save(whole, saves[layer]["conv_whole"])
            halo.wait_recv()
            carried[:, :HALO] = buffers["tails"][layer]

            def block(b):
                keep_one, keep_two = keep[0, b], keep[1, b]
                for lane, lanes in both_lanes():
                    result = (
                        taps_ref[layer, 0:1, lanes] * carried[b, HALO - 2 : HALO - 2 + tokens, lanes] * keep_two
                        + taps_ref[layer, 1:2, lanes] * carried[b, HALO - 1 : HALO - 1 + tokens, lanes] * keep_one
                        + taps_ref[layer, 2:3, lanes] * carried[b, HALO : HALO + tokens, lanes]
                    )
                    mixed[b, :, lanes] = result
                    gated[b, :, lanes] = (c_columns(joint, b, lane) * result).astype(BF16)

            loop(8, block)
            halo.wait_send()
            for name in ("carried", "mixed", "gated"):
                run.save(buffers[name], saves[layer][name])

        def second(chip, j):
            return dot(rows_of(gated[pair(chip)]), out_w[:, tile(j)])

        def after(h, rows, total):
            middle = stream[rows] + total
            middles[layer][rows] = middle
            next_ref[rows] = rounded(middle, gains[2 * layer + 1])

        def before_second():
            load(layer, ("out_w",))
            run.loaded("out_w")

        run.phase(next_ref, first, second, after, before_first, before_second, between)

    def ffn(layer):
        def before_first():
            load(layer, ("both_w",))
            run.loaded("both_w")

        def first(whole, chip):
            at = pair(chip)

            def columns(j):
                ups = pl.ds(pl.multiple_of(main + j * TILE, TILE), TILE)
                gate = dot(rows_of(whole[at]), both_w[:, tile(j)])
                up = dot(rows_of(whole[at]), both_w[:, ups])
                gate_up[at, :, tile(j)] = blocks_of(gate)
                gate_up[at, :, ups] = blocks_of(up)
                hidden[at, :, tile(j)] = blocks_of((gate * jax.nn.sigmoid(gate) * up).astype(BF16))

            loop(main // TILE, columns)
            both = dot(rows_of(whole[at]), both_w[:, 2 * main :])
            gate_up[at, :, 2 * main :] = blocks_of(both)
            lane = lax.broadcasted_iota(jnp.int32, both.shape, 1)
            tail = jnp.where(lane < LANES // 2, both * jax.nn.sigmoid(both) * swap_half(both), 0.0)
            hidden[at, :, main:] = blocks_of(tail.astype(BF16))

        def between(whole):
            run.saved()
            run.save(whole, saves[layer]["ffn_whole"])
            run.save(gate_up, saves[layer]["gate_up"])
            run.save(hidden, saves[layer]["hidden"])

        def second(chip, j):
            return dot(rows_of(hidden[pair(chip)]), down_w[:, tile(j)])

        def after(h, rows, total):
            result = middles[layer][rows] + total
            if layer + 1 < layers:
                sources[layer][rows] = result
                next_ref[rows] = rounded(result, gains[2 * layer + 2])
            else:
                stream_out[rows] = result

        def before_second():
            load(layer, ("down_w",))
            run.loaded("down_w")

        run.phase(next_ref, first, second, after, before_first, before_second, between)

    next_ref[...] = rounded(stream_in[...], gains[0])
    run.enter([place.beside("zh"), place.beside("x")] if moving else [], False)
    if moving:
        for layer in range(layers):
            moves(layer, WEIGHTS if layer else WEIGHTS[2:])
    for layer in range(layers):
        conv(layer, sources[layer - 1] if layer else stream_in)
        ffn(layer)
    run.saved()
    for copy in place.sent:
        copy.wait_send()


class Several:
    def __init__(self, copies):
        self.copies = copies

    def wait(self):
        for copy in self.copies:
            copy.wait()


def forward(stream, gains, taps, keep, weights, mine, tall):
    tokens, features = stream.shape
    layers = taps.shape[0]
    moving = mine is not None
    wide = (weights[0][0].shape[1], mine[0][0].shape[3] if moving else weights[0][2].shape[1])
    forms = forms_of(tokens, features, wide, tall, layers)
    inside = pl.BlockSpec(memory_space=pltpu.VMEM)
    anywhere = pl.BlockSpec(memory_space=pl.ANY)
    outs = [(forms["stream"], inside)] * (1 + layers + layers - 1)
    outs += [(forms[name], anywhere) for _ in range(layers) for name in SAVED]
    if moving:
        outs += [((whole_shape(array.shape), BF16), anywhere) for group in mine for array in group]
    buffers = {name: forms[name] for name in ("joint", "carried", "mixed", "gated", "gate_up", "hidden", "next", "tails")}
    buffers |= {name: forms[name] for name in ("whole", "part", "sib", "yin", "yout", "zin", "zout")}
    buffers |= {"vmem_in_w": forms["in_w"], "vmem_both_w": forms["both_w"]}
    buffers |= {"vmem_out_w": ((forms["gated"][0][2], features), BF16), "vmem_down_w": forms["tall_w"]}
    operands = [array for group in weights for array in group]
    operands += [array for group in mine for array in group] if moving else []
    results = pl.pallas_call(
        functools.partial(forward_kernel, {"layers": layers, "moving": moving, "buffers": tuple(buffers)}),
        out_shape=[jax.ShapeDtypeStruct(*form) for form, _ in outs],
        in_specs=[inside] * 4 + [anywhere] * len(operands),
        out_specs=[spec for _, spec in outs],
        scratch_shapes=[pltpu.VMEM(*form) for form in buffers.values()] + [pltpu.SemaphoreType.DMA((SEMAPHORES,))] * 3,
        compiler_params=pltpu.CompilerParams(
            collective_id=COLLECTIVE_ID["forward"], has_side_effects=True, vmem_limit_bytes=62 << 20
        ),
        name="forward",
    )(stream, gains, taps, keep, *operands)
    stream_out, results = results[0], results[1:]
    middles, results = results[:layers], results[layers:]
    sources, results = results[: layers - 1], results[layers - 1 :]
    count = layers * len(SAVED)
    return stream_out, middles, sources, results[:count], results[count:]


def backward_kernel(plan, *refs):
    refs = list(refs)
    layers, moving, buffer_names = plan["layers"], plan["moving"], plan["buffers"]

    def take(count):
        taken = refs[:count]
        del refs[:count]
        return taken

    grad_out, gains, taps_ref, keep = take(4)
    middles, sources = take(layers), take(layers)
    weights = [dict(zip(WEIGHTS, take(4))) for _ in range(layers)]
    saves = [dict(zip(SAVED, take(len(SAVED)))) for _ in range(layers)]
    (grad_in,) = take(1)
    if moving:
        small_sum, grad_in_w, grad_out_w, gate_out, up_out, down_out = take(6)
    else:
        gain_out, taps_out = take(2)
        raw = [take(4) for _ in range(layers)]
    buffers = dict(zip(buffer_names, take(len(buffer_names))))
    if moving:
        landing = {name: take(5 if name in ("in_w", "both_w") else 4) for name in WEIGHTS}
        staging, slabs, slabs_in = take(2), *take(2)
        free = dict(zip(("both", "down", "conv"), take(3)))
    place = Place(*take(3))
    run = Pass(place, buffers)
    tokens, features = run.tokens, run.features
    rows_of, blocks_of, all_rows, pair = run.rows_of, run.blocks_of, run.all_rows, run.pair
    wide = {"in_w": plan["wide"][0], "both_w": plan["wide"][1]}
    joint, gate_up = buffers["gate_up"].at[:, :, : wide["in_w"]], buffers["gate_up"]
    grad_joint, grad_gate_up = buffers["grad_rows"].at[:, :, : wide["in_w"]], buffers["grad_rows"]
    in_w, both_w = buffers["wide_w"].at[:, : wide["in_w"]], buffers["wide_w"]
    channels, units = buffers["mixed"].shape[2], buffers["hidden"].shape[2]
    out_w, down_w = buffers["tall_w"].at[:channels], buffers["tall_w"]
    gated, hidden = buffers["hidden"].at[:, :, :channels], buffers["hidden"]
    carried, mixed, edges, grad_gated = (buffers[name] for name in ("carried", "mixed", "edges", "grad_gated"))
    kept_whole, next_ref, grad_ref, held = (buffers[name] for name in ("conv_whole", "next", "stream", "held"))
    gain_grads, tap_grads = buffers["gain_grads"], buffers["tap_grads"]
    main = gate_up.shape[2] // (2 * LANES) * LANES

    def load_rows(name, source, target):
        if len(source.shape) == 2:
            run.load(name, source, target)
            return
        rows, lead = source.shape[-2], source.shape[:-2]
        copies = []
        for n, index in enumerate(itertools.product(*(range(size) for size in lead))):
            copies.append(place.copy(source.at[index], target.at[pl.ds(n * rows, rows)]))
            copies[-1].start()
        filled = rows * len(copies)
        if filled < target.shape[0]:
            target[filled:] = jnp.zeros((target.shape[0] - filled, target.shape[1]), BF16)
        run.loading[name] = Several(copies)

    def deliver_columns(outs, layer, views):
        def deliver(landed):
            run.saved()
            shards_to(landed, views)
            for source, out in outs:
                run.save(source, out.at[layer])

        return deliver

    def deliver_rows(out, layer):
        def deliver(final):
            run.save(final, out.at[layer])

        return deliver

    reduced = {"both": 0, "down": 0, "conv": 0}
    under_way = {"both": [], "down": [], "conv": []}

    def reduce(layer, kind, names):
        if not moving:
            for name in names:
                source = buffers["grad_" + name]
                target = raw[layer][WEIGHTS.index(name)]
                run.save(source.at[: target.shape[0]] if source.shape != target.shape else source, target)
            return
        if reduced[kind]:
            pl.semaphore_wait(free[kind], 9)
        reduced[kind] += 1
        run.saved()
        items = []
        for name in names:
            if name == "in_w":
                width = features
                views = [staging[0].at[:, i * width : (i + 1) * width] for i in range(3)]
                deliver = deliver_columns([(staging[0], grad_in_w)], layer, views)
            elif name == "both_w":
                deliver = deliver_columns([(staging[0], gate_out), (staging[1], up_out)], layer, list(staging))
            else:
                deliver = deliver_rows(grad_out_w if name == "out_w" else down_out, layer)
            total = buffers["grad_" + name]
            if name in ("out_w", "down_w"):
                total = total.at[: 4 * landing[name][3].shape[0]]
            items.append(Reduce(place, total, landing[name], deliver))
            items[-1].start()
        run.begin(items)
        under_way[kind] = items

    def settle(kind):
        items, under_way[kind] = under_way[kind], []
        run.settle(items)
        if items and reduced[kind] < layers:
            for device in [place.member(flips) for flips in FLIPS] + [place.beside("zh"), place.beside("x")]:
                pl.semaphore_signal(free[kind], inc=1, device_id=device, device_id_type=MESH)

    def step_back(h, rows, total, stream, gain, row):
        scale = rms_scale(stream)
        gain_grad = jnp.sum(total * stream * scale, axis=0, keepdims=True)
        gain_grads[row : row + 1] = gain_grad if h == 0 else gain_grads[row : row + 1] + gain_grad
        scaled = total * gain
        grad = (
            grad_ref[rows]
            + scale * scaled
            - stream * (scale * scale * scale) * jnp.mean(scaled * stream, axis=-1, keepdims=True)
        )
        grad_ref[rows] = grad
        next_ref[rows] = grad.astype(BF16)
        return grad

    def ffn_back(layer):
        def before_first():
            load_rows("down_w", weights[layer]["down_w"], down_w)
            run.load("gate_up", saves[layer]["gate_up"], gate_up)
            load_rows("both_w", weights[layer]["both_w"], both_w)
            run.load("hidden", saves[layer]["hidden"], hidden)
            run.load("whole", saves[layer]["ffn_whole"], kept_whole)
            run.load("held", middles[layer], held)
            run.loaded("down_w", "gate_up")

        def grads(grad_hidden, gate, up):
            sigmoid = jax.nn.sigmoid(gate)
            return grad_hidden * up * sigmoid * (1.0 + gate * (1.0 - sigmoid)), grad_hidden * gate * sigmoid

        def first(whole, chip):
            at = pair(chip)

            def columns(j):
                ups = pl.ds(pl.multiple_of(main + j * TILE, TILE), TILE)
                grad_hidden = dot_cols(rows_of(whole[at]), down_w[tile(j), :])
                gate, up = (rows_of(gate_up[at, :, lanes]) for lanes in (tile(j), ups))
                grad_gate, grad_up = grads(grad_hidden, gate, up)
                grad_gate_up[at, :, tile(j)] = blocks_of(grad_gate.astype(BF16))
                grad_gate_up[at, :, ups] = blocks_of(grad_up.astype(BF16))

            loop(main // TILE, columns)
            grad_hidden = dot_cols(rows_of(whole[at]), down_w[main:, :])
            both = rows_of(gate_up[at, :, 2 * main :])
            grad_gate, grad_up = grads(grad_hidden, both, swap_half(both))
            grad_gate_up[at, :, 2 * main :] = blocks_of((grad_gate + swap_half(grad_up)).astype(BF16))

        def second(chip, j):
            return dot_cols(rows_of(grad_gate_up[pair(chip)]), both_w[tile(j), :])

        def aside(whole):
            run.loaded("whole", "hidden")
            settle("both")
            settle("down")
            grad_both, grad_down = buffers["grad_both_w"], buffers["grad_down_w"]
            width = features // 4

            def both_rows(c):
                left = all_rows(kept_whole[:, :, tile(c, width)])
                result = dot_rows(left, all_rows(grad_gate_up[...])).astype(BF16)
                grad_both[c] = result.reshape(grad_both.shape[1:])

            def down_rows(j):
                left = all_rows(hidden[:, :, tile(j, LANES)])
                grad_down[tile(j, LANES), :] = dot_rows(left, all_rows(whole[...])).astype(BF16)

            loop(4, both_rows)
            reduce(layer, "both", ("both_w",))
            loop(units // LANES, down_rows)
            reduce(layer, "down", ("down_w",))

        def after(h, rows, total):
            step_back(h, rows, total, held[rows], gains[2 * layer + 1], 2 * layer + 1)

        run.phase(next_ref, first, second, after, before_first, lambda: run.loaded("both_w", "held"), None, aside)

    def conv_back(layer):
        taps = taps_ref.at[layer]

        def before_first():
            load_rows("out_w", weights[layer]["out_w"], out_w)
            for name, target in (("joint", joint), ("carried", carried), ("mixed", mixed)):
                run.load(name, saves[layer][name], target)
            load_rows("in_w", weights[layer]["in_w"], in_w)
            run.load("gated", saves[layer]["gated"], gated)
            run.load("whole", saves[layer]["conv_whole"], kept_whole)
            run.load("held", sources[layer], held)
            run.loaded("out_w")

        def first(whole, chip):
            at = pair(chip)
            grad_gated[at] = blocks_of(dot_cols(rows_of(whole[at]), out_w[...]))

        def between(whole):
            run.loaded("joint", "carried", "mixed")
            tap_grads[layer] = jnp.zeros(tap_grads.shape[1:], F32)

            def block(b):
                keep_one, keep_two = keep[0, b], keep[1, b]
                for lane, lanes in both_lanes():
                    grad_value = grad_gated[b, :, lanes]
                    grad_mixed = grad_value * c_columns(joint, b, lane)
                    first_tap, second_tap = grad_mixed * keep_two, grad_mixed * keep_one
                    edges[0, b, :tokens, lanes] = second_tap * taps[1:2, lanes]
                    edges[1, b, :tokens, lanes] = first_tap * taps[0:1, lanes]
                    mixed[b, :, lanes] = grad_value * mixed[b, :, lanes]
                    grad_gated[b, :, lanes] = grad_mixed * taps[2:3, lanes]
                    for row, grad, back_by in ((0, first_tap, 2), (1, second_tap, 1), (2, grad_mixed, 0)):
                        tap_in = carried[b, HALO - back_by : HALO - back_by + tokens, lanes]
                        tap_grads[layer, row : row + 1, lanes] += jnp.sum(grad * tap_in, axis=0, keepdims=True)

            loop(8, block)
            halo = Halo(place, edges, pl.ds(0, HALO), buffers["heads"].at[layer], False)
            halo.start()
            halo.wait_recv()
            edges[:, :, tokens:] = buffers["heads"][layer]

            def block_after(b):
                for lane, lanes in both_lanes():
                    grad_carried = (
                        grad_gated[b, :, lanes] + edges[0, b, 1 : 1 + tokens, lanes] + edges[1, b, 2 : 2 + tokens, lanes]
                    )
                    grad_c = mixed[b, :, lanes]
                    if lane == 0:
                        grad_joint[b, :, :LANES] = (grad_carried * joint[b, :, 2 * LANES : 3 * LANES]).astype(BF16)
                        grad_joint[b, :, LANES : 2 * LANES] = grad_c.astype(BF16)
                        grad_joint[b, :, 2 * LANES : 3 * LANES] = (grad_carried * joint[b, :, :LANES]).astype(BF16)
                    else:
                        grad_b = grad_carried * joint[b, :, 4 * LANES :]
                        grad_joint[b, :, 3 * LANES : 4 * LANES] = (grad_b + swap_half(grad_c)).astype(BF16)
                        grad_joint[b, :, 4 * LANES :] = (grad_carried * joint[b, :, 3 * LANES : 4 * LANES]).astype(BF16)

            loop(8, block_after)
            halo.wait_send()
            if layer == 0:
                gradients(whole)

        def second(chip, j):
            return dot_cols(rows_of(grad_joint[pair(chip)]), in_w[tile(j), :])

        def gradients(whole):
            run.loaded("whole", "gated")
            settle("conv")
            grad_in_rows, grad_out_rows = buffers["grad_in_w"], buffers["grad_out_w"]
            width = features // 4

            def in_rows(c):
                left = all_rows(kept_whole[:, :, tile(c, width)])
                result = dot_rows(left, all_rows(grad_joint[...])).astype(BF16)
                grad_in_rows[c] = result.reshape(grad_in_rows.shape[1:])

            def out_rows(j):
                left = all_rows(gated[:, :, tile(j, LANES)])
                grad_out_rows[tile(j, LANES), :] = dot_rows(left, all_rows(whole[...])).astype(BF16)

            loop(4, in_rows)
            loop(channels // LANES, out_rows)
            reduce(layer, "conv", ("in_w", "out_w"))

        def after(h, rows, total):
            grad = step_back(h, rows, total, held[rows], gains[2 * layer], 2 * layer)
            if layer == 0:
                grad_in[rows] = grad

        run.phase(
            next_ref, first, second, after, before_first, lambda: run.loaded("in_w", "held"), between, gradients if layer else None
        )

    grad_ref[...] = grad_out[...]
    next_ref[...] = grad_out[...].astype(BF16)
    run.enter([], moving)
    for layer in reversed(range(layers)):
        ffn_back(layer)
        conv_back(layer)
    if moving:
        owned = features // 32
        slabs[...] = jnp.zeros(slabs.shape, F32)
        for owner in range(32):
            slabs[owner, : 2 * layers, :owned] = gain_grads[:, owner * owned : (owner + 1) * owned]
        for layer in range(layers):
            row = 2 * layers + 3 * layer
            for zh, x in itertools.product(range(2), repeat=2):
                owner = ((place.yl * 2 + place.core) * 2 + zh) * 4 + place.zl * 2 + x
                low = (zh * 2 + x) * owned
                slabs[owner, row : row + 3, :owned] = tap_grads[layer, :3, low : low + owned]
        copies = []
        for i, (device, flips) in enumerate(every_other(place)):
            copies.append(place.push(slabs.at[place.owner(flips)], slabs_in.at[i], device))
            copies[-1].start()
        run.launch(len(run.queue))
        for kind in ("both", "down", "conv"):
            settle(kind)
        for copy in copies:
            copy.wait_recv()
        small_sum[...] = slabs[place.owner()] + jnp.sum(slabs_in[...], axis=0)
    else:
        gain_out[...] = gain_grads[...]
        taps_out[...] = tap_grads[...]
    run.saved()
    for copy in place.sent:
        copy.wait_send()


def backward(grad_out, gains, taps, keep, middles, sources, weights, saved, tall, moving):
    tokens, features = grad_out.shape
    layers = taps.shape[0]
    wide = (weights[0][0].shape[-1], weights[0][2].shape[-1])
    forms = forms_of(tokens, features, wide, tall, layers)
    inside = pl.BlockSpec(memory_space=pltpu.VMEM)
    anywhere = pl.BlockSpec(memory_space=pl.ANY)
    owned = features // 32
    outs = [(forms["stream"], inside)]
    if moving:
        outs.append((((16, LANES), F32), inside))
        shapes = ((owned, 3 * features), (owned, features), (owned, 4 * tall[1] * 2), (owned, 4 * tall[1] * 2), (tall[1] // 4, features))
        outs += [(((layers,) + shape, F32), anywhere) for shape in shapes]
    else:
        outs.append((((2 * layers, features), F32), inside))
        outs.append((((layers, HALO, forms["mixed"][0][2]), F32), inside))
        for _ in range(layers):
            for name in WEIGHTS:
                shape = forms["grad_" + name][0]
                outs.append((((tall[0] if name == "out_w" else tall[1], features) if len(shape) == 2 else shape, BF16), anywhere))
    names = ("conv_whole", "gate_up", "carried", "mixed", "hidden", "grad_rows", "grad_gated", "edges", "heads", "tall_w")
    names += ("next", "stream", "whole", "part", "sib", "yin", "yout", "zin", "zout")
    names += ("grad_in_w", "grad_both_w", "grad_out_w", "grad_down_w")
    buffers = {name: forms[name] for name in names}
    buffers["wide_w"], buffers["held"] = forms["both_w"], forms["stream"]
    buffers["gain_grads"] = ((2 * layers, features), F32)
    buffers["tap_grads"] = ((layers, HALO, forms["mixed"][0][2]), F32)
    scratch = [pltpu.VMEM(*form) for form in buffers.values()]
    if moving:
        for name in WEIGHTS:
            shape = forms["grad_" + name][0]
            if len(shape) == 2:
                shape = (tall[0] if name == "out_w" else tall[1], features)
            scratch += [pltpu.VMEM(*form) for form in landing_shapes(shape)]
        scratch += [pltpu.VMEM((owned, 3 * features), F32)] * 2
        scratch += [pltpu.VMEM((32, 16, LANES), F32), pltpu.VMEM((31, 16, LANES), F32)]
        scratch += [pltpu.SemaphoreType.REGULAR] * 3
    operands = list(middles) + list(sources) + [array for group in weights for array in group] + list(saved)
    plan = {"layers": layers, "moving": moving, "buffers": tuple(buffers), "wide": wide}
    return pl.pallas_call(
        functools.partial(backward_kernel, plan),
        out_shape=[jax.ShapeDtypeStruct(*form) for form, _ in outs],
        in_specs=[inside] * 4 + [anywhere] * len(operands),
        out_specs=[spec for _, spec in outs],
        scratch_shapes=scratch + [pltpu.SemaphoreType.DMA((SEMAPHORES,))] * 3,
        compiler_params=pltpu.CompilerParams(
            collective_id=COLLECTIVE_ID["backward"], has_side_effects=True, vmem_limit_bytes=63 << 20
        ),
        name="backward",
    )(grad_out, gains, taps, keep, *operands)


def sizes_of(axes):
    return tuple(lax.axis_size(axis) for axis in axes)


def split_owners(array, dim):
    owners = sizes_of(OWNERS)
    count = 1
    for size in owners:
        count *= size
    shape = array.shape
    return array.reshape(shape[:dim] + owners + (shape[dim] // count,) + shape[dim + 1 :])


def column_shards(weights):
    rows = weights[0].shape[0]
    mains, rests = [], []
    for weight in weights:
        parts = split_owners(weight, 1).transpose(5, 2, 3, 0, 1, 4, 6, 7).reshape(8, rows, -1)
        main = parts.shape[2] // LANES * LANES
        mains.append(parts[:, :, :main])
        rests.append(parts[:, :, main:])
    shards = jnp.concatenate(mains + rests, axis=2)
    return jnp.pad(shards, ((0, 0), (0, 0), (0, -shards.shape[2] % LANES)))


def column_whole(shards, groups, width):
    rows = shards.shape[1]
    yh, yl, core, zh, zl, x = sizes_of(OWNERS)
    wholes = []
    for group in range(groups):
        part = jnp.concatenate(
            [shards[..., a:b] for a, b in pieces_of(groups, width, group, 0, width)], axis=-1
        ).reshape(zl, yl, core, rows, yh, zh, x, -1)
        wholes.append(part.transpose(3, 4, 1, 2, 5, 0, 6, 7).reshape(rows, -1))
    return wholes


def gather_columns(shards):
    mine = lax.all_to_all(shards, TP, split_axis=0, concat_axis=0, tiled=True)
    whole = lax.all_gather(mine, DP, axis=0, tiled=False)
    yh, yl, core, zh, zl, x = sizes_of(OWNERS)
    rows, columns = shards.shape[1:]
    whole = whole.reshape(yh, zh, x, zl, yl, core, rows, columns)
    return whole.transpose(0, 4, 5, 1, 3, 2, 6, 7).reshape(-1, columns)


def scatter_columns(total):
    yh, yl, core, zh, zl, x = sizes_of(OWNERS)
    columns = total.shape[1]
    parts = split_owners(total, 0).transpose(0, 3, 5, 4, 1, 2, 6, 7)
    parts = parts.reshape(yh * zh * x, -1, columns)
    mine = lax.psum_scatter(parts, DP, scatter_dimension=0, tiled=False)
    mine = mine.reshape(8, -1, columns)
    return lax.all_to_all(mine, TP, split_axis=0, concat_axis=0, tiled=True)


def tap_masks(starts, token_count):
    zh, x, x_size = lax.axis_index("zh"), lax.axis_index("x"), lax.axis_size("x")
    blocks = (zh * 2 + jnp.arange(2, dtype=jnp.int32)) * x_size + x
    places = blocks[:, None] * token_count + jnp.arange(token_count, dtype=jnp.int32)

    def segment_of(where):
        return jnp.sum((starts[None, :, None, :] <= where[:, None, :, None]).astype(jnp.int32), axis=3)

    own_segment = segment_of(places)
    keep_one = (segment_of(places - 1) == own_segment).astype(F32)
    keep_two = (segment_of(places - 2) == own_segment).astype(F32)
    return keep_one.reshape(8, token_count, 1), keep_two.reshape(8, token_count, 1)


def local(stream_in, doc_starts, norm_mix, in_proj, conv_taps, out_proj, norm_ffn, w_gate, w_up, w_down, grad_out):
    _, token_count, features = stream_in.shape
    layers = norm_mix.shape[0]
    own_kernels = sizes_of(DP) == (1, 2, 2)
    stream = stream_in.reshape(-1, features)
    grad_stream = grad_out.reshape(-1, features)
    small = jnp.concatenate([norm_mix[:, None], norm_ffn[:, None], conv_taps.transpose(0, 2, 1)], axis=1)
    small = small.astype(BF16).astype(F32)
    owned = small.shape[2]
    tall = (features // 8, w_gate.shape[2] // 8)
    mine = None
    if own_kernels:
        packed = jnp.zeros((16, LANES), F32).at[: 5 * layers, :owned].set(small.reshape(-1, owned))
        packed = packed.at[15, : doc_starts.shape[1]].set(doc_starts[0].astype(F32))
        spread, shards, rounded, wholes = prepare(packed, in_proj, w_gate, w_up, out_proj, w_down)
        mine = [(shards[1], rounded[1])]
        for layer in range(1, layers):
            mine.append((shards[2 * layer], rounded[2 * layer], shards[2 * layer + 1], rounded[2 * layer + 1]))
        params = spread[:, : 5 * layers, :owned].transpose(1, 0, 2)
        gains = params.reshape(layers, 5, features)[:, :2].reshape(2 * layers, 1, features)
        params = params.reshape(layers, 5, 4, 2, 2, 2, owned)[:, 2:]
        others = lax.axis_index("yl") * 2 + lax.axis_index("core")
        params = lax.dynamic_index_in_dim(params, others, 2, False)
        taps = lax.dynamic_index_in_dim(params, lax.axis_index("zl"), 3, False).reshape(layers, 3, -1)
        starts = spread.reshape(4, 8, 16, LANES)[:, 0, 15, : doc_starts.shape[1]].astype(jnp.int32)
        weights = [tuple(whole.reshape(-1, whole.shape[-1]) for whole in wholes)]
    else:
        starts = lax.all_gather(doc_starts, ("yl", "core"), axis=0, tiled=True)
        small = small.astype(BF16)
        gains = lax.all_gather(small[:, :2], OWNERS, axis=2, tiled=True).astype(F32).reshape(2 * layers, 1, features)
        taps = lax.all_gather(small[:, 2:], DP, axis=2, tiled=True).astype(F32)
        weights = []
        for layer in range(layers):
            in_w = gather_columns(column_shards(jnp.split(in_proj[layer].astype(BF16), 3, axis=1)))
            both_w = gather_columns(column_shards([w_gate[layer].astype(BF16), w_up[layer].astype(BF16)]))
            out_w = lax.all_gather(out_proj[layer].astype(BF16), DP, axis=0, tiled=True)
            down_w = lax.all_gather(w_down[layer].astype(BF16), DP, axis=0, tiled=True)
            weights.append((in_w, out_w, both_w, down_w))
    channels = taps.shape[2]
    taps = jnp.pad(taps, ((0, 0), (0, HALO - 3), (0, -channels % LANES)))
    keep = jnp.stack(tap_masks(starts, token_count))

    stream_out, middles, sources, saved, wholes = forward(stream, gains, taps, keep, weights, mine, tall)
    if own_kernels:
        weights = [weights[0] + tuple(wholes[:2])]
        weights += [tuple(wholes[2 + 4 * i : 6 + 4 * i]) for i in range(layers - 1)]
    grad_in, *results = backward(
        grad_stream, gains, taps, keep, middles, [stream] + list(sources), weights, saved, tall, own_kernels
    )
    if own_kernels:
        small_sums, grad_in_w, grad_out_w, grad_gate, grad_up, grad_down = results
        small_sums = small_sums[:, :owned]
        gain_grads = small_sums[: 2 * layers].reshape(layers, 2, owned)
        tap_grads = small_sums[2 * layers : 5 * layers].reshape(layers, 3, owned)
    else:
        gain_grads, tap_grads, *raw = results
        gain_grads = lax.psum_scatter(gain_grads, OWNERS, scatter_dimension=1, tiled=True).reshape(layers, 2, -1)
        tap_grads = lax.psum_scatter(tap_grads[:, :3, :channels], DP, scatter_dimension=2, tiled=True)
        sums = []
        for layer in range(layers):
            grad_in_w, grad_out_w, grad_both, grad_down = raw[4 * layer : 4 * layer + 4]
            columns = [
                column_whole(scatter_columns(grad.reshape(features, -1)).astype(F32), groups, width)
                for grad, groups, width in ((grad_in_w, 3, tall[0]), (grad_both, 2, tall[1]))
            ]
            rows = [
                lax.psum_scatter(grad, DP, scatter_dimension=0, tiled=True).astype(F32) for grad in (grad_out_w, grad_down)
            ]
            sums.append((jnp.concatenate(columns[0], axis=1), rows[0], *columns[1], rows[1]))
        grad_in_w, grad_out_w, grad_gate, grad_up, grad_down = (jnp.stack(parts) for parts in zip(*sums))
    return (
        stream_out[None],
        grad_in[None],
        gain_grads[:, 0],
        grad_in_w,
        tap_grads.transpose(0, 2, 1),
        grad_out_w,
        gain_grads[:, 1],
        grad_gate,
        grad_up,
        grad_down,
    )


def solution(mesh):
    dp, seq = mesh.shape["dp"], mesh.shape["seq"]
    side = dp // 2
    split = Mesh(mesh.devices.reshape(side // 2, 2, 2, seq // side // 2, 2, side), OWNERS)
    token = P(ROW_AXES, SEQ_AXES, None)
    vector = P(None, OWNERS)
    matrix = P(None, OWNERS, None)
    return jax.shard_map(
        local,
        mesh=split,
        in_specs=(token, P(ROW_AXES, None), vector, matrix, matrix, matrix, vector, matrix, matrix, matrix, token),
        out_specs=(token, token, vector, matrix, matrix, matrix, vector, matrix, matrix, matrix),
        check_vma=False,
    )
```

time: 2070 us -> 665 us (0.32)
  waiting for transfers between devices: 1410 us -> 0 us
  Pallas kernels: 0 us -> 631 us
  blocking collectives: 247 us -> 0 us
  local copies, waits for them, and re-layouts: 175 us -> 22.3 us
  matrix products: 134 us -> 0 us
  other arithmetic: 61.9 us -> 3.35 us
  starting transfers between devices: 20.7 us -> 0 us
    reduce_scatter x16 -> x0, waiting for transfers between devices: 832 us -> none  [the longest x8 401 us: scatter_tokens(): return lax.psum_scatter(partial, TP, scatter_dimension=0, tiled=True)]
    pallas_call x0 -> x3, Pallas kernels: none -> 631 us  [the longest x1 320 us: backward(): pl.pallas_call(functools.partial(backward_kernel, plan), out_shape=[jax.S...]
    all_gather x14 -> x0, waiting for transfers between devices: 432 us -> none  [the longest x8 194 us: gather_tokens(): return lax.all_gather(array, TP, axis=0, tiled=True)]
    all_gather x5 -> x0, blocking collectives: 139 us -> none  [the longest x1 76.2 us: local(): lax.all_gather(small[:, :, :2], OWNERS, axis=1, tiled=True).astype(F32)]
    dot_general x24 -> x0, matrix products: 134 us -> none  [the longest x8 46.2 us: matmul(): return jnp.dot(left, right, preferred_element_type=F32)]
    unnamed x34 -> x0, waiting for transfers between devices: 115 us -> none
    all_to_all x6 -> x0, blocking collectives: 108 us -> none  [the longest x4 63.3 us: gather_columns(): mine = lax.all_to_all(shards, TP, split_axis=0, concat_axis=0, tiled=True)]
    slice x18 -> x5, local copies, waits for them, and re-layouts: 49.5 us -> 1.53 us  [the longest x1 0.8 us: local(): gain_grads = small_sums[:2 * layers].reshape(layers, 2, owned)]
  transfers between devices with their start and end apart: 38 -> 0, of which waited for: 32 -> 0; matrix products, arithmetic and copies ran while one was open for 13% -> 0% of each run, Pallas kernels for 0% -> 0%
where the time goes in v5:
time: 665 us; the launch traced here: 658 us
  Pallas kernels  631 us (95%)
  local copies, waits for them, and re-layouts  22.3 us (3%)
    pallas_call x1, Pallas kernels, backward(): pl.pallas_call(functools.partial(backward_kernel, plan), out_shape=[jax.S...  320 us
    pallas_call x1, Pallas kernels, forward(): pl.pallas_call(functools.partial(forward_kernel, {'layers': layers, 'movi...  244 us
    pallas_call x1, Pallas kernels, prepare(): pl.pallas_call(functools.partial(prepare_kernel, layers), out_shape=[jax....  67.6 us
    unnamed x36, local copies, waits for them, and re-layouts  17.9 us

profile of v5, /device:TPU:0, one launch (start us, length us, event | category | flops | bytes accessed | tf_op | source)
XLA Modules:
  0.0 658.1 jit_solution(11957649668284216300)
XLA Ops:
  0.7 0.7 convert_element_type.56
  1.3 0.7 convert_bitcast_fusion.2
  2.0 0.7 convert_bitcast_fusion.1
  2.8 0.1 fusion
  2.8 0.2 scatter.14.small
  3.0 0.0 copy-start.3
  3.0 1.1 copy-done.3
  4.1 67.6 %prepare.1 = (f32[32,16,128]{2,1,0:T(8,128)S(1)}, bf16[4,2,48,640]{3,2,1,0:T(8,128)(2,1)}, bf16[4,2,48,1152]{3,2,1,0:T(8,128)(2,1)S(1)}, bf16[4,2,48,640]{3,2,1,...) custom-call(f32[16,128]{1,0:T(8,128)S(1)} %scatter.14.small, ...), custom_call_target="tpu_custom_call" | custom-call | tf_op jit(solution)/shard_map/prepare/pallas_call | solution.py:218
  71.7 0.0 copy-start
  71.7 0.8 copy-done
  72.5 0.0 copy-start.1
  72.5 0.9 copy-done.1
  73.4 0.0 copy-start.2
  73.4 0.9 copy-done.2
  74.3 0.0 copy-start.4
  74.3 0.8 copy-done.4
  75.1 0.8 copy-done.5
  75.9 0.8 copy-done.6
  76.6 0.7 copy-done.7
  77.3 0.1 convert_reduce_fusion.2
  77.5 0.5 copy.54
  78.0 0.1 copy.49
  78.1 0.1 reshape.248
  78.2 0.6 pad.14.refs_2_
  78.8 0.1 reshape.238
  78.9 0.6 reshape.239.refs_1_
  79.6 1.1 stack.6.refs_3_
  80.7 243.8 %forward.1 = (f32[128,1536]{1,0:T(8,128)}, f32[128,1536]{1,0:T(8,128)}, f32[128,1536]{1,0:T(8,128)}, f32[128,1536]{1,0:T(8,128)}, bf16[8,128,1536]{2,1,0:T(8,128...) custom-call(f32[128,1536]{1,0:T(8,128)} %bitcast.39, ...), custom_call_target="tpu_custom_call" | custom-call | tf_op jit(solution)/shard_map/forward/pallas_call | solution.py:894
  324.5 0.0 copy-start.12
  324.5 320.0 %backward.1 = (f32[128,1536]{1,0:T(8,128)}, f32[16,128]{1,0:T(8,128)}, f32[2,48,4608]{2,1,0:T(8,128)}, f32[2,48,1536]{2,1,0:T(8,128)}, f32[2,48,4608]{2,1,0:T(8,...) custom-call(f32[128,1536]{1,0:T(8,128)} %bitcast.44, f32[4,1,1536]{2,1,0:T(1,128)} %reshape.239.refs_1_, ...), custom_call_target="tpu_custom_call" | custom-call | tf_op jit(solution)/shard_map/backward/pallas_call | solution.py:1260
  644.5 0.0 copy-start.11
  644.5 0.8 slice.70
  645.3 0.7 slice.72
  646.0 0.6 copy.57
  646.6 0.6 fusion.3
  647.2 0.0 copy-done.12
  647.2 0.9 copy.70
  648.1 2.1 copy.71
  650.1 0.0 copy-done.11
  650.1 1.2 copy.72
  651.4 0.2 copy-done.13
  651.6 0.8 copy.73
  652.4 0.0 copy-done.10
  652.5 1.2 copy.74
  653.7 0.9 copy-done.9
  654.6 1.2 copy.75
  655.8 0.9 copy-done.8
  656.7 1.2 copy.76
  (21 shorter events, 0.1 us)
Async XLA Ops:
  3.0 1.1 copy-start.3
  71.7 0.8 copy-start
  72.5 0.9 copy-start.1
  73.4 0.9 copy-start.2
  74.3 0.8 copy-start.4
  75.1 0.8 copy-start.5
  75.9 0.8 copy-start.6
  76.6 0.7 copy-start.7
  324.5 322.7 %copy-start.12 = (f32[128,1536]{1,0:T(8,128)S(1)}, f32[128,1536]{1,0:T(8,128)}, u32[]{:S(2)}) copy-start(f32[128,1536]{1,0:T(8,128)} %get-tuple-element.85) | copy-start | bytes 2359300
  644.5 5.6 copy-start.11
  650.1 1.4 copy-start.13
  650.1 2.3 copy-start.10
  652.4 2.1 copy-start.9
  654.6 2.1 copy-start.8

commit v6 on v5

--- a/solution.py
+++ b/solution.py
@@ -18,12 +18,12 @@
 F32 = jnp.float32
 MESH = pl.DeviceIdType.MESH
 HALVES = 2
-COLLECTIVE_ID = {"prepare": 0, "forward": 1, "backward": 2}
+COLLECTIVE_ID = {"forward": 0, "backward": 1}
 FLIPS = ((1, 1, 1), (1, 1, 0), (1, 0, 1), (1, 0, 0), (0, 1, 1), (0, 1, 0), (0, 0, 1))
 OTHERS = tuple(itertools.product((0, 1), repeat=5))[1:]
 OTHER_AXES = ("yl", "core", "zh", "zl", "x")
 SEMAPHORES = 288
-FLYING = 2
+PACE = ((1, 1),) * 11
 LANES = 128
 TILE = 256
 HALO = 8
@@ -130,110 +130,9 @@
     ]
 
 
-def prepare_kernel(layers, small, in_proj, gate, up, out_proj, down, *refs):
-    refs = list(refs)
-
-    def take(count):
-        taken = refs[:count]
-        del refs[:count]
-        return taken
-
-    (spread,), mine, rounded, wholes = take(1), take(2 * layers), take(2 * layers), take(2)
-    shards, (send, recv, local) = take(2 * layers), take(3)
-    place = Place(send, recv, local)
-    barrier = pltpu.get_barrier_semaphore()
-    for device, _ in every_other(place):
-        pl.semaphore_signal(barrier, inc=1, device_id=device, device_id_type=MESH)
-    width = in_proj.shape[2] // 3
-
-    def cut(layer, which):
-        if which == 0:
-            shards_from([in_proj.at[layer, :, i * width : (i + 1) * width] for i in range(3)], shards[2 * layer])
-        else:
-            shards_from([gate.at[layer], up.at[layer]], shards[2 * layer + 1])
-
-    def scatter(index):
-        here = mine[index].at[place.yl * 2 + place.core, place.zl]
-        copies = [place.push(shards[index].at[place.rank(*flips)], here, place.member(flips)) for flips in FLIPS]
-        copies.append(place.copy(shards[index].at[place.rank(0, 0, 0)], here))
-        for copy in copies:
-            copy.start()
-        return copies
-
-    def landed(copies):
-        for copy in copies[:-1]:
-            copy.wait_recv()
-        copies[-1].wait()
-
-    cut(0, 0)
-    for layer in range(layers):
-        rounded[2 * layer][...] = out_proj[layer].astype(BF16)
-        rounded[2 * layer + 1][...] = down[layer].astype(BF16)
-    pl.semaphore_wait(barrier, len(OTHERS))
-    kept = place.copy(small, spread.at[place.owner()])
-    kept.start()
-    spreads = [place.push(small, spread.at[place.owner()], device) for device, _ in every_other(place)]
-    first = scatter(0)
-    for copy in spreads:
-        copy.start()
-    gathers = [Gather(place, own, whole) for own, whole in zip((mine[0], rounded[0]), wholes)]
-    for gather in gathers[1:]:
-        for launch, _ in gather.pairs():
-            launch()
-    cut(0, 1)
-    landed(first)
-    for launch, _ in gathers[0].pairs():
-        launch()
-    others = [scatter(1)]
-    for layer in range(1, layers):
-        for which in range(2):
-            cut(layer, which)
-            others.append(scatter(2 * layer + which))
-    for gather in gathers[1:] + gathers[:1]:
-        for _, land in gather.pairs():
-            land()
-    for copies in others:
-        landed(copies)
-    kept.wait()
-    for copy in spreads:
-        copy.wait_recv()
-    for gather in gathers:
-        gather.finish()
-    for copy in place.sent:
-        copy.wait_send()
-
-
-def whole_shape(mine):
-    return (4, 2, 2, 2) + mine[2:] if len(mine) == 4 else (2, 2) + mine
-
-
-def prepare(small, in_proj, gate, up, out_proj, down):
-    layers, rows, columns = in_proj.shape
-    widths = (-(-columns // 8 // LANES) * LANES, gate.shape[2] // 4)
-    inside = pl.BlockSpec(memory_space=pltpu.VMEM)
-    anywhere = pl.BlockSpec(memory_space=pl.ANY)
-    mine = [(4, 2, rows, width) for _ in range(layers) for width in widths]
-    rounded = [array.shape[1:] for _ in range(layers) for array in (out_proj, down)]
-    wholes = [whole_shape(shape) for shape in (mine[0], rounded[0])]
-    outs = pl.pallas_call(
-        functools.partial(prepare_kernel, layers),
-        out_shape=[jax.ShapeDtypeStruct((32,) + small.shape, F32)]
-        + [jax.ShapeDtypeStruct(shape, BF16) for shape in mine + rounded + wholes],
-        in_specs=[inside] * 6,
-        out_specs=[anywhere] * (1 + len(mine)) + [inside] * len(rounded) + [anywhere] * 2,
-        scratch_shapes=[pltpu.VMEM((8, rows, width), BF16) for _ in range(layers) for width in widths]
-        + [pltpu.SemaphoreType.DMA((SEMAPHORES,))] * 3,
-        compiler_params=pltpu.CompilerParams(
-            collective_id=COLLECTIVE_ID["prepare"], has_side_effects=True, vmem_limit_bytes=48 << 20
-        ),
-        name="prepare",
-    )(small, in_proj, gate, up, out_proj, down)
-    spread, outs = outs[0], outs[1:]
-    return spread, outs[: len(mine)], outs[len(mine) : -2], outs[-2:]
-
-
 class Gather:
     def __init__(self, place, mine, whole):
+        self.ready = None
         x, own, other = place.x, place.zh, 1 - place.zh
         if len(whole.shape) == 6:
             parts = [
@@ -255,6 +154,8 @@
 
     def pairs(self):
         def launch(c):
+            if c == 0 and self.ready is not None:
+                self.ready()
             self.along_z[c].start()
             self.along_x[c].start()
             self.kept[c].start()
@@ -520,10 +421,11 @@
             item.left -= 1
         del self.flying[:count]
 
-    def step(self):
-        if len(self.flying) >= FLYING:
+    def step(self, point):
+        fly, count = PACE[point]
+        while len(self.flying) > fly:
             self.land(1)
-        self.launch(1)
+        self.launch(count)
 
     def settle(self, items):
         for item in items:
@@ -595,7 +497,7 @@
         for h in range(HALVES):
             for copies in (from_z, from_y, own_to_core):
                 copies[h].start()
-        self.step()
+        self.step(0)
         if before_first is not None:
             before_first()
         own_place.wait()
@@ -605,22 +507,22 @@
             from_z[h].wait_recv()
             from_corner[h].start()
             z_to_core[h].start()
-        self.step()
+        self.step(1)
         for h in range(HALVES):
             from_y[h].wait_recv()
             y_to_core[h].start()
         landed(z_to_core)
         first(whole, chips[1])
-        self.step()
+        self.step(2)
         landed(y_to_core)
         first(whole, chips[2])
-        self.step()
+        self.step(3)
         for h in range(HALVES):
             from_corner[h].wait_recv()
             corner_to_core[h].start()
         landed(corner_to_core)
         first(whole, chips[3])
-        self.step()
+        self.step(4)
         if between is not None:
             between(whole)
         if before_second is not None:
@@ -650,20 +552,20 @@
         multiply(0)
         multiply(1)
         to_y_side(0)
-        self.step()
+        self.step(5)
         multiply(2)
         to_y_side(1)
         multiply(3)
-        self.step()
+        self.step(6)
         sib_copies[2].wait_recv()
         for h, rows in enumerate(halves):
             y_copies[0][h].wait_recv()
             zout[rows] = (chip_sum(2, rows) + yin[0, rows].astype(F32)).astype(BF16)
             z_copies[h].start()
-        self.step()
+        self.step(7)
         if aside is not None:
             aside(whole)
-        self.step()
+        self.step(8)
         sib_copies[3].wait_recv()
         for copy in sent:
             copy.wait_send()
@@ -671,9 +573,9 @@
             y_copies[1][h].wait_recv()
             z_copies[h].wait_recv()
             if h == HALVES - 1:
-                self.step()
+                self.step(9)
             after(h, rows, chip_sum(3, rows) + yin[1, rows].astype(F32) + zin[rows].astype(F32))
-        self.step()
+        self.step(10)
 
 
 def c_columns(joint, b, lane):
@@ -695,20 +597,22 @@
         del refs[:count]
         return taken
 
-    stream_in, gains, taps_ref, keep = take(4)
-    weights = [dict(zip(WEIGHTS, take(2 if moving else 4))) for _ in range(1 if moving else layers)]
-    mine = [take(4 if layer else 2) for layer in range(layers)] if moving else None
+    (stream_in,) = take(1)
+    if moving:
+        small, in_proj, gate_in, up_in, out_in, down_in = take(6)
+    else:
+        gains, taps_ref, keep = take(3)
+        weights = [dict(zip(WEIGHTS, take(4))) for _ in range(layers)]
     stream_out, middles, sources = take(1)[0], take(layers), take(layers - 1)
     saves = [dict(zip(SAVED, take(len(SAVED)))) for _ in range(layers)]
-    flat = []
     if moving:
-        for layer in range(layers):
-            names = WEIGHTS if layer else WEIGHTS[2:]
-            wholes = dict(zip(names, take(len(names))))
-            if layer:
-                weights.append({})
-            weights[layer].update(wholes)
+        weights = [dict(zip(WEIGHTS, take(4))) for _ in range(layers)]
+        gains, taps_ref, keep = take(3)
     buffers = dict(zip(buffer_names, take(len(buffer_names))))
+    if moving:
+        (spread,) = take(1)
+        shards, mine = ([dict(zip(WEIGHTS[::2], take(2))) for _ in range(layers)] for _ in range(2))
+        rounds = [dict(zip(WEIGHTS[1::2], take(2))) for _ in range(layers)]
     place = Place(*take(3))
     run = Pass(place, buffers)
     tokens, features = run.tokens, run.features
@@ -719,13 +623,64 @@
     main = gate_up.shape[2] // (2 * LANES) * LANES
     next_ref = buffers["next"]
 
-    coming = {}
+    coming, scattered = {}, {}
 
     def moves(layer, names):
-        own = dict(zip(WEIGHTS if layer else WEIGHTS[2:], mine[layer]))
         for name in names:
-            coming[layer, name] = Gather(place, own[name], weights[layer][name])
+            own = mine[layer][name] if name in mine[layer] else rounds[layer][name]
+            coming[layer, name] = Gather(place, own, weights[layer][name])
+            if name in mine[layer]:
+                coming[layer, name].ready = functools.partial(landed, layer, name)
             run.begin([coming[layer, name]])
+
+    def cut(layer, name):
+        if name == "in_w":
+            width = in_proj.shape[2] // 3
+            groups = [in_proj.at[layer, :, i * width : (i + 1) * width] for i in range(3)]
+        else:
+            groups = [gate_in.at[layer], up_in.at[layer]]
+        shards_from(groups, shards[layer][name])
+
+    def scatter(layer, name):
+        source = shards[layer][name]
+        here = mine[layer][name].at[place.yl * 2 + place.core, place.zl]
+        copies = [place.push(source.at[place.rank(*flips)], here, place.member(flips)) for flips in FLIPS]
+        copies.append(place.copy(source.at[place.rank(0, 0, 0)], here))
+        for copy in copies:
+            copy.start()
+        scattered[layer, name] = copies
+
+    def landed(layer, name):
+        copies = scattered.pop((layer, name))
+        for copy in copies[:-1]:
+            copy.wait_recv()
+        copies[-1].wait()
+
+    def parameters():
+        owned = features // 32
+        for layer in range(layers):
+            for i in range(2):
+                row = 5 * layer + i
+                gains[2 * layer + i] = jnp.concatenate([spread[o, row : row + 1, :owned] for o in range(32)], axis=1)
+            rows = pl.ds(5 * layer + 2, 3)
+            parts = [
+                spread[((place.yl * 2 + place.core) * 2 + zh) * 4 + place.zl * 2 + x, rows, :owned]
+                for zh, x in itertools.product(range(2), repeat=2)
+            ]
+            taps_ref[layer] = jnp.zeros(taps_ref.shape[1:], F32)
+            taps_ref[layer, :3, : 4 * owned] = jnp.concatenate(parts, axis=1)
+        count = lax.broadcasted_iota(jnp.int32, (tokens, 1), 0)
+        for block in range(8):
+            zl, others = block // 4, block % 4
+            places = (((place.zh * 2 + zl) * 2 + place.x) * tokens + count).astype(F32)
+            starts = [spread[others * 8, 15:16, n : n + 1] for n in range(plan["documents"])]
+
+            def segment(where):
+                return sum(jnp.where(start <= where, 1.0, 0.0) for start in starts)
+
+            own = segment(places)
+            keep[0, block] = jnp.where(segment(places - 1.0) == own, 1.0, 0.0)
+            keep[1, block] = jnp.where(segment(places - 2.0) == own, 1.0, 0.0)
 
     def load(layer, names):
         for name in names:
@@ -801,6 +756,8 @@
 
         def before_second():
             load(layer, ("out_w",))
+            if moving and layer + 1 < layers:
+                scatter(layer + 1, "in_w")
             run.loaded("out_w")
 
         run.phase(next_ref, first, second, after, before_first, before_second, between)
@@ -847,15 +804,42 @@
 
         def before_second():
             load(layer, ("down_w",))
+            if moving and layer + 1 < layers:
+                scatter(layer + 1, "both_w")
             run.loaded("down_w")
 
         run.phase(next_ref, first, second, after, before_first, before_second, between)
 
-    next_ref[...] = rounded(stream_in[...], gains[0])
-    run.enter([place.beside("zh"), place.beside("x")] if moving else [], False)
     if moving:
-        for layer in range(layers):
-            moves(layer, WEIGHTS if layer else WEIGHTS[2:])
+        cut(0, "in_w")
+        rounds[0]["out_w"][...] = out_in[0].astype(BF16)
+        run.enter([], True)
+        kept = place.copy(small, spread.at[place.owner()])
+        kept.start()
+        spreads = [place.push(small, spread.at[place.owner()], device) for device, _ in every_other(place)]
+        scatter(0, "in_w")
+        for copy in spreads:
+            copy.start()
+        moves(0, ("out_w", "in_w", "both_w", "down_w"))
+        run.launch(1)
+        cut(0, "both_w")
+        run.launch(8)
+        scatter(0, "both_w")
+        rounds[0]["down_w"][...] = down_in[0].astype(BF16)
+        for layer in range(1, layers):
+            cut(layer, "in_w")
+            cut(layer, "both_w")
+            rounds[layer]["out_w"][...] = out_in[layer].astype(BF16)
+            rounds[layer]["down_w"][...] = down_in[layer].astype(BF16)
+            moves(layer, WEIGHTS)
+        kept.wait()
+        for copy in spreads:
+            copy.wait_recv()
+        parameters()
+        next_ref[...] = rounded(stream_in[...], gains[0])
+    else:
+        next_ref[...] = rounded(stream_in[...], gains[0])
+        run.enter([], False)
     for layer in range(layers):
         conv(layer, sources[layer - 1] if layer else stream_in)
         ffn(layer)
@@ -873,40 +857,59 @@
             copy.wait()
 
 
-def forward(stream, gains, taps, keep, weights, mine, tall):
+def whole_shape(mine):
+    return (4, 2, 2, 2) + mine[2:] if len(mine) == 4 else (2, 2) + mine
+
+
+def forward(stream, given, tall, moving, documents=0):
     tokens, features = stream.shape
-    layers = taps.shape[0]
-    moving = mine is not None
-    wide = (weights[0][0].shape[1], mine[0][0].shape[3] if moving else weights[0][2].shape[1])
+    if moving:
+        layers, owned = given[1].shape[:2]
+        wide = (-(-3 * tall[0] // LANES) * LANES, 2 * tall[1])
+    else:
+        layers = given[1].shape[0]
+        wide = (given[3].shape[1], given[5].shape[1])
     forms = forms_of(tokens, features, wide, tall, layers)
     inside = pl.BlockSpec(memory_space=pltpu.VMEM)
     anywhere = pl.BlockSpec(memory_space=pl.ANY)
     outs = [(forms["stream"], inside)] * (1 + layers + layers - 1)
     outs += [(forms[name], anywhere) for _ in range(layers) for name in SAVED]
-    if moving:
-        outs += [((whole_shape(array.shape), BF16), anywhere) for group in mine for array in group]
     buffers = {name: forms[name] for name in ("joint", "carried", "mixed", "gated", "gate_up", "hidden", "next", "tails")}
     buffers |= {name: forms[name] for name in ("whole", "part", "sib", "yin", "yout", "zin", "zout")}
     buffers |= {"vmem_in_w": forms["in_w"], "vmem_both_w": forms["both_w"]}
     buffers |= {"vmem_out_w": ((forms["gated"][0][2], features), BF16), "vmem_down_w": forms["tall_w"]}
-    operands = [array for group in weights for array in group]
-    operands += [array for group in mine for array in group] if moving else []
+    scratch = [pltpu.VMEM(*form) for form in buffers.values()]
+    if moving:
+        columns = [(4, 2, owned, width) for width in wide]
+        rows = [(owned, features), (tall[1] // 4, features)]
+        wholes = [whole_shape(shape) for pair in zip(columns, rows) for shape in pair]
+        outs += [((shape, BF16), anywhere) for _ in range(layers) for shape in wholes]
+        outs += [(((2 * layers, 1, features), F32), inside), (((layers, HALO, forms["mixed"][0][2]), F32), inside)]
+        outs.append((((2, 8, tokens, 1), F32), inside))
+        scratch.append(pltpu.VMEM((32,) + given[0].shape, F32))
+        scratch += [pltpu.VMEM((8, owned, width), BF16) for _ in range(layers) for width in wide]
+        scratch += [pltpu.VMEM(shape, BF16) for _ in range(layers) for shape in columns]
+        scratch += [pltpu.VMEM(shape, BF16) for _ in range(layers) for shape in rows]
+    plan = {"layers": layers, "moving": moving, "buffers": tuple(buffers), "documents": documents}
     results = pl.pallas_call(
-        functools.partial(forward_kernel, {"layers": layers, "moving": moving, "buffers": tuple(buffers)}),
+        functools.partial(forward_kernel, plan),
         out_shape=[jax.ShapeDtypeStruct(*form) for form, _ in outs],
-        in_specs=[inside] * 4 + [anywhere] * len(operands),
+        in_specs=[inside] * 7 if moving else [inside] * 4 + [anywhere] * (len(given) - 3),
         out_specs=[spec for _, spec in outs],
-        scratch_shapes=[pltpu.VMEM(*form) for form in buffers.values()] + [pltpu.SemaphoreType.DMA((SEMAPHORES,))] * 3,
+        scratch_shapes=scratch + [pltpu.SemaphoreType.DMA((SEMAPHORES,))] * 3,
         compiler_params=pltpu.CompilerParams(
             collective_id=COLLECTIVE_ID["forward"], has_side_effects=True, vmem_limit_bytes=62 << 20
         ),
         name="forward",
-    )(stream, gains, taps, keep, *operands)
+    )(stream, *given)
     stream_out, results = results[0], results[1:]
     middles, results = results[:layers], results[layers:]
     sources, results = results[: layers - 1], results[layers - 1 :]
     count = layers * len(SAVED)
-    return stream_out, middles, sources, results[:count], results[count:]
+    saved, results = results[:count], results[count:]
+    if not moving:
+        return stream_out, middles, sources, saved, given[3:], given[:3]
+    return stream_out, middles, sources, saved, results[:-3], results[-3:]
 
 
 def backward_kernel(plan, *refs):
@@ -1350,44 +1353,28 @@
     small = small.astype(BF16).astype(F32)
     owned = small.shape[2]
     tall = (features // 8, w_gate.shape[2] // 8)
-    mine = None
     if own_kernels:
         packed = jnp.zeros((16, LANES), F32).at[: 5 * layers, :owned].set(small.reshape(-1, owned))
         packed = packed.at[15, : doc_starts.shape[1]].set(doc_starts[0].astype(F32))
-        spread, shards, rounded, wholes = prepare(packed, in_proj, w_gate, w_up, out_proj, w_down)
-        mine = [(shards[1], rounded[1])]
-        for layer in range(1, layers):
-            mine.append((shards[2 * layer], rounded[2 * layer], shards[2 * layer + 1], rounded[2 * layer + 1]))
-        params = spread[:, : 5 * layers, :owned].transpose(1, 0, 2)
-        gains = params.reshape(layers, 5, features)[:, :2].reshape(2 * layers, 1, features)
-        params = params.reshape(layers, 5, 4, 2, 2, 2, owned)[:, 2:]
-        others = lax.axis_index("yl") * 2 + lax.axis_index("core")
-        params = lax.dynamic_index_in_dim(params, others, 2, False)
-        taps = lax.dynamic_index_in_dim(params, lax.axis_index("zl"), 3, False).reshape(layers, 3, -1)
-        starts = spread.reshape(4, 8, 16, LANES)[:, 0, 15, : doc_starts.shape[1]].astype(jnp.int32)
-        weights = [tuple(whole.reshape(-1, whole.shape[-1]) for whole in wholes)]
+        given = (packed, in_proj, w_gate, w_up, out_proj, w_down)
     else:
         starts = lax.all_gather(doc_starts, ("yl", "core"), axis=0, tiled=True)
         small = small.astype(BF16)
         gains = lax.all_gather(small[:, :2], OWNERS, axis=2, tiled=True).astype(F32).reshape(2 * layers, 1, features)
         taps = lax.all_gather(small[:, 2:], DP, axis=2, tiled=True).astype(F32)
-        weights = []
+        taps = jnp.pad(taps, ((0, 0), (0, HALO - 3), (0, -taps.shape[2] % LANES)))
+        given = (gains, taps, jnp.stack(tap_masks(starts, token_count)))
         for layer in range(layers):
             in_w = gather_columns(column_shards(jnp.split(in_proj[layer].astype(BF16), 3, axis=1)))
             both_w = gather_columns(column_shards([w_gate[layer].astype(BF16), w_up[layer].astype(BF16)]))
             out_w = lax.all_gather(out_proj[layer].astype(BF16), DP, axis=0, tiled=True)
             down_w = lax.all_gather(w_down[layer].astype(BF16), DP, axis=0, tiled=True)
-            weights.append((in_w, out_w, both_w, down_w))
-    channels = taps.shape[2]
-    taps = jnp.pad(taps, ((0, 0), (0, HALO - 3), (0, -channels % LANES)))
-    keep = jnp.stack(tap_masks(starts, token_count))
-
-    stream_out, middles, sources, saved, wholes = forward(stream, gains, taps, keep, weights, mine, tall)
-    if own_kernels:
-        weights = [weights[0] + tuple(wholes[:2])]
-        weights += [tuple(wholes[2 + 4 * i : 6 + 4 * i]) for i in range(layers - 1)]
+            given += (in_w, out_w, both_w, down_w)
+
+    stream_out, middles, sources, saved, weights, params = forward(stream, given, tall, own_kernels, doc_starts.shape[1])
+    weights = [tuple(weights[4 * layer : 4 * layer + 4]) for layer in range(layers)]
     grad_in, *results = backward(
-        grad_stream, gains, taps, keep, middles, [stream] + list(sources), weights, saved, tall, own_kernels
+        grad_stream, *params, middles, [stream] + list(sources), weights, saved, tall, own_kernels
     )
     if own_kernels:
         small_sums, grad_in_w, grad_out_w, grad_gate, grad_up, grad_down = results
@@ -1397,7 +1384,7 @@
     else:
         gain_grads, tap_grads, *raw = results
         gain_grads = lax.psum_scatter(gain_grads, OWNERS, scatter_dimension=1, tiled=True).reshape(layers, 2, -1)
-        tap_grads = lax.psum_scatter(tap_grads[:, :3, :channels], DP, scatter_dimension=2, tiled=True)
+        tap_grads = lax.psum_scatter(tap_grads[:, :3, : tall[0]], DP, scatter_dimension=2, tiled=True)
         sums = []
         for layer in range(layers):
             grad_in_w, grad_out_w, grad_both, grad_down = raw[4 * layer : 4 * layer + 4]

time: 665 us -> 633 us (0.952)
  Pallas kernels: 631 us -> 611 us
  local copies, waits for them, and re-layouts: 22.3 us -> 14.2 us
    pallas_call x2 -> x1, Pallas kernels: 311 us -> 292 us  [forward(): pl.pallas_call(functools.partial(forward_kernel, plan), out_shape=[jax.Sh...]
    unnamed x36 -> x22, local copies, waits for them, and re-layouts: 17.9 us -> 11.9 us
where the time goes in v6:
time: 633 us; the launch traced here: 628 us
  Pallas kernels  611 us (97%)
  local copies, waits for them, and re-layouts  14.2 us (2%)
    pallas_call x1, Pallas kernels, backward(): pl.pallas_call(functools.partial(backward_kernel, plan), out_shape=[jax.S...  319 us
    pallas_call x1, Pallas kernels, forward(): pl.pallas_call(functools.partial(forward_kernel, plan), out_shape=[jax.Sh...  292 us

profile of v6, /device:TPU:0, one launch (start us, length us, event | category | flops | bytes accessed | tf_op | source)
XLA Modules:
  0.0 628.1 jit_solution(14885850320992011749)
XLA Ops:
  0.6 0.7 convert_element_type.13
  1.3 0.7 convert_bitcast_fusion.1
  2.0 0.7 convert_bitcast_fusion
  2.7 0.2 scatter.14.refs_1_
  2.9 0.0 copy-start.6
  2.9 0.6 copy-done.6
  3.5 292.0 %forward.1 = (f32[128,1536]{1,0:T(8,128)}, f32[128,1536]{1,0:T(8,128)}, f32[128,1536]{1,0:T(8,128)}, f32[128,1536]{1,0:T(8,128)}, bf16[8,128,1536]{2,1,0:T(8,128...) custom-call(f32[128,1536]{1,0:T(8,128)} %bitcast.18, ...), custom_call_target="tpu_custom_call" | custom-call | tf_op jit(solution)/shard_map/forward/pallas_call | solution.py:894
  295.6 0.0 copy-start.4
  295.6 318.9 %backward.1 = (f32[128,1536]{1,0:T(8,128)}, f32[16,128]{1,0:T(8,128)}, f32[2,48,4608]{2,1,0:T(8,128)}, f32[2,48,1536]{2,1,0:T(8,128)}, f32[2,48,4608]{2,1,0:T(8,...) custom-call(f32[128,1536]{1,0:T(8,128)} %bitcast.22, f32[4,1,1536]{2,1,0:T(1,128)} %get-tuple-element.73.refs_1_, ...), custom_call_target="tpu_custom_call" | custom-call | tf_op jit(solution)/shard_map/backward/pallas_call | solution.py:1263
  614.5 0.0 copy-start.3
  614.5 0.8 slice.54
  615.3 0.7 slice.56
  616.1 0.6 copy.28
  616.6 0.6 fusion
  617.2 0.0 copy-done.4
  617.2 0.9 copy.39
  618.1 2.1 copy.40
  620.2 0.0 copy-done.3
  620.2 0.0 copy-start.5
  620.2 0.0 copy-start.2
  620.2 1.2 copy.41
  621.4 0.2 copy-done.5
  621.6 0.8 copy.42
  622.4 0.0 copy-done.2
  622.5 0.0 copy-start.1
  622.5 1.2 copy.43
  623.7 0.9 copy-done.1
  624.6 0.0 copy-start
  624.6 1.2 copy.44
  625.8 0.9 copy-done
  626.7 1.2 copy.45
  (5 shorter events, 0.1 us)
Async XLA Ops:
  2.9 0.6 copy-start.6
  295.6 321.6 %copy-start.4 = (f32[128,1536]{1,0:T(8,128)S(1)}, f32[128,1536]{1,0:T(8,128)}, u32[]{:S(2)}) copy-start(f32[128,1536]{1,0:T(8,128)} %get-tuple-element.72) | copy-start | bytes 2359300
  614.5 5.6 copy-start.3
  620.2 1.4 copy-start.5
  620.2 2.3 copy-start.2
  622.5 2.1 copy-start.1
  624.6 2.1 copy-start

commit v7 on v6

--- a/solution.py
+++ b/solution.py
@@ -23,7 +23,8 @@
 OTHERS = tuple(itertools.product((0, 1), repeat=5))[1:]
 OTHER_AXES = ("yl", "core", "zh", "zl", "x")
 SEMAPHORES = 288
-PACE = ((1, 1),) * 11
+FORWARD_PACE = ((1, 1),) * 7 + ((1, 0),) + ((1, 1),) * 3
+BACKWARD_PACE = ((1, 1), (1, 2)) + ((2, 1),) * 8 + ((1, 1),)
 LANES = 128
 TILE = 256
 HALO = 8
@@ -371,8 +372,8 @@
 
 
 class Pass:
-    def __init__(self, place, buffers):
-        self.place, self.buffers = place, buffers
+    def __init__(self, place, buffers, pace):
+        self.place, self.buffers, self.pace = place, buffers, pace
         self.tokens, self.features = buffers["zin"].shape
         half = self.tokens // HALVES
         self.halves = [pl.ds(h * half, half) for h in range(HALVES)]
@@ -422,7 +423,7 @@
         del self.flying[:count]
 
     def step(self, point):
-        fly, count = PACE[point]
+        fly, count = self.pace[point]
         while len(self.flying) > fly:
             self.land(1)
         self.launch(count)
@@ -614,7 +615,7 @@
         shards, mine = ([dict(zip(WEIGHTS[::2], take(2))) for _ in range(layers)] for _ in range(2))
         rounds = [dict(zip(WEIGHTS[1::2], take(2))) for _ in range(layers)]
     place = Place(*take(3))
-    run = Pass(place, buffers)
+    run = Pass(place, buffers, FORWARD_PACE)
     tokens, features = run.tokens, run.features
     rows_of, blocks_of, pair = run.rows_of, run.blocks_of, run.pair
     joint, carried, mixed, gated = (buffers[name] for name in ("joint", "carried", "mixed", "gated"))
@@ -824,7 +825,6 @@
         run.launch(1)
         cut(0, "both_w")
         run.launch(8)
-        scatter(0, "both_w")
         rounds[0]["down_w"][...] = down_in[0].astype(BF16)
         for layer in range(1, layers):
             cut(layer, "in_w")
@@ -835,6 +835,7 @@
         kept.wait()
         for copy in spreads:
             copy.wait_recv()
+        scatter(0, "both_w")
         parameters()
         next_ref[...] = rounded(stream_in[...], gains[0])
     else:
@@ -937,7 +938,7 @@
         staging, slabs, slabs_in = take(2), *take(2)
         free = dict(zip(("both", "down", "conv"), take(3)))
     place = Place(*take(3))
-    run = Pass(place, buffers)
+    run = Pass(place, buffers, BACKWARD_PACE)
     tokens, features = run.tokens, run.features
     rows_of, blocks_of, all_rows, pair = run.rows_of, run.blocks_of, run.all_rows, run.pair
     wide = {"in_w": plan["wide"][0], "both_w": plan["wide"][1]}

time: 633 us -> 626 us (0.989)
  Pallas kernels: 611 us -> 603 us
where the time goes in v7:
time: 626 us; the launch traced here: 620 us
  Pallas kernels  603 us (96%)
  local copies, waits for them, and re-layouts  14.2 us (2%)
    pallas_call x1, Pallas kernels, backward(): pl.pallas_call(functools.partial(backward_kernel, plan), out_shape=[jax.S...  313 us
    pallas_call x1, Pallas kernels, forward(): pl.pallas_call(functools.partial(forward_kernel, plan), out_shape=[jax.Sh...  290 us

profile of v7, /device:TPU:0, one launch (start us, length us, event | category | flops | bytes accessed | tf_op | source)
XLA Modules:
  0.0 620.5 jit_solution(14197990757413386111)
XLA Ops:
  0.6 0.7 convert_element_type.13
  1.3 0.7 convert_bitcast_fusion.1
  2.0 0.7 convert_bitcast_fusion
  2.7 0.2 scatter.14.refs_1_
  2.9 0.0 copy-start.6
  2.9 0.6 copy-done.6
  3.5 290.2 %forward.1 = (f32[128,1536]{1,0:T(8,128)}, f32[128,1536]{1,0:T(8,128)}, f32[128,1536]{1,0:T(8,128)}, f32[128,1536]{1,0:T(8,128)}, bf16[8,128,1536]{2,1,0:T(8,128...) custom-call(f32[128,1536]{1,0:T(8,128)} %bitcast.18, ...), custom_call_target="tpu_custom_call" | custom-call | tf_op jit(solution)/shard_map/forward/pallas_call | solution.py:895
  293.7 0.0 copy-start.4
  293.7 313.2 %backward.1 = (f32[128,1536]{1,0:T(8,128)}, f32[16,128]{1,0:T(8,128)}, f32[2,48,4608]{2,1,0:T(8,128)}, f32[2,48,1536]{2,1,0:T(8,128)}, f32[2,48,4608]{2,1,0:T(8,...) custom-call(f32[128,1536]{1,0:T(8,128)} %bitcast.22, f32[4,1,1536]{2,1,0:T(1,128)} %get-tuple-element.73.refs_1_, ...), custom_call_target="tpu_custom_call" | custom-call | tf_op jit(solution)/shard_map/backward/pallas_call | solution.py:1264
  606.9 0.0 copy-start.3
  606.9 0.8 slice.54
  607.7 0.7 slice.56
  608.4 0.6 copy.28
  609.0 0.6 fusion
  609.6 0.0 copy-done.4
  609.6 0.9 copy.39
  610.4 2.1 copy.40
  612.5 0.0 copy-done.3
  612.5 0.0 copy-start.5
  612.5 0.0 copy-start.2
  612.5 1.2 copy.41
  613.7 0.2 copy-done.5
  614.0 0.8 copy.42
  614.8 0.0 copy-done.2
  614.8 0.0 copy-start.1
  614.8 1.2 copy.43
  616.0 0.9 copy-done.1
  616.9 0.0 copy-start
  616.9 1.2 copy.44
  618.1 0.9 copy-done
  619.1 1.2 copy.45
  (5 shorter events, 0.1 us)
Async XLA Ops:
  2.9 0.6 copy-start.6
  293.7 315.9 %copy-start.4 = (f32[128,1536]{1,0:T(8,128)S(1)}, f32[128,1536]{1,0:T(8,128)}, u32[]{:S(2)}) copy-start(f32[128,1536]{1,0:T(8,128)} %get-tuple-element.72) | copy-start | bytes 2359300
  606.9 5.6 copy-start.3
  612.5 1.4 copy-start.5
  612.5 2.3 copy-start.2
  614.8 2.1 copy-start.1
  616.9 2.1 copy-start

commit v8 on v7

--- a/solution.py
+++ b/solution.py
@@ -1194,6 +1194,7 @@
         ffn_back(layer)
         conv_back(layer)
     if moving:
+        run.launch(len(run.queue))
         owned = features // 32
         slabs[...] = jnp.zeros(slabs.shape, F32)
         for owner in range(32):
@@ -1208,7 +1209,6 @@
         for i, (device, flips) in enumerate(every_other(place)):
             copies.append(place.push(slabs.at[place.owner(flips)], slabs_in.at[i], device))
             copies[-1].start()
-        run.launch(len(run.queue))
         for kind in ("both", "down", "conv"):
             settle(kind)
         for copy in copies:

time: 626 us -> 624 us (level)
  no operation moved by 1% of the time
where the time goes in v8:
time: 624 us; the launch traced here: 619 us
  Pallas kernels  602 us (96%)
  local copies, waits for them, and re-layouts  14.2 us (2%)
    pallas_call x1, Pallas kernels, backward(): pl.pallas_call(functools.partial(backward_kernel, plan), out_shape=[jax.S...  312 us
    pallas_call x1, Pallas kernels, forward(): pl.pallas_call(functools.partial(forward_kernel, plan), out_shape=[jax.Sh...  290 us

profile of v8, /device:TPU:0, one launch (start us, length us, event | category | flops | bytes accessed | tf_op | source)
XLA Modules:
  0.0 619.2 jit_solution(16726184431951112316)
XLA Ops:
  0.6 0.7 convert_element_type.13
  1.3 0.7 convert_bitcast_fusion.1
  2.0 0.7 convert_bitcast_fusion
  2.7 0.2 scatter.14.refs_1_
  2.9 0.0 copy-start.6
  2.9 0.6 copy-done.6
  3.5 290.2 %forward.1 = (f32[128,1536]{1,0:T(8,128)}, f32[128,1536]{1,0:T(8,128)}, f32[128,1536]{1,0:T(8,128)}, f32[128,1536]{1,0:T(8,128)}, bf16[8,128,1536]{2,1,0:T(8,128...) custom-call(f32[128,1536]{1,0:T(8,128)} %bitcast.18, ...), custom_call_target="tpu_custom_call" | custom-call | tf_op jit(solution)/shard_map/forward/pallas_call | solution.py:895
  293.7 0.0 copy-start.4
  293.7 311.8 %backward.1 = (f32[128,1536]{1,0:T(8,128)}, f32[16,128]{1,0:T(8,128)}, f32[2,48,4608]{2,1,0:T(8,128)}, f32[2,48,1536]{2,1,0:T(8,128)}, f32[2,48,4608]{2,1,0:T(8,...) custom-call(f32[128,1536]{1,0:T(8,128)} %bitcast.22, f32[4,1,1536]{2,1,0:T(1,128)} %get-tuple-element.73.refs_1_, ...), custom_call_target="tpu_custom_call" | custom-call | tf_op jit(solution)/shard_map/backward/pallas_call | solution.py:1264
  605.6 0.0 copy-start.3
  605.6 0.8 slice.54
  606.4 0.7 slice.56
  607.1 0.6 copy.28
  607.7 0.6 fusion
  608.2 0.0 copy-done.4
  608.2 0.9 copy.39
  609.1 2.1 copy.40
  611.2 0.0 copy-done.3
  611.2 0.0 copy-start.5
  611.2 0.0 copy-start.2
  611.2 1.2 copy.41
  612.4 0.2 copy-done.5
  612.6 0.8 copy.42
  613.5 0.0 copy-done.2
  613.5 0.0 copy-start.1
  613.5 1.2 copy.43
  614.7 0.9 copy-done.1
  615.6 0.0 copy-start
  615.6 1.2 copy.44
  616.8 0.9 copy-done
  617.7 1.2 copy.45
  (5 shorter events, 0.1 us)
Async XLA Ops:
  2.9 0.6 copy-start.6
  293.7 314.5 %copy-start.4 = (f32[128,1536]{1,0:T(8,128)S(1)}, f32[128,1536]{1,0:T(8,128)}, u32[]{:S(2)}) copy-start(f32[128,1536]{1,0:T(8,128)} %get-tuple-element.72) | copy-start | bytes 2359300
  605.6 5.6 copy-start.3
  611.2 1.4 copy-start.5
  611.2 2.3 copy-start.2
  613.5 2.1 copy-start.1
  615.6 2.1 copy-start
